TPU v7x, 32 devices: a whole 2x2x4 slice. The times are simulated.
32 devices in a mesh: seq: 8 (over z, x), rows: 4 (over y, core).
Axes of the slice: x: 2, y: 2, z: 4, core: 2. Of those that a mesh axis runs over, the one named last changes fastest.
Arguments:
- tokens: bfloat16 [32, 1024, 512], P('rows', 'seq'), may hold values from -6 to 6
- segments: int32 [32, 1024], P('rows'), may hold values from 0 to 7, as said below
- gain_attn: float32 [512], replicated, may hold values from 0.5 to 1.5
- gain_ffn: float32 [512], replicated, may hold values from 0.5 to 1.5
- w_query: bfloat16 [512, 512], replicated, may hold values from -0.25 to 0.25
- w_key: bfloat16 [512, 512], replicated, may hold values from -0.25 to 0.25
- w_value: bfloat16 [512, 512], replicated, may hold values from -0.25 to 0.25
- w_out: bfloat16 [512, 512], replicated, may hold values from -0.75 to 0.75
- w_up: bfloat16 [512, 2048], replicated, may hold values from -0.25 to 0.25
- w_down: bfloat16 [2048, 512], replicated, may hold values from -0.1875 to 0.1875
- cotangent: bfloat16 [32, 1024, 512], P('rows', 'seq'), may hold values from -6 to 6
Outputs:
- output: bfloat16 [32, 1024, 512], P('rows', 'seq')
- d_tokens: bfloat16 [32, 1024, 512], P('rows', 'seq')
- d_gain_attn: float32 [512], replicated
- d_gain_ffn: float32 [512], replicated
- d_w_query: float32 [512, 512], replicated
- d_w_key: float32 [512, 512], replicated
- d_w_value: float32 [512, 512], replicated
- d_w_out: float32 [512, 512], replicated
- d_w_up: float32 [512, 2048], replicated
- d_w_down: float32 [2048, 512], replicated
Inputs may be any that keep to these rules, and one draw needn't show every extreme that they name: `segments`: along each row the document numbers start at 0, never fall and rise by at most one from a token to the next; in every aligned group of 8 rows one row is a single document.
All inputs are finite; a program needn't handle non-finite values.
Results may differ from a plain program's by a relative error of at most 0.014.
Values may be sent and summed in bfloat16 or wider, within the bound.
No kernel may reach another device: no remote copies, remote signals or barrier semaphores. Data moves between devices by JAX's collectives and lax.ppermute only.
A program may use at most 256 MiB of HBM per device.

v0:
```python
import jax
import jax.numpy as jnp
from jax import lax
from jax.sharding import PartitionSpec as P

HEADS = 8
HEAD = 64
BAND = 30


EPSILON = 1e-06
SCALE = 0.125
EXACT_MATMUL = lax.Precision.HIGHEST


def shifted(array, axis, by):
    devices = lax.axis_size(axis)
    pairs = [(i, i + by) for i in range(devices) if 0 <= i + by < devices]
    return lax.ppermute(array, axis, pairs)


def dense(matrix_a, matrix_b):
    return jnp.dot(matrix_a, matrix_b, preferred_element_type=jnp.float32)


def dense_tn(matrix_a, matrix_b):
    return lax.dot_general(
        matrix_a, matrix_b, (((0,), (0,)), ((), ())), preferred_element_type=jnp.float32
    )


def dense_right_transposed(matrix_a, matrix_b):
    return lax.dot_general(
        matrix_a, matrix_b, (((1,), (1,)), ((), ())), preferred_element_type=jnp.float32
    )


def norm_rows(inputs, gain_vec):
    return inputs * lax.rsqrt(jnp.mean(inputs * inputs, -1, keepdims=True) + EPSILON) * gain_vec


def norm_back(inputs, gain_vec, grad_in):
    _, pull = jax.vjp(norm_rows, inputs, gain_vec)
    return pull(grad_in)


def gelu_tanh(inputs):
    return (
        0.5
        * inputs
        * (1.0 + jnp.tanh(0.7978845608028654 * (inputs + 0.044715 * inputs * inputs * inputs)))
    )


def phi_elu(inputs):
    return jnp.where(inputs > 0, inputs + 1.0, jnp.exp(jnp.minimum(inputs, 0.0)))


def phi_tanh(inputs):
    return 1.0 + jnp.tanh(inputs)


def features(inputs):
    return jnp.stack([phi_elu(inputs), phi_tanh(inputs)], 1)


def join(earlier, later):
    carry_on = 1.0 - later[2]
    return (
        later[0] + carry_on[:, None, None, None, None] * earlier[0],
        later[1] + carry_on[:, None, None, None] * earlier[1],
        jnp.maximum(earlier[2], later[2]),
    )


def local(
    tokens, segments, gain_attn, gain_ffn, w_query, w_key, w_value, w_out, w_up, w_down, cotangent
):
    row_count, shard_len, model_dim = tokens.shape
    seq_count = lax.axis_size("seq")
    seq_start = lax.axis_index("seq") * shard_len
    seg_pad = jnp.concatenate([jnp.full((row_count, BAND), -1, jnp.int32), segments], axis=1)
    seg_own = lax.dynamic_slice_in_dim(segments, seq_start, shard_len, 1)
    seg_ext = lax.dynamic_slice_in_dim(seg_pad, seq_start, shard_len + BAND, 1)
    seg_before = seg_ext[:, BAND - 1]
    inputs = tokens.reshape(row_count * shard_len, model_dim).astype(jnp.float32)
    hidden = norm_rows(inputs, gain_attn).astype(jnp.bfloat16)
    query = dense(hidden, w_query).astype(jnp.bfloat16).reshape(row_count, shard_len, HEADS, HEAD)
    keys = dense(hidden, w_key).astype(jnp.bfloat16).reshape(row_count, shard_len, HEADS, HEAD)
    values = dense(hidden, w_value).astype(jnp.bfloat16).reshape(row_count, shard_len, HEADS, HEAD)
    rim = shifted((keys[:, shard_len - BAND :], values[:, shard_len - BAND :]), "seq", 1)
    key_ext = jnp.concatenate([rim[0], keys], 1)
    value_ext = jnp.concatenate([rim[1], values], 1)
    offset = jnp.arange(shard_len)[:, None] + BAND - jnp.arange(shard_len + BAND)[None, :]
    allowed = ((offset >= 0) & (offset <= BAND))[None] & (
        seg_own[:, :, None] == seg_ext[:, None, :]
    )

    def band_scores():
        score = (
            jnp.einsum("rihd,rjhd->rhij", query, key_ext, preferred_element_type=jnp.float32)
            * SCALE
        )
        return jnp.where(allowed[:, None], score, -1e30)

    score = band_scores()
    score_max = jnp.max(score, -1, keepdims=True)
    exponent = jnp.exp(score - score_max)
    log_total = score_max + jnp.log(jnp.sum(exponent, -1, keepdims=True))
    attn_prob = jnp.exp(score - log_total)
    near_out = jnp.einsum(
        "rhij,rjhd->rihd",
        attn_prob.astype(jnp.bfloat16),
        value_ext,
        preferred_element_type=jnp.float32,
    )
    causal = jnp.arange(shard_len)[:, None] >= jnp.arange(shard_len)[None, :]
    same_doc = (causal[None] & (seg_own[:, :, None] == seg_own[:, None, :])).astype(jnp.float32)
    carry_applied_state = (seg_own == seg_before[:, None]).astype(jnp.float32)
    tail_mask = (seg_own == seg_own[:, shard_len - 1 :]).astype(jnp.float32)
    reset = jnp.logical_or(
        seg_own[:, 0] != seg_own[:, shard_len - 1], seg_own[:, 0] != seg_before
    ).astype(jnp.float32)
    query_f = query.astype(jnp.float32)
    keys_f = keys.astype(jnp.float32)
    values_f = values.astype(jnp.float32)
    feat_q, feat_q_pull = jax.vjp(features, query_f)
    feat_k, feat_k_pull = jax.vjp(features, keys_f)
    far_weight = (
        jnp.einsum("rmihd,rmjhd->rmhij", feat_q, feat_k, precision=EXACT_MATMUL)
        * same_doc[:, None, None]
    )
    tail_k = feat_k * tail_mask[:, None, :, None, None]
    element = (
        jnp.einsum("rmjhd,rjhe->rmhde", tail_k, values_f, precision=EXACT_MATMUL),
        jnp.sum(tail_k, 2),
        reset,
    )
    neutral = jax.tree.map(jnp.zeros_like, element)

    def relay_forward(turn_index, prefix):
        return shifted(join(prefix, element), "seq", 1)

    carried = lax.fori_loop(0, seq_count - 1, relay_forward, neutral)
    numerator = jnp.einsum("rmhij,rjhe->rmihe", far_weight, values_f, precision=EXACT_MATMUL)
    numerator = numerator + carry_applied_state[:, None, :, None, None] * jnp.einsum(
        "rmihd,rmhde->rmihe", feat_q, carried[0], precision=EXACT_MATMUL
    )
    normalizer_sum = jnp.transpose(jnp.sum(far_weight, -1), (0, 1, 3, 2))
    normalizer_sum = normalizer_sum + carry_applied_state[:, None, :, None] * jnp.einsum(
        "rmihd,rmhd->rmih", feat_q, carried[1], precision=EXACT_MATMUL
    )
    far_out = numerator / normalizer_sum[..., None]
    attended = (
        (near_out + jnp.sum(far_out, 1))
        .reshape(row_count * shard_len, model_dim)
        .astype(jnp.bfloat16)
    )
    residual = inputs + dense(attended, w_out)
    hidden_two = norm_rows(residual, gain_ffn).astype(jnp.bfloat16)
    up_proj = dense(hidden_two, w_up)
    activated = gelu_tanh(up_proj).astype(jnp.bfloat16)
    output = (
        (residual + dense(activated, w_down))
        .astype(jnp.bfloat16)
        .reshape(row_count, shard_len, model_dim)
    )
    grad_out = cotangent.reshape(row_count * shard_len, model_dim)
    d_w_down = dense_tn(activated, grad_out)
    d_activated = dense_right_transposed(grad_out, w_down)
    _, gelu_pull = jax.vjp(gelu_tanh, up_proj)
    d_up_proj = gelu_pull(d_activated)[0].astype(jnp.bfloat16)
    d_w_up = dense_tn(hidden_two, d_up_proj)
    d_hidden_two = dense_right_transposed(d_up_proj, w_up)
    d_res_norm, d_gain_ffn = norm_back(residual, gain_ffn, d_hidden_two)
    d_residual = grad_out.astype(jnp.float32) + d_res_norm
    ffn_grads = (d_w_up, d_w_down, d_gain_ffn)
    d_branch = d_residual.astype(jnp.bfloat16)
    d_w_out = dense_tn(attended, d_branch)
    attended_gradient = (
        dense_right_transposed(d_branch, w_out)
        .astype(jnp.bfloat16)
        .reshape(row_count, shard_len, HEADS, HEAD)
    )
    attn_prob = jnp.exp(band_scores() - log_total)
    d_prob = jnp.einsum(
        "rihd,rjhd->rhij", attended_gradient, value_ext, preferred_element_type=jnp.float32
    )
    d_value_ext = jnp.einsum(
        "rhij,rihd->rjhd",
        attn_prob.astype(jnp.bfloat16),
        attended_gradient,
        preferred_element_type=jnp.float32,
    )
    delta = jnp.sum(attn_prob * d_prob, -1, keepdims=True)
    d_score = (attn_prob * (d_prob - delta)).astype(jnp.bfloat16)
    d_query = SCALE * jnp.einsum(
        "rhij,rjhd->rihd", d_score, key_ext, preferred_element_type=jnp.float32
    )
    d_key_ext = SCALE * jnp.einsum(
        "rhij,rihd->rjhd", d_score, query, preferred_element_type=jnp.float32
    )
    grad_far = attended_gradient.astype(jnp.float32)[:, None]
    d_numer = grad_far / normalizer_sum[..., None]
    d_denom = -jnp.sum(grad_far * far_out, -1) / normalizer_sum
    d_weight = (
        jnp.einsum("rmihe,rjhe->rmhij", d_numer, values_f, precision=EXACT_MATMUL)
        + jnp.transpose(d_denom, (0, 1, 3, 2))[..., None]
    ) * same_doc[:, None, None]
    d_feat_q = jnp.einsum("rmhij,rmjhd->rmihd", d_weight, feat_k, precision=EXACT_MATMUL)
    d_feat_q = d_feat_q + carry_applied_state[:, None, :, None, None] * (
        jnp.einsum("rmihe,rmhde->rmihd", d_numer, carried[0], precision=EXACT_MATMUL)
        + d_denom[..., None] * carried[1][:, :, None]
    )
    d_feat_k = jnp.einsum("rmhij,rmihd->rmjhd", d_weight, feat_q, precision=EXACT_MATMUL)
    d_value_far = jnp.einsum("rmhij,rmihe->rjhe", far_weight, d_numer, precision=EXACT_MATMUL)
    used_q = feat_q * carry_applied_state[:, None, :, None, None]
    back_element = (
        jnp.einsum("rmihd,rmihe->rmhde", used_q, d_numer, precision=EXACT_MATMUL),
        jnp.einsum("rmihd,rmih->rmhd", used_q, d_denom, precision=EXACT_MATMUL),
        reset,
    )

    def relay_backward(turn_index, prefix):
        return shifted(join(prefix, back_element), "seq", -1)

    incoming = lax.fori_loop(0, seq_count - 1, relay_backward, neutral)
    final_five_tokens = tail_mask[:, None, :, None, None]
    d_feat_k = d_feat_k + final_five_tokens * (
        jnp.einsum("rmhde,rjhe->rmjhd", incoming[0], values_f, precision=EXACT_MATMUL)
        + incoming[1][:, :, None]
    )
    d_value_far = d_value_far + jnp.einsum(
        "rmjhd,rmhde->rjhe", tail_k, incoming[0], precision=EXACT_MATMUL
    )
    d_query_far = feat_q_pull(d_feat_q)[0]
    d_key_far = feat_k_pull(d_feat_k)[0]
    rim_back = shifted((d_key_ext[:, :BAND], d_value_ext[:, :BAND]), "seq", -1)
    zero_fill = jnp.zeros((row_count, shard_len - BAND, HEADS, HEAD), jnp.float32)
    d_key_all = d_key_ext[:, BAND:] + jnp.concatenate([zero_fill, rim_back[0]], 1) + d_key_far
    d_value_all = d_value_ext[:, BAND:] + jnp.concatenate([zero_fill, rim_back[1]], 1) + d_value_far
    flat_shape = (row_count * shard_len, model_dim)
    d_query_low = (d_query + d_query_far).astype(jnp.bfloat16).reshape(flat_shape)
    d_key_low = d_key_all.astype(jnp.bfloat16).reshape(flat_shape)
    d_value_low = d_value_all.astype(jnp.bfloat16).reshape(flat_shape)
    d_w_query = dense_tn(hidden, d_query_low)
    d_w_key = dense_tn(hidden, d_key_low)
    d_w_value = dense_tn(hidden, d_value_low)
    d_hidden = (
        dense_right_transposed(d_query_low, w_query)
        + dense_right_transposed(d_key_low, w_key)
        + dense_right_transposed(d_value_low, w_value)
    )
    d_in_norm, d_gain_attn = norm_back(inputs, gain_attn, d_hidden)
    d_tokens = (
        (d_residual + d_in_norm).astype(jnp.bfloat16).reshape(row_count, shard_len, model_dim)
    )
    totals = lax.psum(
        (
            d_w_query,
            d_w_key,
            d_w_value,
            d_w_out,
            ffn_grads[0],
            ffn_grads[1],
            d_gain_attn,
            ffn_grads[2],
        ),
        ("seq", "rows"),
    )
    return (
        output,
        d_tokens,
        totals[6],
        totals[7],
        totals[0],
        totals[1],
        totals[2],
        totals[3],
        totals[4],
        totals[5],
    )


def solution(mesh):
    placed = (
        P("rows", "seq", None),
        P("rows", None),
        P(),
        P(),
        P(),
        P(),
        P(),
        P(),
        P(),
        P(),
        P("rows", "seq", None),
    )
    return jax.shard_map(
        local,
        mesh=mesh,
        in_specs=placed,
        out_specs=(
            P("rows", "seq", None),
            P("rows", "seq", None),
            P(),
            P(),
            P(),
            P(),
            P(),
            P(),
            P(),
            P(),
        ),
        check_vma=False,
    )
```

profile of v0, /device:TPU:0, one launch (start us, length us, event | category | flops | bytes accessed | tf_op | source)
XLA Modules:
  0.0 2002.4 jit_solution(12038742466536082558)
XLA Ops:
  116.4 700.2 %while.24 = (s32[]{:T(128)}, f32[8,2,8,64,64]{4,3,2,1,0:T(8,128)}, f32[8,2,8,64]{3,2,1,0:T(8,128)S(1)}, f32[8]{0:T(128)S(1)}, f32[8,2,8,64,64]{4,3,2,1,0:T(8,128)}, /*index=5*/f32[8,2,8,64]{3,2,1,0:T(8,128)S(1)}, s32[]{:T(128)}) while((s32[]{:T(128)}, f32[8,2,8,64,64]{4,3,2,1,0:T(8,128)}, f32[8,2,8,64]{3,2,1,0:T(8,128)S(1)}, f32[8]{0:T(128)S(1)}, ...), condition=%wide.region_5.6_spmd, body=%wide.region_4.5_spmd.sunk | while | flops 1064970 | bytes 14909725 | solution.py:144
  129.6 87.3 %collective-permute-done.1 = f32[8,2,8,64]{3,2,1,0:T(8,128)S(1)} collective-permute-done((f32[8,2,8,64]{3,2,1,0:T(8,128)S(1)}, f32[8,2,8,64]{3,2,1,0:T(8,128)S(1)}, u32[]{:S(2)}, u32[]{:S(2)}) %collective-permute-start.1) | collective-permute-done | bytes 32800 | tf_op jit(solution)/shard_map/while/body/eval_jaxpr/ppermute | solution.py:19
  232.7 85.6 %collective-permute-done.1 = f32[8,2,8,64]{3,2,1,0:T(8,128)S(1)} collective-permute-done((f32[8,2,8,64]{3,2,1,0:T(8,128)S(1)}, f32[8,2,8,64]{3,2,1,0:T(8,128)S(1)}, u32[]{:S(2)}, u32[]{:S(2)}) %collective-permute-start.1) | collective-permute-done | bytes 32800 | tf_op jit(solution)/shard_map/while/body/eval_jaxpr/ppermute | solution.py:19
  335.0 83.9 %collective-permute-done.1 = f32[8,2,8,64]{3,2,1,0:T(8,128)S(1)} collective-permute-done((f32[8,2,8,64]{3,2,1,0:T(8,128)S(1)}, f32[8,2,8,64]{3,2,1,0:T(8,128)S(1)}, u32[]{:S(2)}, u32[]{:S(2)}) %collective-permute-start.1) | collective-permute-done | bytes 32800 | tf_op jit(solution)/shard_map/while/body/eval_jaxpr/ppermute | solution.py:19
  436.5 82.9 %collective-permute-done.1 = f32[8,2,8,64]{3,2,1,0:T(8,128)S(1)} collective-permute-done((f32[8,2,8,64]{3,2,1,0:T(8,128)S(1)}, f32[8,2,8,64]{3,2,1,0:T(8,128)S(1)}, u32[]{:S(2)}, u32[]{:S(2)}) %collective-permute-start.1) | collective-permute-done | bytes 32800 | tf_op jit(solution)/shard_map/while/body/eval_jaxpr/ppermute | solution.py:19
  537.2 82.1 %collective-permute-done.1 = f32[8,2,8,64]{3,2,1,0:T(8,128)S(1)} collective-permute-done((f32[8,2,8,64]{3,2,1,0:T(8,128)S(1)}, f32[8,2,8,64]{3,2,1,0:T(8,128)S(1)}, u32[]{:S(2)}, u32[]{:S(2)}) %collective-permute-start.1) | collective-permute-done | bytes 32800 | tf_op jit(solution)/shard_map/while/body/eval_jaxpr/ppermute | solution.py:19
  637.1 81.3 %collective-permute-done.1 = f32[8,2,8,64]{3,2,1,0:T(8,128)S(1)} collective-permute-done((f32[8,2,8,64]{3,2,1,0:T(8,128)S(1)}, f32[8,2,8,64]{3,2,1,0:T(8,128)S(1)}, u32[]{:S(2)}, u32[]{:S(2)}) %collective-permute-start.1) | collective-permute-done | bytes 32800 | tf_op jit(solution)/shard_map/while/body/eval_jaxpr/ppermute | solution.py:19
  736.2 80.5 %collective-permute-done.1 = f32[8,2,8,64]{3,2,1,0:T(8,128)S(1)} collective-permute-done((f32[8,2,8,64]{3,2,1,0:T(8,128)S(1)}, f32[8,2,8,64]{3,2,1,0:T(8,128)S(1)}, u32[]{:S(2)}, u32[]{:S(2)}) %collective-permute-start.1) | collective-permute-done | bytes 32800 | tf_op jit(solution)/shard_map/while/body/eval_jaxpr/ppermute | solution.py:19
  822.1 9.0 fusion.20
  831.2 14.2 fusion.158
  945.2 668.5 %while.25 = (s32[]{:T(128)}, f32[8,2,8,64,64]{4,3,2,1,0:T(8,128)}, f32[8,2,8,64]{3,2,1,0:T(8,128)S(1)}, f32[8]{0:T(128)S(1)}, f32[8,2,8,64,64]{4,3,2,1,0:T(8,128)}, /*index=5*/f32[8,2,8,64]{3,2,1,0:T(8,128)S(1)}, s32[]{:T(128)}) while((s32[]{:T(128)}, f32[8,2,8,64,64]{4,3,2,1,0:T(8,128)}, f32[8,2,8,64]{3,2,1,0:T(8,128)S(1)}, ...), condition=%wide.region_13.14_spmd, body=%wide.region_12.13_spmd.sunk | while | flops 1064970 | bytes 14909725 | solution.py:227
  955.5 87.9 %collective-permute-done.3 = f32[8,2,8,64]{3,2,1,0:T(8,128)S(1)} collective-permute-done((f32[8,2,8,64]{3,2,1,0:T(8,128)}, f32[8,2,8,64]{3,2,1,0:T(8,128)S(1)}, u32[]{:S(2)}, u32[]{:S(2)}) %collective-permute-start.3) | collective-permute-done | bytes 32800 | tf_op jit(solution)/shard_map/while/body/eval_jaxpr/ppermute | solution.py:19
  1053.7 87.4 %collective-permute-done.3 = f32[8,2,8,64]{3,2,1,0:T(8,128)S(1)} collective-permute-done((f32[8,2,8,64]{3,2,1,0:T(8,128)}, f32[8,2,8,64]{3,2,1,0:T(8,128)S(1)}, u32[]{:S(2)}, u32[]{:S(2)}) %collective-permute-start.3) | collective-permute-done | bytes 32800 | tf_op jit(solution)/shard_map/while/body/eval_jaxpr/ppermute | solution.py:19
  1151.4 85.8 %collective-permute-done.3 = f32[8,2,8,64]{3,2,1,0:T(8,128)S(1)} collective-permute-done((f32[8,2,8,64]{3,2,1,0:T(8,128)}, f32[8,2,8,64]{3,2,1,0:T(8,128)S(1)}, u32[]{:S(2)}, u32[]{:S(2)}) %collective-permute-start.3) | collective-permute-done | bytes 32800 | tf_op jit(solution)/shard_map/while/body/eval_jaxpr/ppermute | solution.py:19
  1247.5 85.0 %collective-permute-done.3 = f32[8,2,8,64]{3,2,1,0:T(8,128)S(1)} collective-permute-done((f32[8,2,8,64]{3,2,1,0:T(8,128)}, f32[8,2,8,64]{3,2,1,0:T(8,128)S(1)}, u32[]{:S(2)}, u32[]{:S(2)}) %collective-permute-start.3) | collective-permute-done | bytes 32800 | tf_op jit(solution)/shard_map/while/body/eval_jaxpr/ppermute | solution.py:19
  1342.8 84.2 %collective-permute-done.3 = f32[8,2,8,64]{3,2,1,0:T(8,128)S(1)} collective-permute-done((f32[8,2,8,64]{3,2,1,0:T(8,128)}, f32[8,2,8,64]{3,2,1,0:T(8,128)S(1)}, u32[]{:S(2)}, u32[]{:S(2)}) %collective-permute-start.3) | collective-permute-done | bytes 32800 | tf_op jit(solution)/shard_map/while/body/eval_jaxpr/ppermute | solution.py:19
  1437.2 83.3 %collective-permute-done.3 = f32[8,2,8,64]{3,2,1,0:T(8,128)S(1)} collective-permute-done((f32[8,2,8,64]{3,2,1,0:T(8,128)}, f32[8,2,8,64]{3,2,1,0:T(8,128)S(1)}, u32[]{:S(2)}, u32[]{:S(2)}) %collective-permute-start.3) | collective-permute-done | bytes 32800 | tf_op jit(solution)/shard_map/while/body/eval_jaxpr/ppermute | solution.py:19
  1530.8 82.5 %collective-permute-done.3 = f32[8,2,8,64]{3,2,1,0:T(8,128)S(1)} collective-permute-done((f32[8,2,8,64]{3,2,1,0:T(8,128)}, f32[8,2,8,64]{3,2,1,0:T(8,128)S(1)}, u32[]{:S(2)}, u32[]{:S(2)}) %collective-permute-start.3) | collective-permute-done | bytes 32800 | tf_op jit(solution)/shard_map/while/body/eval_jaxpr/ppermute | solution.py:19
  1658.6 8.9 fusion.18
  1674.6 18.4 fusion.16
  1694.8 10.2 fusion.13
  1708.2 12.9 fusion.88
  1751.8 48.9 %all-reduce.3 = (f32[512]{0:T(512)}, f32[512]{0:T(512)}) all-reduce(f32[512]{0:T(512)S(1)} %get-tuple-element.100, f32[512]{0:T(512)S(1)} %get-tuple-element.98), channel_id=1, replica_groups=mesh['seq'=8,'rows'=4] {'seq','rows'}, use_global_device_ids=true, to_apply=%region_16.17 | all-reduce | flops 1024 | bytes 8192 | tf_op jit(solution)/shard_map/psum | solution.py:258
  1803.9 179.0 %all-reduce.7.cloned.1.call-done = (f32[512,512]{1,0:T(8,128)}, f32[512,512]{1,0:T(8,128)}, f32[512,512]{1,0:T(8,128)}, f32[512,512]{1,0:T(8,128)}, f32[512,2048]{1,0:T(8,128)}, /*index=5*/f32[2048,512]{1,0:T(8,128)}) async-done(((f32[512,512]{1,0:T(8,128)}, f32[512,512]{1,0:T(8,128)}, f32[512,512]{1,0:T(8,128)}, f32[512,512]{1,0:T(8,128)}, f32[512,2048]{1,0:T(8,128)}, /*index=5*/f32[2048,512]{1,0:T(8,128)}), ...) | async-done | bytes 12582928 | tf_op jit(solution)/shard_map/psum | solution.py:258
  (351 shorter events, 505.5 us)
Async XLA Ops:
  7.2 1975.7 %all-reduce.7.cloned.1.call-start = ((), (), s32[]{:S(2)}) async-start(), calls=%async_computation | async-start | bytes 25165824 | tf_op jit(solution)/shard_map/psum | solution.py:258
  20.8 851.9 %collective-permute-start.4 = (bf16[8,30,8,64]{3,2,1,0:T(8,128)(2,1)}, bf16[8,30,8,64]{3,2,1,0:T(8,128)(2,1)}, u32[]{:S(2)}, u32[]{:S(2)}) collective-permute-start(bf16[8,30,8,64]{3,2,1,0:T(8,128)(2,1)} %copy.122), channel_id=1, source_target_pairs={{0,4},{4,8},{8,12},{12,16},{16,20},{20,24},{24,28},{1,5},{5,9},{9,... | collective-permute-start | bytes 737288 | tf_op jit(solution)/shard_map/ppermute | solution.py:19
  40.1 822.1 %collective-permute-start.5 = (bf16[8,30,8,64]{3,2,1,0:T(8,128)(2,1)}, bf16[8,30,8,64]{3,2,1,0:T(8,128)(2,1)}, u32[]{:S(2)}, u32[]{:S(2)}) collective-permute-start(bf16[8,30,8,64]{3,2,1,0:T(8,128)(2,1)} %copy.127), channel_id=1, source_target_pairs={{0,4},{4,8},{8,12},{12,16},{16,20},{20,24},{24,28},{1,5},{5,9},{9,... | collective-permute-start | bytes 737288 | tf_op jit(solution)/shard_map/ppermute | solution.py:19
  123.4 93.5 %collective-permute-start = (f32[8,2,8,64,64]{4,3,2,1,0:T(8,128)}, f32[8,2,8,64,64]{4,3,2,1,0:T(8,128)}, u32[]{:S(2)}, u32[]{:S(2)}) collective-permute-start(f32[8,2,8,64,64]{4,3,2,1,0:T(8,128)} %multiply_add_fusion.13), channel_id=1, source_target_pairs={{0,4},{4,8},{8,12},{12,16},{16,20},{20,24},{24,28},{1,5},{5,9},{9,... | collective-permute-start | bytes 6291464 | tf_op jit(solution)/shard_map/while/body/eval_jaxpr/ppermute | solution.py:19
  128.1 88.8 %collective-permute-start.1 = (f32[8,2,8,64]{3,2,1,0:T(8,128)S(1)}, f32[8,2,8,64]{3,2,1,0:T(8,128)S(1)}, u32[]{:S(2)}, u32[]{:S(2)}) collective-permute-start(f32[8,2,8,64]{3,2,1,0:T(8,128)S(1)} %multiply_add_fusion.14), channel_id=1, source_target_pairs={{0,4},{4,8},{8,12},{12,16},{16,20},{20,24},{24,28},{1,5},{5,9},{9,... | collective-permute-start | bytes 98312 | tf_op jit(solution)/shard_map/while/body/eval_jaxpr/ppermute | solution.py:19
  223.9 94.4 %collective-permute-start = (f32[8,2,8,64,64]{4,3,2,1,0:T(8,128)}, f32[8,2,8,64,64]{4,3,2,1,0:T(8,128)}, u32[]{:S(2)}, u32[]{:S(2)}) collective-permute-start(f32[8,2,8,64,64]{4,3,2,1,0:T(8,128)} %multiply_add_fusion.13), channel_id=1, source_target_pairs={{0,4},{4,8},{8,12},{12,16},{16,20},{20,24},{24,28},{1,5},{5,9},{9,... | collective-permute-start | bytes 6291464 | tf_op jit(solution)/shard_map/while/body/eval_jaxpr/ppermute | solution.py:19
  230.3 88.0 %collective-permute-start.1 = (f32[8,2,8,64]{3,2,1,0:T(8,128)S(1)}, f32[8,2,8,64]{3,2,1,0:T(8,128)S(1)}, u32[]{:S(2)}, u32[]{:S(2)}) collective-permute-start(f32[8,2,8,64]{3,2,1,0:T(8,128)S(1)} %multiply_add_fusion.14), channel_id=1, source_target_pairs={{0,4},{4,8},{8,12},{12,16},{16,20},{20,24},{24,28},{1,5},{5,9},{9,... | collective-permute-start | bytes 98312 | tf_op jit(solution)/shard_map/while/body/eval_jaxpr/ppermute | solution.py:19
  325.3 93.6 %collective-permute-start = (f32[8,2,8,64,64]{4,3,2,1,0:T(8,128)}, f32[8,2,8,64,64]{4,3,2,1,0:T(8,128)}, u32[]{:S(2)}, u32[]{:S(2)}) collective-permute-start(f32[8,2,8,64,64]{4,3,2,1,0:T(8,128)} %multiply_add_fusion.13), channel_id=1, source_target_pairs={{0,4},{4,8},{8,12},{12,16},{16,20},{20,24},{24,28},{1,5},{5,9},{9,... | collective-permute-start | bytes 6291464 | tf_op jit(solution)/shard_map/while/body/eval_jaxpr/ppermute | solution.py:19
  331.8 87.1 %collective-permute-start.1 = (f32[8,2,8,64]{3,2,1,0:T(8,128)S(1)}, f32[8,2,8,64]{3,2,1,0:T(8,128)S(1)}, u32[]{:S(2)}, u32[]{:S(2)}) collective-permute-start(f32[8,2,8,64]{3,2,1,0:T(8,128)S(1)} %multiply_add_fusion.14), channel_id=1, source_target_pairs={{0,4},{4,8},{8,12},{12,16},{16,20},{20,24},{24,28},{1,5},{5,9},{9,... | collective-permute-start | bytes 98312 | tf_op jit(solution)/shard_map/while/body/eval_jaxpr/ppermute | solution.py:19
  425.9 93.6 %collective-permute-start = (f32[8,2,8,64,64]{4,3,2,1,0:T(8,128)}, f32[8,2,8,64,64]{4,3,2,1,0:T(8,128)}, u32[]{:S(2)}, u32[]{:S(2)}) collective-permute-start(f32[8,2,8,64,64]{4,3,2,1,0:T(8,128)} %multiply_add_fusion.13), channel_id=1, source_target_pairs={{0,4},{4,8},{8,12},{12,16},{16,20},{20,24},{24,28},{1,5},{5,9},{9,... | collective-permute-start | bytes 6291464 | tf_op jit(solution)/shard_map/while/body/eval_jaxpr/ppermute | solution.py:19
  433.2 86.2 %collective-permute-start.1 = (f32[8,2,8,64]{3,2,1,0:T(8,128)S(1)}, f32[8,2,8,64]{3,2,1,0:T(8,128)S(1)}, u32[]{:S(2)}, u32[]{:S(2)}) collective-permute-start(f32[8,2,8,64]{3,2,1,0:T(8,128)S(1)} %multiply_add_fusion.14), channel_id=1, source_target_pairs={{0,4},{4,8},{8,12},{12,16},{16,20},{20,24},{24,28},{1,5},{5,9},{9,... | collective-permute-start | bytes 98312 | tf_op jit(solution)/shard_map/while/body/eval_jaxpr/ppermute | solution.py:19
  526.5 92.9 %collective-permute-start = (f32[8,2,8,64,64]{4,3,2,1,0:T(8,128)}, f32[8,2,8,64,64]{4,3,2,1,0:T(8,128)}, u32[]{:S(2)}, u32[]{:S(2)}) collective-permute-start(f32[8,2,8,64,64]{4,3,2,1,0:T(8,128)} %multiply_add_fusion.13), channel_id=1, source_target_pairs={{0,4},{4,8},{8,12},{12,16},{16,20},{20,24},{24,28},{1,5},{5,9},{9,... | collective-permute-start | bytes 6291464 | tf_op jit(solution)/shard_map/while/body/eval_jaxpr/ppermute | solution.py:19
  626.3 92.1 %collective-permute-start = (f32[8,2,8,64,64]{4,3,2,1,0:T(8,128)}, f32[8,2,8,64,64]{4,3,2,1,0:T(8,128)}, u32[]{:S(2)}, u32[]{:S(2)}) collective-permute-start(f32[8,2,8,64,64]{4,3,2,1,0:T(8,128)} %multiply_add_fusion.13), channel_id=1, source_target_pairs={{0,4},{4,8},{8,12},{12,16},{16,20},{20,24},{24,28},{1,5},{5,9},{9,... | collective-permute-start | bytes 6291464 | tf_op jit(solution)/shard_map/while/body/eval_jaxpr/ppermute | solution.py:19
  725.4 91.3 %collective-permute-start = (f32[8,2,8,64,64]{4,3,2,1,0:T(8,128)}, f32[8,2,8,64,64]{4,3,2,1,0:T(8,128)}, u32[]{:S(2)}, u32[]{:S(2)}) collective-permute-start(f32[8,2,8,64,64]{4,3,2,1,0:T(8,128)} %multiply_add_fusion.13), channel_id=1, source_target_pairs={{0,4},{4,8},{8,12},{12,16},{16,20},{20,24},{24,28},{1,5},{5,9},{9,... | collective-permute-start | bytes 6291464 | tf_op jit(solution)/shard_map/while/body/eval_jaxpr/ppermute | solution.py:19
  952.2 91.2 %collective-permute-start.2 = (f32[8,2,8,64,64]{4,3,2,1,0:T(8,128)}, f32[8,2,8,64,64]{4,3,2,1,0:T(8,128)}, u32[]{:S(2)}, u32[]{:S(2)}) collective-permute-start(f32[8,2,8,64,64]{4,3,2,1,0:T(8,128)} %multiply_add_fusion.15), channel_id=1, source_target_pairs={{4,0},{8,4},{12,8},{16,12},{20,16},{24,20},{28,24},{5,1},{9,5},{13... | collective-permute-start | bytes 6291464 | tf_op jit(solution)/shard_map/while/body/eval_jaxpr/ppermute | solution.py:19
  954.2 89.2 %collective-permute-start.3 = (f32[8,2,8,64]{3,2,1,0:T(8,128)}, f32[8,2,8,64]{3,2,1,0:T(8,128)S(1)}, u32[]{:S(2)}, u32[]{:S(2)}) collective-permute-start(f32[8,2,8,64]{3,2,1,0:T(8,128)} %multiply_add_fusion.16), channel_id=1, source_target_pairs={{4,0},{8,4},{12,8},{16,12},{20,16},{24,20},{28,24},{5,1},{9,5},{13... | collective-permute-start | bytes 98312 | tf_op jit(solution)/shard_map/while/body/eval_jaxpr/ppermute | solution.py:19
  1050.4 90.7 %collective-permute-start.2 = (f32[8,2,8,64,64]{4,3,2,1,0:T(8,128)}, f32[8,2,8,64,64]{4,3,2,1,0:T(8,128)}, u32[]{:S(2)}, u32[]{:S(2)}) collective-permute-start(f32[8,2,8,64,64]{4,3,2,1,0:T(8,128)} %multiply_add_fusion.15), channel_id=1, source_target_pairs={{4,0},{8,4},{12,8},{16,12},{20,16},{24,20},{28,24},{5,1},{9,5},{13... | collective-permute-start | bytes 6291464 | tf_op jit(solution)/shard_map/while/body/eval_jaxpr/ppermute | solution.py:19
  1052.4 88.7 %collective-permute-start.3 = (f32[8,2,8,64]{3,2,1,0:T(8,128)}, f32[8,2,8,64]{3,2,1,0:T(8,128)S(1)}, u32[]{:S(2)}, u32[]{:S(2)}) collective-permute-start(f32[8,2,8,64]{3,2,1,0:T(8,128)} %multiply_add_fusion.16), channel_id=1, source_target_pairs={{4,0},{8,4},{12,8},{16,12},{20,16},{24,20},{28,24},{5,1},{9,5},{13... | collective-permute-start | bytes 98312 | tf_op jit(solution)/shard_map/while/body/eval_jaxpr/ppermute | solution.py:19
  1148.1 89.1 %collective-permute-start.2 = (f32[8,2,8,64,64]{4,3,2,1,0:T(8,128)}, f32[8,2,8,64,64]{4,3,2,1,0:T(8,128)}, u32[]{:S(2)}, u32[]{:S(2)}) collective-permute-start(f32[8,2,8,64,64]{4,3,2,1,0:T(8,128)} %multiply_add_fusion.15), channel_id=1, source_target_pairs={{4,0},{8,4},{12,8},{16,12},{20,16},{24,20},{28,24},{5,1},{9,5},{13... | collective-permute-start | bytes 6291464 | tf_op jit(solution)/shard_map/while/body/eval_jaxpr/ppermute | solution.py:19
  1150.1 87.1 %collective-permute-start.3 = (f32[8,2,8,64]{3,2,1,0:T(8,128)}, f32[8,2,8,64]{3,2,1,0:T(8,128)S(1)}, u32[]{:S(2)}, u32[]{:S(2)}) collective-permute-start(f32[8,2,8,64]{3,2,1,0:T(8,128)} %multiply_add_fusion.16), channel_id=1, source_target_pairs={{4,0},{8,4},{12,8},{16,12},{20,16},{24,20},{28,24},{5,1},{9,5},{13... | collective-permute-start | bytes 98312 | tf_op jit(solution)/shard_map/while/body/eval_jaxpr/ppermute | solution.py:19
  1244.2 88.3 %collective-permute-start.2 = (f32[8,2,8,64,64]{4,3,2,1,0:T(8,128)}, f32[8,2,8,64,64]{4,3,2,1,0:T(8,128)}, u32[]{:S(2)}, u32[]{:S(2)}) collective-permute-start(f32[8,2,8,64,64]{4,3,2,1,0:T(8,128)} %multiply_add_fusion.15), channel_id=1, source_target_pairs={{4,0},{8,4},{12,8},{16,12},{20,16},{24,20},{28,24},{5,1},{9,5},{13... | collective-permute-start | bytes 6291464 | tf_op jit(solution)/shard_map/while/body/eval_jaxpr/ppermute | solution.py:19
  1246.2 86.3 %collective-permute-start.3 = (f32[8,2,8,64]{3,2,1,0:T(8,128)}, f32[8,2,8,64]{3,2,1,0:T(8,128)S(1)}, u32[]{:S(2)}, u32[]{:S(2)}) collective-permute-start(f32[8,2,8,64]{3,2,1,0:T(8,128)} %multiply_add_fusion.16), channel_id=1, source_target_pairs={{4,0},{8,4},{12,8},{16,12},{20,16},{24,20},{28,24},{5,1},{9,5},{13... | collective-permute-start | bytes 98312 | tf_op jit(solution)/shard_map/while/body/eval_jaxpr/ppermute | solution.py:19
  1339.5 87.4 %collective-permute-start.2 = (f32[8,2,8,64,64]{4,3,2,1,0:T(8,128)}, f32[8,2,8,64,64]{4,3,2,1,0:T(8,128)}, u32[]{:S(2)}, u32[]{:S(2)}) collective-permute-start(f32[8,2,8,64,64]{4,3,2,1,0:T(8,128)} %multiply_add_fusion.15), channel_id=1, source_target_pairs={{4,0},{8,4},{12,8},{16,12},{20,16},{24,20},{28,24},{5,1},{9,5},{13... | collective-permute-start | bytes 6291464 | tf_op jit(solution)/shard_map/while/body/eval_jaxpr/ppermute | solution.py:19
  1433.9 86.6 %collective-permute-start.2 = (f32[8,2,8,64,64]{4,3,2,1,0:T(8,128)}, f32[8,2,8,64,64]{4,3,2,1,0:T(8,128)}, u32[]{:S(2)}, u32[]{:S(2)}) collective-permute-start(f32[8,2,8,64,64]{4,3,2,1,0:T(8,128)} %multiply_add_fusion.15), channel_id=1, source_target_pairs={{4,0},{8,4},{12,8},{16,12},{20,16},{24,20},{28,24},{5,1},{9,5},{13... | collective-permute-start | bytes 6291464 | tf_op jit(solution)/shard_map/while/body/eval_jaxpr/ppermute | solution.py:19
  (82 other events, 2189.3 us)
Sparse Core Ops, SparseCore 0:
  1736.5 246.3 all-reduce.6
where the time goes:
time: 2010 us; the launch traced here: 2000 us
  waiting for transfers between devices  1360 us (68%)
  matrix products  214 us (11%)
  other arithmetic  141 us (7%)
  local copies, waits for them, and re-layouts  126 us (6%)
  starting transfers between devices  97 us (5%)
  blocking collectives  48.9 us (2%)
    ppermute x32, waiting for transfers between devices, shifted(): return lax.ppermute(array, axis, pairs)  1180 us
    psum x1, waiting for transfers between devices, local(): lax.psum((d_w_query, d_w_key, d_w_value, d_w_out, ffn_grads[0], ffn_grads...  179 us
    add x14, other arithmetic, join(): later[0] + carry_on[:, None, None, None, None] * earlier[0]  97.8 us
    ppermute x32, starting transfers between devices, shifted(): return lax.ppermute(array, axis, pairs)  96.9 us
    psum x1, blocking collectives, local(): lax.psum((d_w_query, d_w_key, d_w_value, d_w_out, ffn_grads[0], ffn_grads...  48.9 us
  transfers between devices with their start and end apart: 33, of which 15 were waited for; matrix products, arithmetic and copies ran while one was open for 15% of the time, Pallas kernels for 0%

commit v1 on v0

v1 whole, which is shorter than its diff:
```python
import functools

import jax
import jax.numpy as jnp
from jax import lax
from jax.experimental import pallas as pl
from jax.experimental.pallas import tpu as pltpu
from jax.sharding import PartitionSpec as P

HEADS = 8
HEAD = 64
BAND = 30
EPSILON = 1e-06
SCALE = 0.125
CHUNK = 128
BLOCK = 256
PAIRS = HEADS // 2
NEG = -1e30
GELU_A = 0.7978845608028654
GELU_B = 0.044715
F32 = jnp.float32
BF16 = jnp.bfloat16
VMEM_LIMIT = 56 * 1024 * 1024


def nn(a, b):
    return lax.dot_general(a, b, (((1,), (0,)), ((), ())), preferred_element_type=F32)


def nt(a, b):
    return lax.dot_general(a, b, (((1,), (1,)), ((), ())), preferred_element_type=F32)


def tn(a, b):
    return lax.dot_general(a, b, (((0,), (0,)), ((), ())), preferred_element_type=F32)


def low_lanes(shape):
    return lax.broadcasted_iota(jnp.int32, shape, len(shape) - 1) < HEAD


def split_heads(pair):
    low = low_lanes(pair.shape)
    zero = jnp.zeros_like(pair)
    return jnp.concatenate([jnp.where(low, pair, zero), jnp.where(low, zero, pair)], 0)


def with_ones(pair):
    low = low_lanes(pair.shape)
    one = jnp.ones_like(pair)
    return jnp.where(low, pair, one), jnp.where(low, one, pair)


def pick(top, bottom):
    return jnp.where(low_lanes(top.shape), top, bottom)


def elu_one(t):
    return jnp.where(t > 0, t + 1.0, jnp.exp(jnp.minimum(t, 0.0)))


def chunk_masks(segc_ref, segr_ref, chunk):
    seg_q = segc_ref[chunk + 1]
    seg_prev = segr_ref[chunk]
    seg_own = segr_ref[chunk + 1]
    row = lax.broadcasted_iota(jnp.int32, (CHUNK, CHUNK), 0)
    col = lax.broadcasted_iota(jnp.int32, (CHUNK, CHUNK), 1)
    same_own = seg_q == seg_own
    same_prev = seg_q == seg_prev
    gap = row - col
    far = same_own & (gap >= 0)
    band_own = far & (gap <= BAND)
    band_prev = same_prev & (gap + CHUNK <= BAND)
    band = jnp.concatenate([band_prev, band_own], 1)
    before = seg_prev[:, CHUNK - 1 :]
    last = seg_own[:, CHUNK - 1 :]
    carry = seg_q == before
    tail = seg_q == last
    keep = (before == last).astype(F32)
    return (
        jnp.concatenate([band, band], 0),
        jnp.concatenate([far, far], 0),
        carry,
        tail,
        keep,
    )


def forward_kernel(
    x_ref, segc_ref, segr_ref, ga_ref, gf_ref, wq_ref, wk_ref, wv_ref, wo_ref, wu_ref, wd_ref,
    s0_ref, k0_ref, v0_ref,
    out_ref, x1_ref, a_ref, q_ref, k_ref, v_ref, lse_ref, far1_ref, far2_ref, iz1_ref, iz2_ref,
    states_ref, s_end_ref,
    s_ref, kp_ref, vp_ref,
):
    step = pl.program_id(0)

    @pl.when(step == 0)
    def _():
        s_ref[...] = s0_ref[...]
        kp_ref[...] = k0_ref[...]
        vp_ref[...] = v0_ref[...]

    x = x_ref[...].astype(F32)
    inv = lax.rsqrt(jnp.mean(x * x, -1, keepdims=True) + EPSILON)
    hidden = (x * inv * ga_ref[...]).astype(BF16)
    q_ref[...] = nn(hidden, wq_ref[...]).astype(BF16)
    k_ref[...] = nn(hidden, wk_ref[...]).astype(BF16)
    v_ref[...] = nn(hidden, wv_ref[...]).astype(BF16)
    far_refs = (far1_ref, far2_ref)
    iz_refs = (iz1_ref, iz2_ref)
    lane = lax.broadcasted_iota(jnp.int32, (CHUNK, CHUNK), 1)
    row_low = lax.broadcasted_iota(jnp.int32, (CHUNK, CHUNK), 0) < HEAD
    for sub in range(BLOCK // CHUNK):
        rows = slice(sub * CHUNK, (sub + 1) * CHUNK)
        chunk = step * (BLOCK // CHUNK) + sub
        band, far_mask, carry, tail, keep = chunk_masks(segc_ref, segr_ref, chunk)
        carry = carry.astype(BF16)
        tail = tail.astype(BF16)
        lse_all = jnp.zeros((CHUNK, CHUNK), F32)
        for p in range(PAIRS):
            lanes = slice(p * 128, (p + 1) * 128)
            qp = q_ref[rows, lanes]
            kp = k_ref[rows, lanes]
            vp = v_ref[rows, lanes]
            k_ext = jnp.concatenate([kp_ref[:, lanes], kp], 0)
            v_ext = jnp.concatenate([vp_ref[:, lanes], vp], 0)
            score = nt(split_heads(qp * SCALE), k_ext)
            score = jnp.where(band, score, NEG)
            top = jnp.max(score, -1, keepdims=True)
            expo = jnp.exp(score - top).astype(BF16)
            one0, one1 = with_ones(v_ext)
            acc0 = nn(expo[:CHUNK], one0)
            acc1 = nn(expo[CHUNK:], one1)
            total = pltpu.roll(pick(acc1, acc0), HEAD, 1)
            attended = pick(acc0, acc1) / total
            log_total = jnp.log(total)
            lse_all = jnp.where(lane == 2 * p, top[:CHUNK] + log_total[:, :1], lse_all)
            lse_all = jnp.where(
                lane == 2 * p + 1, top[CHUNK:] + log_total[:, HEAD : HEAD + 1], lse_all
            )
            qf = qp.astype(F32)
            kf = kp.astype(F32)
            own0, own1 = one0[CHUNK:], one1[CHUNK:]
            own01 = jnp.concatenate([own0, own1], 1)
            for m in range(2):
                if m == 0:
                    fq, fk = elu_one(qf).astype(BF16), elu_one(kf).astype(BF16)
                else:
                    fq, fk = (1.0 + jnp.tanh(qf)).astype(BF16), (1.0 + jnp.tanh(kf)).astype(BF16)
                state = s_ref[2 * p + m]
                state_low = state.astype(BF16)
                states_ref[sub, 2 * p + m] = state_low
                fq2 = split_heads(fq)
                weight = jnp.where(far_mask, nt(fq2, fk), 0.0).astype(BF16)
                fq2 = split_heads(fq * carry)
                acc0 = nn(weight[:CHUNK], own0) + nn(fq2[:CHUNK], state_low)
                acc1 = nn(weight[CHUNK:], own1) + nn(fq2[CHUNK:], state_low)
                inv_z = 1.0 / pltpu.roll(pick(acc1, acc0), HEAD, 1)
                far = pick(acc0, acc1) * inv_z
                attended = attended + far
                far_refs[m][rows, lanes] = far.astype(BF16)
                iz_refs[m][rows, lanes] = inv_z.astype(BF16)
                update = tn(fk * tail, own01)
                s_ref[2 * p + m] = keep * state + jnp.where(
                    row_low, update[:, :CHUNK], update[:, CHUNK:]
                )
            a_ref[rows, lanes] = attended.astype(BF16)
        lse_ref[rows] = lse_all
        kp_ref[...] = k_ref[rows]
        vp_ref[...] = v_ref[rows]
    s_end_ref[...] = s_ref[...]
    x1 = x + nn(a_ref[...], wo_ref[...])
    x1_ref[...] = x1
    inv = lax.rsqrt(jnp.mean(x1 * x1, -1, keepdims=True) + EPSILON)
    hidden = (x1 * inv * gf_ref[...]).astype(BF16)
    total = x1
    width = 512
    for f in range(wu_ref.shape[1] // width):
        cols = slice(f * width, (f + 1) * width)
        up = nn(hidden, wu_ref[:, cols])
        act = 0.5 * up * (1.0 + jnp.tanh(GELU_A * (up + GELU_B * up * up * up)))
        total = total + nn(act.astype(BF16), wd_ref[cols])
    out_ref[...] = total.astype(BF16)


def norm_backward(x, gain, grad):
    inv = lax.rsqrt(jnp.mean(x * x, -1, keepdims=True) + EPSILON)
    unit = x * inv
    scaled = grad * gain
    d_gain = jnp.sum(grad * unit, 0, keepdims=True)
    return inv * (scaled - unit * jnp.mean(unit * scaled, -1, keepdims=True)), d_gain


def ffn_backward_kernel(
    dy_ref, x1_ref, a_ref, gf_ref, wo_ref, wu_ref, wd_ref,
    dx1_ref, da_ref, dwd_ref, dwu_ref, dwo_ref, dg_ref,
    dwd_acc, dwu_acc, dwo_acc, dg_acc,
):
    step = pl.program_id(0)

    @pl.when(step == 0)
    def _():
        dwd_acc[...] = jnp.zeros_like(dwd_acc)
        dwu_acc[...] = jnp.zeros_like(dwu_acc)
        dwo_acc[...] = jnp.zeros_like(dwo_acc)
        dg_acc[...] = jnp.zeros_like(dg_acc)

    dy = dy_ref[...]
    x1 = x1_ref[...]
    gain = gf_ref[...]
    inv = lax.rsqrt(jnp.mean(x1 * x1, -1, keepdims=True) + EPSILON)
    hidden = (x1 * inv * gain).astype(BF16)
    d_hidden = jnp.zeros(x1.shape, F32)
    width = 512
    for f in range(wu_ref.shape[1] // width):
        cols = slice(f * width, (f + 1) * width)
        up = nn(hidden, wu_ref[:, cols])
        square = up * up
        tanh = jnp.tanh(GELU_A * up * (1.0 + GELU_B * square))
        half = 0.5 * (1.0 + tanh)
        act = (up * half).astype(BF16)
        slope = half + 0.5 * up * (1.0 - tanh * tanh) * (
            GELU_A + (3.0 * GELU_A * GELU_B) * square
        )
        d_up = (slope * nt(dy, wd_ref[cols])).astype(BF16)
        dwd_acc[cols] += tn(act, dy)
        dwu_acc[:, cols] += tn(hidden, d_up)
        d_hidden = d_hidden + nt(d_up, wu_ref[:, cols])
    d_norm, d_gain = norm_backward(x1, gain, d_hidden)
    dx1 = dy.astype(F32) + d_norm
    dg_acc[...] += jnp.broadcast_to(d_gain, dg_acc.shape)
    dx1_ref[...] = dx1
    d_branch = dx1.astype(BF16)
    dwo_acc[...] += tn(a_ref[...], d_branch)
    da_ref[...] = nt(d_branch, wo_ref[...]).astype(BF16)

    @pl.when(step == pl.num_programs(0) - 1)
    def _():
        dwd_ref[...] = dwd_acc[...].astype(BF16)
        dwu_ref[...] = dwu_acc[...].astype(BF16)
        dwo_ref[...] = dwo_acc[...].astype(BF16)
        dg_ref[...] = dg_acc[...]


def attention_backward_kernel(
    x_ref, dx1_ref, da_ref, q_ref, k_ref, v_ref, kprev_ref, vprev_ref,
    lse_ref, far1_ref, far2_ref, iz1_ref, iz2_ref,
    states_ref, segc_ref, segr_ref, ga_ref, wq_ref, wk_ref, wv_ref, r0_ref, dk0_ref, dv0_ref,
    dx_ref, dwq_ref, dwk_ref, dwv_ref, dg_ref, r_end_ref, dk_end_ref, dv_end_ref,
    r_ref, dkc_ref, dvc_ref, dq_ref, dk_ref, dv_ref, dwq_acc, dwk_acc, dwv_acc, dg_acc,
):
    step = pl.program_id(0)
    block = pl.num_programs(0) - 1 - step

    @pl.when(step == 0)
    def _():
        r_ref[...] = r0_ref[...]
        dkc_ref[...] = dk0_ref[...]
        dvc_ref[...] = dv0_ref[...]
        dwq_acc[...] = jnp.zeros_like(dwq_acc)
        dwk_acc[...] = jnp.zeros_like(dwk_acc)
        dwv_acc[...] = jnp.zeros_like(dwv_acc)
        dg_acc[...] = jnp.zeros_like(dg_acc)

    far_refs = (far1_ref, far2_ref)
    iz_refs = (iz1_ref, iz2_ref)
    row_low = lax.broadcasted_iota(jnp.int32, (CHUNK, CHUNK), 0) < HEAD
    lane_low = lax.broadcasted_iota(jnp.int32, (CHUNK, CHUNK), 1) < HEAD
    diagonal = row_low == lane_low
    swap = jnp.where(diagonal, 0.0, -1.0 / HEAD).astype(BF16)
    for sub in reversed(range(BLOCK // CHUNK)):
        rows = slice(sub * CHUNK, (sub + 1) * CHUNK)
        chunk = block * (BLOCK // CHUNK) + sub
        band, far_mask, carry, tail, keep = chunk_masks(segc_ref, segr_ref, chunk)
        carry = carry.astype(BF16)
        tail = tail.astype(BF16)
        lse_all = lse_ref[rows]
        for p in range(PAIRS):
            lanes = slice(p * 128, (p + 1) * 128)
            qp = q_ref[rows, lanes]
            kp = k_ref[rows, lanes]
            vp = v_ref[rows, lanes]
            da = da_ref[rows, lanes]
            if sub == 0:
                k_prev, v_prev = kprev_ref[:, lanes], vprev_ref[:, lanes]
            else:
                before = slice((sub - 1) * CHUNK, sub * CHUNK)
                k_prev, v_prev = k_ref[before, lanes], v_ref[before, lanes]
            k_ext = jnp.concatenate([k_prev, kp], 0)
            v_ext = jnp.concatenate([v_prev, vp], 0)
            q2 = split_heads(qp * SCALE)
            lse = jnp.concatenate(
                [lse_all[:, 2 * p : 2 * p + 1], lse_all[:, 2 * p + 1 : 2 * p + 2]], 0
            )
            prob = jnp.exp(jnp.where(band, nt(q2, k_ext) - lse, NEG))
            da2 = split_heads(da)
            d_prob = nt(da2, v_ext)
            delta = jnp.sum(prob * d_prob, -1, keepdims=True)
            d_score = (prob * (d_prob - delta)).astype(BF16)
            dq2 = nn(d_score, k_ext)
            dq = SCALE * pick(dq2[:CHUNK], dq2[CHUNK:])
            dk_ext = tn(d_score, q2)
            dv_ext = tn(prob.astype(BF16), da2)
            dk = dk_ext[CHUNK:] + dkc_ref[:, lanes]
            dv = dv_ext[CHUNK:] + dvc_ref[:, lanes]
            dkc_ref[:, lanes] = dk_ext[:CHUNK]
            dvc_ref[:, lanes] = dv_ext[:CHUNK]
            qf = qp.astype(F32)
            kf = kp.astype(F32)
            daf = da.astype(F32)
            one0, one1 = with_ones(vp)
            for m in range(2):
                if m == 0:
                    exp_q = jnp.exp(jnp.minimum(qf, 0.0))
                    exp_k = jnp.exp(jnp.minimum(kf, 0.0))
                    fq = jnp.where(qf > 0, qf + 1.0, exp_q).astype(BF16)
                    fk = jnp.where(kf > 0, kf + 1.0, exp_k).astype(BF16)
                    slope_q, slope_k = exp_q, exp_k
                else:
                    tanh_q, tanh_k = jnp.tanh(qf), jnp.tanh(kf)
                    fq, fk = (1.0 + tanh_q).astype(BF16), (1.0 + tanh_k).astype(BF16)
                    slope_q, slope_k = 1.0 - tanh_q * tanh_q, 1.0 - tanh_k * tanh_k
                state = states_ref[sub, 2 * p + m]
                back = r_ref[2 * p + m]
                back_low = back.astype(BF16)
                d_num = daf * iz_refs[m][rows, lanes].astype(F32)
                d_num_low = d_num.astype(BF16)
                d_den = nn((d_num * far_refs[m][rows, lanes].astype(F32)).astype(BF16), swap)
                d_den = d_den.astype(BF16)
                grad0 = pick(d_num_low, d_den)
                grad1 = pick(d_den, d_num_low)
                fq2 = split_heads(fq)
                weight = jnp.where(far_mask, nt(fq2, fk), 0.0).astype(BF16)
                d_weight = jnp.concatenate([nt(grad0, one0), nt(grad1, one1)], 0)
                d_weight = jnp.where(far_mask, d_weight, 0.0).astype(BF16)
                grad01 = jnp.concatenate([grad0, grad1], 0)
                carry2 = jnp.concatenate([carry, carry], 0)
                dfq2 = nn(d_weight, fk) + nt(grad01 * carry2, state)
                dfq = pick(dfq2[:CHUNK], dfq2[CHUNK:])
                dfk = tn(d_weight, fq2) + pick(
                    nt(one0 * tail, back_low), nt(one1 * tail, back_low)
                )
                dv = dv + tn(weight, split_heads(d_num_low))
                dv = dv + nn(fk * tail, jnp.where(diagonal, back_low, jnp.zeros_like(back_low)))
                dq = dq + slope_q * dfq
                dk = dk + slope_k * dfk
                update = tn(fq * carry, jnp.concatenate([grad0, grad1], 1))
                r_ref[2 * p + m] = keep * back + jnp.where(
                    row_low, update[:, :CHUNK], update[:, CHUNK:]
                )
            dq_ref[rows, lanes] = dq.astype(BF16)
            dk_ref[rows, lanes] = dk.astype(BF16)
            dv_ref[rows, lanes] = dv.astype(BF16)
    r_end_ref[...] = r_ref[...]
    dk_end_ref[...] = dkc_ref[...]
    dv_end_ref[...] = dvc_ref[...]
    x = x_ref[...].astype(F32)
    gain = ga_ref[...]
    inv = lax.rsqrt(jnp.mean(x * x, -1, keepdims=True) + EPSILON)
    hidden = (x * inv * gain).astype(BF16)
    dwq_acc[...] += tn(hidden, dq_ref[...])
    dwk_acc[...] += tn(hidden, dk_ref[...])
    dwv_acc[...] += tn(hidden, dv_ref[...])
    d_hidden = (
        nt(dq_ref[...], wq_ref[...])
        + nt(dk_ref[...], wk_ref[...])
        + nt(dv_ref[...], wv_ref[...])
    )
    d_norm, d_gain = norm_backward(x, gain, d_hidden)
    dg_acc[...] += jnp.broadcast_to(d_gain, dg_acc.shape)
    dx_ref[...] = (dx1_ref[...] + d_norm).astype(BF16)

    @pl.when(step == pl.num_programs(0) - 1)
    def _():
        dwq_ref[...] = dwq_acc[...].astype(BF16)
        dwk_ref[...] = dwk_acc[...].astype(BF16)
        dwv_ref[...] = dwv_acc[...].astype(BF16)
        dg_ref[...] = dg_acc[...]


def whole(shape):
    return pl.BlockSpec(shape, lambda i: (0,) * len(shape))


def tokens_of(width, index=lambda i: i):
    return pl.BlockSpec((BLOCK, width), lambda i: (index(i), 0))


def params():
    return pltpu.CompilerParams(
        vmem_limit_bytes=VMEM_LIMIT, dimension_semantics=("arbitrary",)
    )


def sds(shape, dtype):
    return jax.ShapeDtypeStruct(shape, dtype)


def run_forward(x, segc, segr, gain_attn, gain_ffn, wq, wk, wv, wo, wu, wd, s0, k0, v0):
    length, dim = x.shape
    ff = wu.shape[1]
    chunks = length // CHUNK
    steps = length // BLOCK
    per = BLOCK // CHUNK
    row = tokens_of(dim)
    state_shape = (HEADS, CHUNK, CHUNK)
    return pl.pallas_call(
        forward_kernel,
        grid=(steps,),
        in_specs=[
            row, whole(segc.shape), whole(segr.shape), whole((1, dim)), whole((1, dim)),
            whole((dim, dim)), whole((dim, dim)), whole((dim, dim)), whole((dim, dim)),
            whole((dim, ff)), whole((ff, dim)),
            whole(state_shape), whole((CHUNK, dim)), whole((CHUNK, dim)),
        ],
        out_specs=[
            row, row, row, row, row, row, tokens_of(CHUNK), row, row, row, row,
            pl.BlockSpec((per,) + state_shape, lambda i: (i, 0, 0, 0)),
            whole(state_shape),
        ],
        out_shape=[
            sds((length, dim), BF16), sds((length, dim), F32), sds((length, dim), BF16),
            sds((length, dim), BF16), sds((length, dim), BF16), sds((length, dim), BF16),
            sds((length, CHUNK), F32),
            sds((length, dim), BF16), sds((length, dim), BF16),
            sds((length, dim), BF16), sds((length, dim), BF16),
            sds((chunks,) + state_shape, BF16), sds(state_shape, F32),
        ],
        scratch_shapes=[
            pltpu.VMEM(state_shape, F32),
            pltpu.VMEM((CHUNK, dim), BF16),
            pltpu.VMEM((CHUNK, dim), BF16),
        ],
        compiler_params=params(),
        name="layer_forward",
    )(x, segc, segr, gain_attn, gain_ffn, wq, wk, wv, wo, wu, wd, s0, k0, v0)


def run_ffn_backward(dy, x1, a, gain_ffn, wo, wu, wd):
    length, dim = dy.shape
    ff = wu.shape[1]
    row = tokens_of(dim)
    return pl.pallas_call(
        ffn_backward_kernel,
        grid=(length // BLOCK,),
        in_specs=[
            row, row, row, whole((1, dim)), whole((dim, dim)), whole((dim, ff)), whole((ff, dim)),
        ],
        out_specs=[
            row, row, whole((ff, dim)), whole((dim, ff)), whole((dim, dim)), whole((8, dim)),
        ],
        out_shape=[
            sds((length, dim), F32), sds((length, dim), BF16),
            sds((ff, dim), BF16), sds((dim, ff), BF16), sds((dim, dim), BF16), sds((8, dim), F32),
        ],
        scratch_shapes=[
            pltpu.VMEM((ff, dim), F32), pltpu.VMEM((dim, ff), F32),
            pltpu.VMEM((dim, dim), F32), pltpu.VMEM((8, dim), F32),
        ],
        compiler_params=params(),
        name="ffn_backward",
    )(dy, x1, a, gain_ffn, wo, wu, wd)


def run_attention_backward(
    x, dx1, da, q, k, v, k0, v0, lse, far1, far2, iz1, iz2, states, segc, segr, gain_attn,
    wq, wk, wv, r0, dk0, dv0,
):
    length, dim = x.shape
    steps = length // BLOCK
    per = BLOCK // CHUNK
    state_shape = (HEADS, CHUNK, CHUNK)
    k_prev = jnp.concatenate([k0, k[: length - CHUNK]], 0)
    v_prev = jnp.concatenate([v0, v[: length - CHUNK]], 0)
    back = lambda i: steps - 1 - i
    row = tokens_of(dim, back)
    prev = pl.BlockSpec((CHUNK, dim), lambda i: (back(i) * per, 0))
    return pl.pallas_call(
        attention_backward_kernel,
        grid=(steps,),
        in_specs=[
            row, row, row, row, row, row, prev, prev, tokens_of(CHUNK, back),
            row, row, row, row,
            pl.BlockSpec((per,) + state_shape, lambda i: (back(i), 0, 0, 0)),
            whole(segc.shape), whole(segr.shape), whole((1, dim)),
            whole((dim, dim)), whole((dim, dim)), whole((dim, dim)),
            whole(state_shape), whole((CHUNK, dim)), whole((CHUNK, dim)),
        ],
        out_specs=[
            row, whole((dim, dim)), whole((dim, dim)), whole((dim, dim)), whole((8, dim)),
            whole(state_shape), whole((CHUNK, dim)), whole((CHUNK, dim)),
        ],
        out_shape=[
            sds((length, dim), BF16),
            sds((dim, dim), BF16), sds((dim, dim), BF16), sds((dim, dim), BF16), sds((8, dim), F32),
            sds(state_shape, F32), sds((CHUNK, dim), F32), sds((CHUNK, dim), F32),
        ],
        scratch_shapes=[
            pltpu.VMEM(state_shape, F32),
            pltpu.VMEM((CHUNK, dim), F32), pltpu.VMEM((CHUNK, dim), F32),
            pltpu.VMEM((BLOCK, dim), BF16), pltpu.VMEM((BLOCK, dim), BF16),
            pltpu.VMEM((BLOCK, dim), BF16),
            pltpu.VMEM((dim, dim), F32), pltpu.VMEM((dim, dim), F32), pltpu.VMEM((dim, dim), F32),
            pltpu.VMEM((8, dim), F32),
        ],
        compiler_params=params(),
        name="attention_backward",
    )(
        x, dx1, da, q, k, v, k_prev, v_prev, lse, far1, far2, iz1, iz2, states, segc, segr,
        gain_attn, wq, wk, wv, r0, dk0, dv0,
    )


def segment_views(seg_ext):
    chunks = seg_ext.shape[0] // CHUNK
    return seg_ext.reshape(chunks, CHUNK, 1), seg_ext.reshape(chunks, 1, CHUNK)


def local(
    tokens, segments, gain_attn, gain_ffn, w_query, w_key, w_value, w_out, w_up, w_down, cotangent
):
    row_count, shard_len, dim = tokens.shape
    seq_count = lax.axis_size("seq")
    parts = seq_count // row_count
    groups = [[g * row_count + r for r in range(row_count)] for g in range(parts)]
    length = row_count * shard_len
    index = lax.axis_index("seq")
    my_row = index % row_count
    my_part = index // row_count

    def trade(array):
        return lax.all_to_all(
            array.reshape(row_count, shard_len, dim), "seq", 0, 0, axis_index_groups=groups
        )

    def shifted(arrays, by):
        pairs = [
            (i, i + by * row_count)
            for i in range(seq_count)
            if 0 <= i + by * row_count < seq_count
        ]
        return lax.ppermute(arrays, "seq", pairs)

    seg_row = lax.dynamic_index_in_dim(segments, my_row, 0, False)
    seg_row = jnp.concatenate([jnp.full((CHUNK,), -1, jnp.int32), seg_row])
    seg_ext = lax.dynamic_slice_in_dim(seg_row, my_part * length, length + CHUNK, 0)
    segc, segr = segment_views(seg_ext)
    ga, gf = gain_attn.reshape(1, dim), gain_ffn.reshape(1, dim)

    x = trade(tokens).reshape(length, dim)
    dy = trade(cotangent).reshape(length, dim)
    state_zero = jnp.zeros((HEADS, CHUNK, CHUNK), F32)
    rim_zero = jnp.zeros((CHUNK, dim), BF16)
    entry = (state_zero, rim_zero, rim_zero)
    for turn in range(parts):
        (out, x1, a, q, k, v, lse, far1, far2, iz1, iz2, states, s_end) = run_forward(
            x, segc, segr, ga, gf, w_query, w_key, w_value, w_out, w_up, w_down, *entry
        )
        if turn < parts - 1:
            entry = shifted((s_end, k[length - CHUNK :], v[length - CHUNK :]), 1)
    output = trade(out)
    dx1, da, dwd, dwu, dwo, dgf = run_ffn_backward(dy, x1, a, gf, w_out, w_up, w_down)
    axes = ("seq", "rows")
    dwd, dwu, dwo = lax.psum((dwd, dwu, dwo), axes)
    grad_zero = jnp.zeros((CHUNK, dim), F32)
    back = (state_zero, grad_zero, grad_zero)
    for turn in range(parts):
        dx, dwq, dwk, dwv, dga, r_end, dk_end, dv_end = run_attention_backward(
            x, dx1, da, q, k, v, entry[1], entry[2], lse, far1, far2, iz1, iz2, states,
            segc, segr, ga, w_query, w_key, w_value, *back,
        )
        if turn < parts - 1:
            back = shifted((r_end, dk_end, dv_end), -1)
    d_tokens = trade(dx)
    dwq, dwk, dwv, dga, dgf = lax.psum((dwq, dwk, dwv, dga[0].astype(BF16), dgf[0].astype(BF16)), axes)
    wide = lambda array: array.astype(F32)
    return (
        output, d_tokens, wide(dga), wide(dgf),
        wide(dwq), wide(dwk), wide(dwv), wide(dwo), wide(dwu), wide(dwd),
    )


def solution(mesh):
    act = P("rows", "seq", None)
    return jax.shard_map(
        local,
        mesh=mesh,
        in_specs=(act, P("rows", None)) + (P(),) * 8 + (act,),
        out_specs=(act, act) + (P(),) * 8,
        check_vma=False,
    )
```

time: 2010 us -> 365 us (0.18)
  waiting for transfers between devices: 1360 us -> 117 us
  matrix products: 214 us -> 0 us
  other arithmetic: 141 us -> 13 us
  local copies, waits for them, and re-layouts: 126 us -> 10.2 us
  Pallas kernels: 0 us -> 106 us
  starting transfers between devices: 97 us -> 15.7 us
  blocking collectives: 48.9 us -> 87.8 us
    ppermute x32 -> x0, waiting for transfers between devices: 1180 us -> none  [shifted(): return lax.ppermute(array, axis, pairs)]
    dot_general x38 -> x0, matrix products: 214 us -> none  [the longest x6 21.9 us: dense(): return jnp.dot(matrix_a, matrix_b, preferred_element_type=jnp.float32)]
    pallas_call x0 -> x3, Pallas kernels: none -> 106 us  [the longest x1 49 us: run_attention_backward(): pl.pallas_call(attention_backward_kernel, grid=(steps,), in_specs=[row, r...]
    add x32 -> x0, other arithmetic: 104 us -> none  [the longest x14 97.8 us: join(): later[0] + carry_on[:, None, None, None, None] * earlier[0]]
    ppermute x32 -> x0, starting transfers between devices: 96.9 us -> none  [shifted(): return lax.ppermute(array, axis, pairs)]
    psum x1, waiting for transfers between devices: 179 us -> 117 us  [local(): lax.psum((dwq, dwk, dwv, dga[0].astype(BF16), dgf[0].astype(BF16)), axes)]
    all_to_all x0 -> x1, blocking collectives: none -> 33.1 us  [trade(): lax.all_to_all(array.reshape(row_count, shard_len, dim), 'seq', 0, 0, axi...]
    unnamed x155 -> x18, local copies, waits for them, and re-layouts: 34.2 us -> 2.4 us
  transfers between devices with their start and end apart: 33 -> 4, of which waited for: 15 -> 1; matrix products, arithmetic and copies ran while one was open for 15% -> 2% of each run, Pallas kernels for 0% -> 29%
where the time goes in v1:
time: 365 us; the launch traced here: 364 us
  waiting for transfers between devices  117 us (32%)
  Pallas kernels  106 us (29%)
  blocking collectives  87.8 us (24%)
  starting transfers between devices  15.7 us (4%)
  between operations  14.2 us (4%)
  other arithmetic  13 us (4%)
  local copies, waits for them, and re-layouts  10.2 us (3%)
    psum x1, waiting for transfers between devices, local(): lax.psum((dwq, dwk, dwv, dga[0].astype(BF16), dgf[0].astype(BF16)), axes)  117 us
    psum x1, blocking collectives, local(): lax.psum((dwq, dwk, dwv, dga[0].astype(BF16), dgf[0].astype(BF16)), axes)  54.7 us
    pallas_call x1, Pallas kernels, run_attention_backward(): pl.pallas_call(attention_backward_kernel, grid=(steps,), in_specs=[row, r...  49 us
    pallas_call x1, Pallas kernels, run_forward(): pl.pallas_call(forward_kernel, grid=(steps,), in_specs=[row, whole(segc.s...  34.1 us
    all_to_all x1, blocking collectives, trade(): lax.all_to_all(array.reshape(row_count, shard_len, dim), 'seq', 0, 0, axi...  33.1 us
    pallas_call x1, Pallas kernels, run_ffn_backward(): pl.pallas_call(ffn_backward_kernel, grid=(length // BLOCK,), in_specs=[ro...  23.3 us
    all_to_all x3, starting transfers between devices, trade(): lax.all_to_all(array.reshape(row_count, shard_len, dim), 'seq', 0, 0, axi...  15.5 us
    convert_element_type x8, other arithmetic, local(): wide = lambda array: array.astype(F32)  13 us
  transfers between devices with their start and end apart: 4, of which 1 were waited for; matrix products, arithmetic and copies ran while one was open for 2% of the time, Pallas kernels for 29%

profile of v1, /device:TPU:0, one launch (start us, length us, event | category | flops | bytes accessed | tf_op | source)
XLA Modules:
  0.0 364.4 jit_solution(16125167062825578058)
XLA Ops:
  7.2 33.1 %all_to_all.20 = bf16[8,128,512]{2,1,0:T(8,128)(2,1)} all-to-all(bf16[8,128,512]{2,1,0:T(8,128)(2,1)} %param.11), channel_id=1, replica_groups={{0,4,8,12,16,20,24,28},{1,5,9,13,17,21,25,29},{2,6,10,14,18,22,26,30},{..., dimensions={0} | all-to-all | bytes 2097152 | tf_op jit(solution)/shard_map/all_to_all | solution.py:533
  40.3 3.6 all-to-all-start.2
  44.0 1.1 copy.21.segc_ref
  45.6 0.9 broadcast_in_dim.10.s0_ref.r0_ref
  47.2 34.1 %layer_forward.1 = (bf16[1024,512]{1,0:T(8,128)(2,1)}, f32[1024,512]{1,0:T(8,128)}, bf16[1024,512]{1,0:T(8,128)(2,1)}, bf16[1024,512]{1,0:T(8,128)(2,1)}, bf16[1...) custom-call(bf16[1024,512]{1,0:T(8,128)(2,1)} %bitcast.9, ...), custom_call_target="tpu_custom_call" | custom-call | tf_op jit(solution)/shard_map/layer_forward/pallas_call | solution.py:408
  81.3 6.1 %all-to-all-start.1 = ((bf16[8,128,512]{2,1,0:T(8,128)(2,1)}), bf16[8,128,512]{2,1,0:T(8,128)(2,1)S(1)}, u32[]{:S(2)}, u32[]{:S(2)}) async-start(bf16[8,128,512]{2,1,0:T(8,128)(2,1)} %bitcast.12), calls=%async_computation.1 | async-start | bytes 2097152 | tf_op jit(solution)/shard_map/all_to_all | solution.py:533
  87.7 1.1 concatenate.10.kprev_ref
  89.3 1.1 concatenate.11.vprev_ref
  90.4 23.3 %ffn_backward.1 = (f32[1024,512]{1,0:T(8,128)}, bf16[1024,512]{1,0:T(8,128)(2,1)}, bf16[2048,512]{1,0:T(8,128)(2,1)}, bf16[512,2048]{1,0:T(8,128)(2,1)}, bf16[512,512]{1,0:T(8,128)(2,1)}, /*index=5*/f32[8,512]{1,0:T(8,128)}) custom-call(bf16[1024,512]{1,0:T(8,128)(2,1)} %bitcast.11, f32[1024,512]{1,0:T(8,128)} %get-tuple-element.34.x1_ref, ...), custom_call_target="tpu_custom_call" | custom-call | tf_op jit(solution)/shard_map/ffn_backward/pallas_call | solution.py:444
  113.7 0.7 broadcast_in_dim.12.dk0_ref.dv0_ref
  114.4 49.0 %attention_backward.1 = (bf16[1024,512]{1,0:T(8,128)(2,1)}, bf16[512,512]{1,0:T(8,128)(2,1)}, bf16[512,512]{1,0:T(8,128)(2,1)}, bf16[512,512]{1,0:T(8,128)(2,1)}...) custom-call(bf16[1024,512]{1,0:T(8,128)(2,1)} %bitcast.10, ...), custom_call_target="tpu_custom_call" | custom-call | tf_op jit(solution)/shard_map/attention_backward/pallas_call | solution.py:479
  163.5 5.8 %all-to-all-start.3 = ((bf16[8,128,512]{2,1,0:T(8,128)(2,1)}), bf16[8,128,512]{2,1,0:T(8,128)(2,1)S(1)}, u32[]{:S(2)}, u32[]{:S(2)}) async-start(bf16[8,128,512]{2,1,0:T(8,128)(2,1)} %bitcast.7), calls=%async_computation.3 | async-start | bytes 2097152 | tf_op jit(solution)/shard_map/all_to_all | solution.py:533
  169.2 0.7 fusion.1
  170.0 0.7 fusion
  170.7 54.7 %all-reduce.3 = (bf16[512]{0:T(512)(128)(2,1)S(1)}, bf16[512]{0:T(512)(128)(2,1)S(1)}) all-reduce(bf16[512]{0:T(512)(128)(2,1)S(1)} %fusion.1, bf16[512]{0:T(512)(128)(2,1)S(1)} %fusion), channel_id=1, replica_groups=mesh['seq'=8,'rows'=4] {'seq','rows'}, use_global_device_ids=true, to_apply=%region_0.1 | all-reduce | flops 1024 | bytes 4096 | tf_op jit(solution)/shard_map/psum | solution.py:576
  226.6 117.1 %all-reduce.7.cloned.1.call-done = (bf16[512,512]{1,0:T(8,128)(2,1)}, bf16[512,512]{1,0:T(8,128)(2,1)}, bf16[512,512]{1,0:T(8,128)(2,1)}, bf16[512,512]{1,0:T(8,...) async-done(((bf16[512,512]{1,0:T(8,128)(2,1)}, bf16[512,512]{1,0:T(8,128)(2,1)}, bf16[512,512]{1,0:T(8,128)(2,1)}, bf16[512,512]{1,0:T(8,128)(2,1)}, ...) | async-done | bytes 6291472 | tf_op jit(solution)/shard_map/psum | solution.py:576
  343.7 2.2 convert_element_type.36
  346.0 2.3 convert_element_type.37
  348.3 1.1 convert_element_type.38
  349.4 1.1 convert_element_type.39
  350.5 2.5 convert_element_type.40
  353.0 2.6 convert_element_type.41
  355.6 1.0 copy.31
  356.6 1.0 copy.32
  (29 shorter events, 3.3 us)
Async XLA Ops:
  7.2 36.7 %copy-start = (s32[8,1024]{1,0:T(8,128)S(1)}, s32[8,1024]{1,0:T(8,128)}, u32[]{:S(2)}) copy-start(s32[8,1024]{1,0:T(8,128)} %param.12) | copy-start | bytes 98308
  40.3 40.9 %all-to-all-start.2 = ((bf16[8,128,512]{2,1,0:T(8,128)(2,1)}), bf16[8,128,512]{2,1,0:T(8,128)(2,1)S(1)}, u32[]{:S(2)}, u32[]{:S(2)}) async-start(bf16[8,128,512]{2,1,0:T(8,128)(2,1)} %param.21), calls=%async_computation.2 | async-start | bytes 2097152 | tf_op jit(solution)/shard_map/all_to_all | solution.py:533
  81.2 6.4 %copy-start.2 = (bf16[1024,512]{1,0:T(8,128)(2,1)S(1)}, bf16[1024,512]{1,0:T(8,128)(2,1)}, u32[]{:S(2)}) copy-start(bf16[1024,512]{1,0:T(8,128)(2,1)} %get-tuple-element.39.k_ref) | copy-start | bytes 3145732
  81.3 7.5 %copy-start.1 = (bf16[8,128,512]{2,1,0:T(8,128)(2,1)}, bf16[8,128,512]{2,1,0:T(8,128)(2,1)S(1)}, u32[]{:S(2)}) copy-start(bf16[8,128,512]{2,1,0:T(8,128)(2,1)S(1)} %all-to-all-done.2) | copy-start | bytes 3145732
  81.3 82.2 %all-to-all-start.1 = ((bf16[8,128,512]{2,1,0:T(8,128)(2,1)}), bf16[8,128,512]{2,1,0:T(8,128)(2,1)S(1)}, u32[]{:S(2)}, u32[]{:S(2)}) async-start(bf16[8,128,512]{2,1,0:T(8,128)(2,1)} %bitcast.12), calls=%async_computation.1 | async-start | bytes 2097152 | tf_op jit(solution)/shard_map/all_to_all | solution.py:533
  87.4 256.3 %all-reduce.7.cloned.1.call-start = ((), (), s32[]{:S(2)}) async-start(), calls=%async_computation.4 | async-start | bytes 12582912 | tf_op jit(solution)/shard_map/psum | solution.py:576
  87.6 1.6 copy-start.3
  163.5 63.1 %all-to-all-start.3 = ((bf16[8,128,512]{2,1,0:T(8,128)(2,1)}), bf16[8,128,512]{2,1,0:T(8,128)(2,1)S(1)}, u32[]{:S(2)}, u32[]{:S(2)}) async-start(bf16[8,128,512]{2,1,0:T(8,128)(2,1)} %bitcast.7), calls=%async_computation.3 | async-start | bytes 2097152 | tf_op jit(solution)/shard_map/all_to_all | solution.py:533
  343.7 4.5 %copy-start.7 = (bf16[512,512]{1,0:T(8,128)(2,1)S(1)}, bf16[512,512]{1,0:T(8,128)(2,1)}, u32[]{:S(2)}) copy-start(bf16[512,512]{1,0:T(8,128)(2,1)} %get-tuple-element.60) | copy-start | bytes 1572868
  343.7 5.6 %copy-start.6 = (bf16[512,512]{1,0:T(8,128)(2,1)S(1)}, bf16[512,512]{1,0:T(8,128)(2,1)}, u32[]{:S(2)}) copy-start(bf16[512,512]{1,0:T(8,128)(2,1)} %get-tuple-element.61) | copy-start | bytes 1572868
  346.0 4.5 %copy-start.5 = (bf16[512,2048]{1,0:T(8,128)(2,1)S(1)}, bf16[512,2048]{1,0:T(8,128)(2,1)}, u32[]{:S(2)}) copy-start(bf16[512,2048]{1,0:T(8,128)(2,1)} %get-tuple-element.62) | copy-start | bytes 6291460
  350.5 2.5 copy-start.4
Sparse Core Ops, SparseCore 0:
  163.6 180.0 all-reduce.6

commit v2 on v1

v2 whole, which is shorter than its diff:
```python
import functools

import jax
import jax.numpy as jnp
from jax import lax
from jax.experimental import pallas as pl
from jax.experimental.pallas import tpu as pltpu
from jax.sharding import PartitionSpec as P

HEADS = 8
HEAD = 64
BAND = 30
EPSILON = 1e-06
SCALE = 0.125
CHUNK = 128
BLOCK = 256
PAIRS = HEADS // 2
NEG = -1e30
STEP_PAIRS = 2
GAIN_ROWS = 64
CALLS = ((0, 3), (3, 1))
STEPS_BEFORE = (1, 2)
GELU_A = 0.7978845608028654
GELU_B = 0.044715
F32 = jnp.float32
BF16 = jnp.bfloat16
VMEM_LIMIT = 56 * 1024 * 1024


def nn(a, b):
    return lax.dot_general(a, b, (((1,), (0,)), ((), ())), preferred_element_type=F32)


def nt(a, b):
    return lax.dot_general(a, b, (((1,), (1,)), ((), ())), preferred_element_type=F32)


def tn(a, b):
    return lax.dot_general(a, b, (((0,), (0,)), ((), ())), preferred_element_type=F32)


def low_lanes(shape):
    return lax.broadcasted_iota(jnp.int32, shape, len(shape) - 1) < HEAD


def split_heads(pair):
    low = low_lanes(pair.shape)
    zero = jnp.zeros_like(pair)
    return jnp.concatenate([jnp.where(low, pair, zero), jnp.where(low, zero, pair)], 0)


def pick(both):
    half = both.shape[0] // 2
    return jnp.where(low_lanes((half, both.shape[1])), both[:half], both[half:])


def over_lanes(column):
    half = column.shape[0] // 2
    return jnp.where(low_lanes((half, 2 * HEAD)), column[:half], column[half:])


def in_step(bodies):
    bodies = list(bodies)
    while bodies:
        bodies = [body for body in bodies if next(body, True) is None]


def features(t):
    expo = jnp.exp(jnp.minimum(t, 0.0))
    tanh = jnp.tanh(t)
    return (jnp.where(t > 0, t + 1.0, expo), 1.0 + tanh), (expo, 1.0 - tanh * tanh)


def head_mask(lanes):
    row = lax.broadcasted_iota(jnp.int32, (4 * HEAD, lanes), 0)
    lane = lax.broadcasted_iota(jnp.int32, (4 * HEAD, lanes), 1)
    head = (row // HEAD) % 2
    same = (lane < 2 * HEAD) & (lane // HEAD == head)
    return same | (lane == 2 * HEAD + row // HEAD)


def chunk_masks(seg_ref, place_ref, chunk):
    chunk = place_ref[1] + chunk

    def stretch(at):
        rows = seg_ref[:, pl.ds(pl.multiple_of(at * CHUNK, CHUNK), CHUNK)]
        mine = lax.broadcasted_iota(jnp.int32, rows.shape, 0) == place_ref[0]
        return jnp.max(jnp.where(mine, rows, -1), 0, keepdims=True).astype(F32)

    seg_own = stretch(chunk)
    seg_prev = jnp.where(chunk == 0, -1.0, stretch(jnp.maximum(chunk - 1, 0)))
    seg_q = jnp.broadcast_to(seg_own, (CHUNK, CHUNK)).T
    row = lax.broadcasted_iota(jnp.int32, (CHUNK, CHUNK), 0)
    col = lax.broadcasted_iota(jnp.int32, (CHUNK, CHUNK), 1)
    gap = row - col
    far = (seg_q == seg_own) & (gap >= 0)
    band_own = far & (gap <= BAND)
    band_prev = (seg_q == seg_prev) & (gap + CHUNK <= BAND)
    band = jnp.concatenate([band_prev, band_own], 1)
    before = seg_prev[:, CHUNK - 1 :]
    last = seg_own[:, CHUNK - 1 :]
    carry = (seg_q[:, :1] == before).astype(F32)
    tail = (seg_own == last).astype(BF16)
    keep = (before == last).astype(F32)
    return jnp.concatenate([band, band], 0), jnp.concatenate([far, far], 0), carry, tail, keep


def start_with(refs, entry_refs):
    for n, ref in enumerate(refs):
        ref[...] = entry_refs[n][...] if entry_refs else jnp.zeros_like(ref)


def forward_kernel(entries, *refs):
    (x_ref, seg_ref, place_ref, ga_ref, gf_ref, wq_ref, wk_ref, wv_ref, wo_ref, wu_ref, wd_ref,
     *refs) = refs
    entry_refs, refs = refs[:entries], refs[entries:]
    (out_ref, x1_ref, a_ref, h_ref, q_ref, k_ref, v_ref, stats_ref, states_ref, sums_ref,
     *refs) = refs
    end_refs, refs = refs[: min(entries, 2)], refs[min(entries, 2) :]
    s_ref, z_ref, kp_ref, vp_ref, wkt_ref, wvt_ref = refs
    step = pl.program_id(0)

    @pl.when(step == 0)
    def _():
        start_with((s_ref, z_ref, kp_ref, vp_ref), entry_refs)
        wkt_ref[...] = wk_ref[...].T
        wvt_ref[...] = wv_ref[...].T

    x = x_ref[...].astype(F32)
    inv = lax.rsqrt(jnp.mean(x * x, -1, keepdims=True) + EPSILON)
    hidden = (x * inv * ga_ref[...]).astype(BF16)
    h_ref[...] = hidden
    q_ref[...] = nn(hidden, wq_ref[...]).astype(BF16)
    k_ref[...] = nt(wkt_ref[...], hidden).astype(BF16)
    v_ref[...] = nt(wvt_ref[...], hidden).astype(BF16)
    same_head = head_mask(CHUNK)
    for sub in range(BLOCK // CHUNK):
        rows = slice(sub * CHUNK, (sub + 1) * CHUNK)
        chunk = step * (BLOCK // CHUNK) + sub
        band, far_mask, carry, tail, keep = chunk_masks(seg_ref, place_ref, chunk)
        tail_rows = jnp.broadcast_to(tail, (16, CHUNK))

        def body(p):
            lanes = slice(p * 128, (p + 1) * 128)
            qp = q_ref[rows, lanes]
            kt = k_ref[lanes, rows]
            vt = v_ref[lanes, rows]
            kt_ext = jnp.concatenate([kp_ref[lanes], kt], 1)
            vt_ext = jnp.concatenate([vp_ref[lanes], vt], 1)
            score = nn(split_heads(qp * SCALE), kt_ext)
            fq, _ = features(qp.astype(F32))
            fk, _ = features(kt.astype(F32))
            fk = [f.astype(BF16) for f in fk]
            fq = [f.astype(BF16) for f in fq]
            yield
            part = [
                jnp.where(far_mask, nn(split_heads(fq[m]), fk[m]), 0.0) for m in range(2)
            ]
            score = jnp.where(band, score, NEG)
            top = jnp.max(score, -1, keepdims=True)
            yield
            state = s_ref[p]
            state_low = state.astype(BF16)
            sums = z_ref[p]
            states_ref[sub, p] = state_low
            sums_ref[sub, p] = sums
            fk_both = jnp.concatenate(fk, 0)
            update = nt(fk_both * tail, vt)
            s_ref[p] = keep * state + jnp.where(same_head, update, 0.0)
            z_ref[p] = keep * sums + nt(tail_rows, fk_both)[:8]
            expo = jnp.exp(score - top)
            total = jnp.sum(expo, -1, keepdims=True)
            yield
            inv_total = 1.0 / total
            prob_prev = (expo[:, :CHUNK] * inv_total).astype(BF16)
            weight = expo[:, CHUNK:] * inv_total
            columns = [top + jnp.log(total)]
            scaled = []
            for m in range(2):
                fq_carry = fq[m].astype(F32) * carry
                entered = split_heads(fq_carry * sums[:1, m * 128 : (m + 1) * 128])
                inv_z = 1.0 / jnp.sum(part[m] + entered, -1, keepdims=True)
                columns.append(inv_z)
                weight = weight + part[m] * inv_z
                scaled.append((fq_carry * over_lanes(inv_z)).astype(BF16))
            both = jnp.concatenate([prob_prev, weight.astype(BF16)], 1)
            yield
            attended = pick(nt(both, vt_ext)) + nn(jnp.concatenate(scaled, 1), state_low)
            a_ref[rows, lanes] = attended.astype(BF16)
            for n, column in enumerate(columns):
                stats_ref[sub, p, n] = jnp.broadcast_to(column, (2 * CHUNK, CHUNK))

        for first in range(0, PAIRS, STEP_PAIRS):
            in_step(body(p) for p in range(first, first + STEP_PAIRS))
        kp_ref[...] = k_ref[:, rows]
        vp_ref[...] = v_ref[:, rows]
    for end_ref, ref in zip(end_refs, (s_ref, z_ref)):
        end_ref[...] = ref[...]
    x1 = x + nn(a_ref[...], wo_ref[...])
    x1_ref[...] = x1
    inv = lax.rsqrt(jnp.mean(x1 * x1, -1, keepdims=True) + EPSILON)
    hidden = (x1 * inv * gf_ref[...]).astype(BF16)
    total = x1
    width = 512
    for f in range(wu_ref.shape[1] // width):
        cols = slice(f * width, (f + 1) * width)
        up = nn(hidden, wu_ref[:, cols])
        act = 0.5 * up * (1.0 + jnp.tanh(GELU_A * (up + GELU_B * up * up * up)))
        total = total + nn(act.astype(BF16), wd_ref[cols])
    out_ref[...] = total.astype(BF16)


def norm_backward(x, gain, grad):
    inv = lax.rsqrt(jnp.mean(x * x, -1, keepdims=True) + EPSILON)
    unit = x * inv
    scaled = grad * gain
    d_gain = jnp.sum(grad * unit, 0, keepdims=True)
    return inv * (scaled - unit * jnp.mean(unit * scaled, -1, keepdims=True)), d_gain


def ffn_backward_kernel(first, last, *refs):
    dy_ref, x1_ref, gf_ref, wu_ref, wd_ref, core_ref, *refs = refs
    if not first:
        dh_in_ref, *refs = refs
    if last:
        a_ref, wo_ref, dx1_ref, da_ref, dg_ref, *refs = refs
    else:
        dh_out_ref, *refs = refs
    keep_ref, send_ref, dwd_acc, dwu_acc, *refs = refs
    if last:
        dwo_acc, dg_acc = refs
    step = pl.program_id(0)

    @pl.when(step == 0)
    def _():
        dwd_acc[...] = jnp.zeros_like(dwd_acc)
        dwu_acc[...] = jnp.zeros_like(dwu_acc)
        if last:
            dwo_acc[...] = jnp.zeros_like(dwo_acc)
            dg_acc[...] = jnp.zeros_like(dg_acc)

    dy = dy_ref[...]
    x1 = x1_ref[...]
    gain = gf_ref[...]
    inv = lax.rsqrt(jnp.mean(x1 * x1, -1, keepdims=True) + EPSILON)
    hidden = (x1 * inv * gain).astype(BF16)
    d_hidden = jnp.zeros(x1.shape, F32) if first else dh_in_ref[...]
    width = x1.shape[1]
    for f in range(wu_ref.shape[1] // width):
        cols = slice(f * width, (f + 1) * width)
        up = nn(hidden, wu_ref[:, cols])
        square = up * up
        tanh = jnp.tanh(GELU_A * up * (1.0 + GELU_B * square))
        half = 0.5 * (1.0 + tanh)
        act = (up * half).astype(BF16)
        slope = half + 0.5 * up * (1.0 - tanh * tanh) * (
            GELU_A + (3.0 * GELU_A * GELU_B) * square
        )
        d_up = (slope * nt(dy, wd_ref[cols])).astype(BF16)
        dwd_acc[cols] += tn(act, dy)
        dwu_acc[cols] += tn(hidden, d_up)
        d_hidden = d_hidden + nt(d_up, wu_ref[:, cols])
    if last:
        d_norm, d_gain = norm_backward(x1, gain, d_hidden)
        dx1 = dy.astype(F32) + d_norm
        dg_acc[...] += jnp.broadcast_to(d_gain, dg_acc.shape)
        dx1_ref[...] = dx1
        d_branch = dx1.astype(BF16)
        dwo_acc[...] += tn(a_ref[...], d_branch)
        da_ref[...] = nt(d_branch, wo_ref[...]).astype(BF16)
    else:
        dh_out_ref[...] = d_hidden

    @pl.when(step == pl.num_programs(0) - 1)
    def _():
        sums = (dwd_acc, dwu_acc) + ((dwo_acc,) if last else ())
        put_halves(sums, core_ref[0], keep_ref, send_ref)
        if last:
            dg_ref[...] = dg_acc[...]


def put_halves(sums, core, keep_ref, send_ref):
    at = 0
    for total in sums:
        half = total.shape[0] // 2
        for ref, which in ((keep_ref, core), (send_ref, 1 - core)):
            rows = total[pl.ds(pl.multiple_of(which * half, half), half)]
            ref[at : at + half] = rows.astype(BF16)
        at += half
    return at


def attention_backward_kernel(last, earlier, entries, *refs):
    (da_ref, q_ref, k_ref, v_ref, kprev_ref, vprev_ref, stats_ref, states_ref, sums_ref,
     seg_ref, h_ref, place_ref, *refs) = refs
    entry_refs, refs = refs[:entries], refs[entries:]
    if last:
        x_ref, dx1_ref, ga_ref, dgf_ref, wq_ref, wk_ref, wv_ref, *refs = refs
        earlier_refs, refs = refs[: 3 * earlier], refs[3 * earlier :]
        dx_ref, *refs = refs
    dq_ref, dk_ref, dv_ref, keep_ref, send_ref, *refs = refs
    end_refs, refs = refs[: min(entries, 3)], refs[min(entries, 3) :]
    r_ref, dkc_ref, dvc_ref, dwq_acc, dwk_acc, dwv_acc, *refs = refs
    if last:
        dg_acc, wkt_ref, wvt_ref = refs
    step = pl.program_id(0)
    block = pl.num_programs(0) - 1 - step

    @pl.when(step == 0)
    def _():
        start_with((r_ref, dkc_ref, dvc_ref), entry_refs)
        dwq_acc[...] = jnp.zeros_like(dwq_acc)
        dwk_acc[...] = jnp.zeros_like(dwk_acc)
        dwv_acc[...] = jnp.zeros_like(dwv_acc)
        if last:
            dg_acc[...] = jnp.zeros_like(dg_acc)
            wkt_ref[...] = wk_ref[...].T
            wvt_ref[...] = wv_ref[...].T

    lane = lax.broadcasted_iota(jnp.int32, (CHUNK, CHUNK), 1)
    same_head = head_mask(2 * CHUNK)
    for sub in reversed(range(BLOCK // CHUNK)):
        rows = slice(sub * CHUNK, (sub + 1) * CHUNK)
        chunk = block * (BLOCK // CHUNK) + sub
        band, far_mask, carry, tail, keep = chunk_masks(seg_ref, place_ref, chunk)
        tail_rows = jnp.broadcast_to(tail, (CHUNK, CHUNK))

        def body(p):
            lanes = slice(p * 128, (p + 1) * 128)
            qp = q_ref[rows, lanes]
            da = da_ref[rows, lanes]
            kt = k_ref[lanes, rows]
            vt = v_ref[lanes, rows]
            if sub == 0:
                kt_prev, vt_prev = kprev_ref[lanes], vprev_ref[lanes]
                if entry_refs:
                    kt_prev = jnp.where(block == 0, entry_refs[3][lanes], kt_prev)
                    vt_prev = jnp.where(block == 0, entry_refs[4][lanes], vt_prev)
            else:
                before = slice((sub - 1) * CHUNK, sub * CHUNK)
                kt_prev, vt_prev = k_ref[lanes, before], v_ref[lanes, before]
            kt_ext = jnp.concatenate([kt_prev, kt], 1)
            vt_ext = jnp.concatenate([vt_prev, vt], 1)
            q2 = split_heads(qp * SCALE)
            da2 = split_heads(da)
            score = nn(q2, kt_ext)
            d_prob = nn(da2, vt_ext)
            yield
            state = states_ref[sub, p]
            sums = sums_ref[sub, p]
            back = r_ref[p]
            back_low = back.astype(BF16)
            from_state = nt(da, state) * carry
            to_later = nn(back_low, jnp.concatenate([vt * tail, tail_rows], 0))
            fq, slope_q = features(qp.astype(F32))
            fk, slope_k = features(kt.astype(F32))
            fk = [f.astype(BF16) for f in fk]
            fq = [f.astype(BF16) for f in fq]
            fq2 = [split_heads(f) for f in fq]
            yield
            part = [jnp.where(far_mask, nn(fq2[m], fk[m]), 0.0) for m in range(2)]
            lse = stats_ref[sub, p, 0]
            prob = jnp.exp(jnp.where(band, score - jnp.concatenate([lse, lse], 1), NEG))
            delta = jnp.sum(prob * d_prob, -1, keepdims=True)
            d_score = (prob * (d_prob - delta)).astype(BF16)
            yield
            dq = SCALE * pick(nt(d_score, kt_ext))
            dk_ext = tn(q2, d_score)
            dk = dk_ext[:, CHUNK:] + dkc_ref[lanes]
            dkc_ref[lanes] = dk_ext[:, :CHUNK]
            d_own = d_prob[:, CHUNK:]
            weight = prob[:, CHUNK:]
            yield
            scaled = []
            d_part = []
            entries = []
            right = jnp.zeros((CHUNK, CHUNK), F32)
            for m in range(2):
                part_lanes = slice(m * 128, (m + 1) * 128)
                fq_wide = fq[m].astype(F32)
                inv_z = stats_ref[sub, p, m + 1]
                weighted = part[m] * inv_z
                weight = weight + weighted
                entered = from_state[:, part_lanes]
                inv_wide = pick(inv_z)
                taken = fq_wide * inv_wide
                dot = jnp.sum(
                    weighted * d_own + split_heads(taken * entered), -1, keepdims=True
                )
                d_part.append(jnp.where(far_mask, (d_own - dot) * inv_z, 0.0).astype(BF16))
                entries.append(
                    inv_wide * (entered - over_lanes(dot) * (carry * sums[:1, part_lanes]))
                )
                scaled.append((taken * carry).astype(BF16))
                right = jnp.where(lane == 2 * m, -dot[:CHUNK], right)
                right = jnp.where(lane == 2 * m + 1, -dot[CHUNK:], right)
            both = jnp.concatenate([prob[:, :CHUNK].astype(BF16), weight.astype(BF16)], 1)
            yield
            dv_ext = tn(da2, both)
            dv = dv_ext[:, CHUNK:] + dvc_ref[lanes]
            dv = dv + tn(back_low[:, :CHUNK], jnp.concatenate(fk, 0) * tail)
            dvc_ref[lanes] = dv_ext[:, :CHUNK]
            update = tn(
                jnp.concatenate(scaled, 1), jnp.concatenate([da, right.astype(BF16)], 1)
            )
            r_ref[p] = keep * back + jnp.where(same_head, update, 0.0)
            dv_ref[lanes, rows] = dv.astype(BF16)
            yield
            for m in range(2):
                dq = dq + slope_q[m] * (pick(nt(d_part[m], fk[m])) + entries[m])
                dk = dk + slope_k[m] * (
                    tn(fq2[m], d_part[m]) + to_later[m * 128 : (m + 1) * 128]
                )
            dq_ref[rows, lanes] = dq.astype(BF16)
            dk_ref[lanes, rows] = dk.astype(BF16)

        in_step(body(p) for p in range(r_ref.shape[0]))
    for end_ref, ref in zip(end_refs, (r_ref, dkc_ref, dvc_ref)):
        end_ref[...] = ref[...]
    dim = h_ref.shape[1]
    hidden_t = h_ref[...].T
    dwq_acc[...] += nn(hidden_t, dq_ref[...])
    dwk_acc[...] += nt(hidden_t, dk_ref[...])
    dwv_acc[...] += nt(hidden_t, dv_ref[...])
    if last:
        mine = (dq_ref, dk_ref, dv_ref)
        dq, dk, dv = (
            jnp.concatenate([ref[...] for ref in earlier_refs[n::3] + [mine[n]]], min(n, 1) ^ 1)
            for n in range(3)
        )
        d_hidden = nt(dq, wq_ref[...]) + tn(dk, wkt_ref[...]) + tn(dv, wvt_ref[...])
        d_norm, d_gain = norm_backward(x_ref[...].astype(F32), ga_ref[...], d_hidden)
        dg_acc[...] += jnp.broadcast_to(d_gain, dg_acc.shape)
        dx_ref[...] = (dx1_ref[...] + d_norm).astype(BF16)

    @pl.when(step == pl.num_programs(0) - 1)
    def _():
        core = place_ref[2]
        at = put_halves((dwq_acc, dwk_acc, dwv_acc), core, keep_ref, send_ref)
        keep_ref[at:] = jnp.zeros((GAIN_ROWS, keep_ref.shape[1]), BF16)
        send_ref[at:] = jnp.zeros((GAIN_ROWS, keep_ref.shape[1]), BF16)
        if last:
            width = keep_ref.shape[1]
            gains = [
                ref[:1, n : n + width] for ref in (dg_acc, dgf_ref) for n in range(0, dim, width)
            ]
            gains += [jnp.zeros((16 - len(gains), width), F32)]
            gains = jnp.concatenate(gains, 0)
            keep_ref[at : at + 16] = jnp.where(core == 0, gains, 0.0).astype(BF16)
            send_ref[at : at + 16] = jnp.where(core == 0, 0.0, gains).astype(BF16)


def whole(shape):
    return pl.BlockSpec(shape, lambda i: (0,) * len(shape))


def tokens_of(width, index=lambda i: i):
    return pl.BlockSpec((BLOCK, width), lambda i: (index(i), 0))


def params():
    return pltpu.CompilerParams(
        vmem_limit_bytes=VMEM_LIMIT, dimension_semantics=("arbitrary",)
    )


def sds(shape, dtype):
    return jax.ShapeDtypeStruct(shape, dtype)


def run_forward(x, segments, place, gain_attn, gain_ffn, wq, wk, wv, wo, wu, wd, entry):
    length, dim = x.shape
    ff = wu.shape[1]
    chunks = length // CHUNK
    per = BLOCK // CHUNK
    row = tokens_of(dim)
    column = pl.BlockSpec((dim, BLOCK), lambda i: (0, i))
    state_shape = (PAIRS, 4 * HEAD, 2 * HEAD)
    sum_shape = (PAIRS, 8, 4 * HEAD)
    stat_shape = (PAIRS, 3, 2 * CHUNK, CHUNK)
    ends = [(state_shape, F32), (sum_shape, F32)][: len(entry)]
    return pl.pallas_call(
        functools.partial(forward_kernel, len(entry)),
        grid=(length // BLOCK,),
        in_specs=[
            row, whole(segments.shape), SMEM, whole((1, dim)), whole((1, dim)),
            whole((dim, dim)), whole((dim, dim)), whole((dim, dim)), whole((dim, dim)),
            whole((dim, ff)), whole((ff, dim)),
        ] + [whole(array.shape) for array in entry],
        out_specs=[
            row, row, row, row, row, column, column,
            pl.BlockSpec((per,) + stat_shape, lambda i: (i, 0, 0, 0, 0)),
            pl.BlockSpec((per,) + state_shape, lambda i: (i, 0, 0, 0)),
            pl.BlockSpec((per,) + sum_shape, lambda i: (i, 0, 0, 0)),
        ] + [whole(shape) for shape, _ in ends],
        out_shape=[
            sds((length, dim), BF16), sds((length, dim), F32), sds((length, dim), BF16),
            sds((length, dim), BF16), sds((length, dim), BF16),
            sds((dim, length), BF16), sds((dim, length), BF16),
            sds((chunks,) + stat_shape, F32),
            sds((chunks,) + state_shape, BF16), sds((chunks,) + sum_shape, F32),
        ] + [sds(*end) for end in ends],
        scratch_shapes=[
            pltpu.VMEM(state_shape, F32), pltpu.VMEM(sum_shape, F32),
            pltpu.VMEM((dim, CHUNK), BF16), pltpu.VMEM((dim, CHUNK), BF16),
            pltpu.VMEM((dim, dim), BF16), pltpu.VMEM((dim, dim), BF16),
        ],
        compiler_params=params(),
        name="layer_forward",
    )(x, segments, place, gain_attn, gain_ffn, wq, wk, wv, wo, wu, wd, *entry)


SMEM = pl.BlockSpec(memory_space=pltpu.SMEM)
ANY = pl.BlockSpec(memory_space=pl.ANY)


def run_ffn_backward(part, part_count, dy, x1, gain_ffn, wu, wd, core, d_hidden, a, wo):
    first, last = part == 0, part == part_count - 1
    length, dim = dy.shape
    ff = wu.shape[1] // part_count
    half = ff + (dim // 2 if last else 0)
    row = tokens_of(dim)
    more_in, more_args, outs, shapes, scratch = [], [], [], [], []
    if not first:
        more_in, more_args = [row], [d_hidden]
    if last:
        more_in += [row, whole((dim, dim))]
        more_args += [a, wo]
        outs = [row, row, whole((8, dim))]
        shapes = [sds((length, dim), F32), sds((length, dim), BF16), sds((8, dim), F32)]
        scratch = [pltpu.VMEM((dim, dim), F32), pltpu.VMEM((8, dim), F32)]
    else:
        outs, shapes = [row], [sds((length, dim), F32)]
    return pl.pallas_call(
        functools.partial(ffn_backward_kernel, first, last),
        grid=(length // BLOCK,),
        in_specs=[
            row, row, whole((1, dim)),
            pl.BlockSpec((dim, ff), lambda i: (0, part)),
            pl.BlockSpec((ff, dim), lambda i: (part, 0)),
            SMEM,
        ] + more_in,
        out_specs=outs + [whole((half, dim))] * 2,
        out_shape=shapes + [sds((half, dim), BF16)] * 2,
        scratch_shapes=[pltpu.VMEM((ff, dim), F32), pltpu.VMEM((ff, dim), F32)] + scratch,
        compiler_params=params(),
        name="ffn_backward",
    )(dy, x1, gain_ffn, wu, wd, core, *more_args)


def run_attention_backward(
    first, pairs, after, through, x, dx1, da, h, q, k, v, stats, states, sums, segments, place,
    gain_attn, dgf, wq, wk, wv, earlier, entry,
):
    last = first + pairs == PAIRS
    length, dim = x.shape
    width = 2 * HEAD * pairs
    call = first // pairs
    half = 3 * dim // 2 + GAIN_ROWS
    steps = length // BLOCK
    per = BLOCK // CHUNK
    back = lambda i: steps - 1 - i
    row = tokens_of(dim, back)
    part_row = pl.BlockSpec((BLOCK, width), lambda i: (back(i), call))
    part_column = pl.BlockSpec((width, BLOCK), lambda i: (call, back(i)))
    prev = pl.BlockSpec((width, CHUNK), lambda i: (call, jnp.maximum(back(i) * per - 1, 0)))
    rim_in = pl.BlockSpec((width, CHUNK), lambda i: (call, 0))
    rim = whole((width, CHUNK))
    r_shape = (pairs, 4 * HEAD, 4 * HEAD)
    rim_shape = (width, CHUNK)

    def of_pairs(array):
        shape = array.shape[2:]
        return pl.BlockSpec((per, pairs) + shape, lambda i: (back(i), call) + (0,) * len(shape))

    entry_in = [whole(r_shape), rim, rim, rim_in, rim_in][: len(entry)]
    ends = [r_shape, rim_shape, rim_shape][: len(entry)]
    more_in, more_args, outs, shapes, scratch = [], [], [], [], []
    if last:
        square = whole((dim, dim))
        more_in = [row, row, whole((1, dim)), whole(dgf.shape), square, square, square]
        more_args = [x, dx1, gain_attn, dgf, wq, wk, wv]
        for group in earlier:
            size = group[0].shape[1]
            column = pl.BlockSpec((size, BLOCK), lambda i: (0, back(i)))
            more_in += [tokens_of(size, back), column, column]
            more_args += group
        outs = [row]
        shapes = [sds((length, dim), BF16)]
        scratch = [
            pltpu.VMEM((8, dim), F32), pltpu.VMEM((dim, dim), BF16), pltpu.VMEM((dim, dim), BF16),
        ]
    kernel = functools.partial(attention_backward_kernel, last, len(earlier), len(entry))
    skip = len(after) + len(through)
    args = [
        da, q, k, v, k, v, stats, states, sums, segments, h, place, *entry, *more_args,
    ]
    inputs = skip + len(args)

    def body(*refs):
        kernel(*refs[skip:inputs], *refs[inputs + len(through) :])

    return pl.pallas_call(
        body,
        grid=(steps,),
        input_output_aliases={len(after) + n: n for n in range(len(through))},
        in_specs=[ANY] * skip + [
            part_row, part_row, part_column, part_column, prev, prev,
            of_pairs(stats), of_pairs(states), of_pairs(sums), whole(segments.shape), row, SMEM,
        ] + entry_in + more_in,
        out_specs=[ANY] * len(through) + outs + [
            tokens_of(width, back),
            pl.BlockSpec((width, BLOCK), lambda i: (0, back(i))),
            pl.BlockSpec((width, BLOCK), lambda i: (0, back(i))),
            whole((half, width)), whole((half, width)),
        ] + [whole(shape) for shape in ends],
        out_shape=[sds(array.shape, array.dtype) for array in through] + shapes + [
            sds((length, width), BF16), sds((width, length), BF16), sds((width, length), BF16),
            sds((half, width), BF16), sds((half, width), BF16),
        ] + [sds(shape, F32) for shape in ends],
        scratch_shapes=[
            pltpu.VMEM(r_shape, F32), pltpu.VMEM(rim_shape, F32), pltpu.VMEM(rim_shape, F32),
            pltpu.VMEM((dim, width), F32), pltpu.VMEM((dim, width), F32),
            pltpu.VMEM((dim, width), F32),
        ] + scratch,
        compiler_params=params(),
        name="attention_backward",
    )(*after, *through, *args)


def finish_kernel(skip, across, core_ref, own_ref, other_ref, *refs):
    out_refs = refs[skip:]
    at = 0
    width = own_ref.shape[1]
    for wide, out_ref in zip(across, out_refs):
        half = out_ref.shape[0] * out_ref.shape[1] // width // 2
        for ref, which in ((own_ref, core_ref[0]), (other_ref, 1 - core_ref[0])):
            if wide:
                rows = out_ref.shape[0]
                for c in range(half // rows):
                    start = pl.multiple_of((which * (half // rows) + c) * width, width)
                    block = ref[at + c * rows : at + (c + 1) * rows]
                    out_ref[:, pl.ds(start, width)] = block.astype(F32)
            else:
                rows = pl.ds(pl.multiple_of(which * half, half), half)
                out_ref[rows] = ref[at : at + half].astype(F32)
        at += half


def run_finish(core_ref, own, other, across, shapes, after):
    full = pl.BlockSpec(memory_space=pltpu.VMEM)
    return pl.pallas_call(
        functools.partial(finish_kernel, len(after), across),
        in_specs=[SMEM, full, full] + [ANY] * len(after),
        out_specs=[full] * len(shapes),
        out_shape=[sds(shape, F32) for shape in shapes],
        compiler_params=pltpu.CompilerParams(vmem_limit_bytes=VMEM_LIMIT),
        name="finish",
    )(core_ref, own, other, *after)


def partner(array, seq_bits, row_bits):
    seq_count, row_groups = lax.axis_size("seq"), lax.axis_size("rows")
    pairs = [
        (s * row_groups + r, (s ^ seq_bits) * row_groups + (r ^ row_bits))
        for s in range(seq_count)
        for r in range(row_groups)
    ]
    return lax.ppermute(array, ("seq", "rows"), pairs)


def add(*parts):
    parts = [part.astype(F32) for part in parts]
    if len(parts) == 4:
        return ((parts[0] + parts[1]) + (parts[2] + parts[3])).astype(BF16)
    return (parts[0] + parts[1]).astype(BF16)


def take(array, index, size):
    return lax.dynamic_slice_in_dim(array, index * size, size, 0)


PLANE_BITS = ((1, 0), (0, 2), (1, 2))
DEPTH_BITS = ((2, 0), (4, 0), (6, 0))


def cut(total, place):
    size = total.shape[0] // 4
    return [take(total, place ^ d, size) for d in range(4)]


def traded(parts, all_bits):
    return [parts[0]] + [partner(part, *bits) for part, bits in zip(parts[1:], all_bits)]


def joined(parts, place):
    blocks = jnp.stack(parts)
    blocks = [lax.dynamic_index_in_dim(blocks, place ^ d, 0, False) for d in range(4)]
    return jnp.concatenate(blocks, 0)


def all_reduce(places, halves):
    core, plane, depth = places
    others = [partner(send, 0, 1) for _, send in halves]
    keeps = yield [keep for keep, _ in halves]
    sums = [add(keep, other) for keep, other in zip(keeps, others)]
    parts = yield cut(jnp.concatenate(sums, 1) if len(sums) > 1 else sums[0], plane)
    parts = traded(parts, PLANE_BITS)
    parts = yield parts
    parts = yield cut(add(*parts), depth)
    parts = traded(parts, DEPTH_BITS)
    parts = yield parts
    total = add(*parts)
    for bits in further_bits():
        total = add(total, partner(total, *bits))
    (total,) = yield [total]
    parts = traded([total] * 4, DEPTH_BITS)
    parts = yield parts
    (block,) = yield [joined(parts, depth)]
    parts = traded([block] * 4, PLANE_BITS)
    parts = yield parts
    (own,) = yield [joined(parts, plane)]
    yield [own, partner(own, 0, 1)]


class Reduction:
    def __init__(self, *args):
        self.steps = all_reduce(*args)
        self.arrays = next(self.steps)

    def step(self):
        self.arrays = self.steps.send(self.arrays)

    def finish(self):
        for arrays in iter(lambda: self.steps.send(self.arrays), None):
            self.arrays = arrays
            if len(arrays) == 2:
                return arrays


def further_bits():
    bits = []
    bit = 8
    while bit < lax.axis_size("seq"):
        bits.append((bit, 0))
        bit *= 2
    bit = 4
    while bit < lax.axis_size("rows"):
        bits.append((0, bit))
        bit *= 2
    return bits


def all_reduce_small(small):
    small = small + partner(small, 0, 1)
    for bits in (((1, 0), (0, 2), (1, 2)), ((2, 0), (4, 0), (6, 0))):
        got = [small] + [partner(small, *b) for b in bits]
        small = (got[0] + got[1]) + (got[2] + got[3])
    for b in further_bits():
        small = small + partner(small, *b)
    return small


def local(
    tokens, segments, gain_attn, gain_ffn, w_query, w_key, w_value, w_out, w_up, w_down, cotangent
):
    row_count, shard_len, dim = tokens.shape
    seq_count = lax.axis_size("seq")
    parts = seq_count // row_count
    groups = [[g * row_count + r for r in range(row_count)] for g in range(parts)]
    length = row_count * shard_len
    index = lax.axis_index("seq")
    my_row = index % row_count
    my_part = index // row_count

    def trade(array):
        return lax.all_to_all(
            array.reshape(row_count, shard_len, dim), "seq", 0, 0, axis_index_groups=groups
        )

    def shifted(arrays, by):
        pairs = [
            (i, i + by * row_count)
            for i in range(seq_count)
            if 0 <= i + by * row_count < seq_count
        ]
        return lax.ppermute(arrays, "seq", pairs)

    ga, gf = gain_attn.reshape(1, dim), gain_ffn.reshape(1, dim)
    seq_index, row_index = lax.axis_index("seq"), lax.axis_index("rows")
    core, plane = row_index % 2, seq_index % 2 + 2 * (row_index // 2 % 2)
    places = core, plane, seq_index // 2 % 4
    place = jnp.stack([my_row, my_part * (length // CHUNK), core]).astype(jnp.int32)

    x = trade(tokens).reshape(length, dim)
    dy = trade(cotangent).reshape(length, dim)
    entry = ()
    if parts > 1:
        rim_zero = jnp.zeros((dim, CHUNK), BF16)
        entry = (
            jnp.zeros((PAIRS, 4 * HEAD, 2 * HEAD), F32), jnp.zeros((PAIRS, 8, 4 * HEAD), F32),
            rim_zero, rim_zero,
        )
    for turn in range(parts):
        out, x1, a, h, q, k, v, stats, states, sums, *ends = run_forward(
            x, segments, place, ga, gf, w_query, w_key, w_value, w_out, w_up, w_down, entry
        )
        if turn < parts - 1:
            entry = shifted((*ends, k[:, length - CHUNK :], v[:, length - CHUNK :]), 1)
    output = trade(out)
    core_ref = place[2:]
    dx1, da, dgf, keep, send = run_ffn_backward(
        0, 1, dy, x1, gf, w_up, w_down, core_ref, None, a, w_out
    )
    ffn = Reduction(places, [(keep, send)])
    backs = [()] * len(CALLS)
    if parts > 1:
        backs = [
            (
                jnp.zeros((pairs, 4 * HEAD, 4 * HEAD), F32),
                jnp.zeros((pairs * 2 * HEAD, CHUNK), F32),
                jnp.zeros((pairs * 2 * HEAD, CHUNK), F32),
            )
            for _, pairs in CALLS
        ]
    for turn in range(parts):
        earlier, halves = [], []
        for n, (first, pairs) in enumerate(CALLS):
            after, through = [], []
            if turn == parts - 1:
                for _ in range(STEPS_BEFORE[n]):
                    ffn.step()
                through, after = ffn.arrays[:1], ffn.arrays[1:]
                if first + pairs == PAIRS:
                    after.append(output)
            outs = run_attention_backward(
                first, pairs, after, through, x, dx1, da, h, q, k, v, stats, states, sums,
                segments, place, ga, dgf, w_query, w_key, w_value, earlier,
                backs[n] + entry[2:] if parts > 1 else (),
            )
            if through:
                ffn.arrays[0], *outs = outs
            if first + pairs == PAIRS:
                dx, *outs = outs
            dq, dk, dv, keep, send, *ends = outs
            earlier.append((dq, dk, dv))
            halves.append((keep, send))
            if turn < parts - 1:
                backs[n] = shifted(tuple(ends), -1)
    d_tokens = trade(dx)
    attention = Reduction(places, halves)
    ff = w_up.shape[1]
    own, other = ffn.finish()
    dwd, dwu, dwo = run_finish(
        core_ref, own, other, (False, True, False), ((ff, dim), (dim, ff), (dim, dim)), []
    )
    own, other = attention.finish()
    dwq, dwk, dwv = run_finish(
        core_ref, own, other, (False,) * 3, ((dim, dim),) * 3, [dwd, dwu, dwo]
    )
    at = 3 * dim // 2
    gains = jnp.where(core == 0, own[at : at + 16], other[at : at + 16])
    gains = gains[:, dim - 2 * HEAD * CALLS[-1][1] :].astype(F32).reshape(-1)
    return output, d_tokens, gains[:dim], gains[dim : 2 * dim], dwq, dwk, dwv, dwo, dwu, dwd


def solution(mesh):
    act = P("rows", "seq", None)
    return jax.shard_map(
        local,
        mesh=mesh,
        in_specs=(act, P("rows", None)) + (P(),) * 8 + (act,),
        out_specs=(act, act) + (P(),) * 8,
        check_vma=False,
    )
```

time: 365 us -> 274 us (0.75)
  blocking collectives: 87.8 us -> 33.1 us
  waiting for transfers between devices: 117 us -> 76.7 us
  starting transfers between devices: 15.7 us -> 46.1 us
  between operations: 14.2 us -> 1.2 us
  Pallas kernels: 106 us -> 93.5 us
    psum x1 -> x0, waiting for transfers between devices: 117 us -> none  [local(): lax.psum((dwq, dwk, dwv, dga[0].astype(BF16), dgf[0].astype(BF16)), axes)]
    ppermute x0 -> x29, waiting for transfers between devices: none -> 69.2 us  [partner(): return lax.ppermute(array, ('seq', 'rows'), pairs)]
    psum x1 -> x0, blocking collectives: 54.7 us -> none  [local(): lax.psum((dwq, dwk, dwv, dga[0].astype(BF16), dgf[0].astype(BF16)), axes)]
    ppermute x0 -> x29, starting transfers between devices: none -> 32.1 us  [partner(): return lax.ppermute(array, ('seq', 'rows'), pairs)]
    pallas_call x3 -> x6, Pallas kernels: 106 us -> 93.5 us  [the longest x2 34.1 us: run_attention_backward(): pl.pallas_call(body, grid=(steps,), input_output_aliases={len(after) + n:...]
    all_to_all x3, waiting for transfers between devices: 0.01 us -> 7.49 us  [trade(): lax.all_to_all(array.reshape(row_count, shard_len, dim), 'seq', 0, 0, axi...]
    convert_element_type x8, other arithmetic: 13 us -> 6.74 us  [the longest x4 4.18 us: add(): return (parts[0] + parts[1] + (parts[2] + parts[3])).astype(BF16)]
    another operation x0 -> x7, other arithmetic: none -> 3.99 us  [the longest x6 3.43 us: joined(): blocks = jnp.stack(parts)]
  transfers between devices with their start and end apart: 4 -> 32, of which waited for: 1 -> 11; matrix products, arithmetic and copies ran while one was open for 2% -> 6% of each run, Pallas kernels for 29% -> 22%
where the time goes in v2:
time: 274 us
  Pallas kernels  93.5 us (34%)
  waiting for transfers between devices  76.7 us (28%)
  starting transfers between devices  46.1 us (17%)
  blocking collectives  33.1 us (12%)
  other arithmetic  13.3 us (5%)
  local copies, waits for them, and re-layouts  9.71 us (4%)
    ppermute x29, waiting for transfers between devices, partner(): return lax.ppermute(array, ('seq', 'rows'), pairs)  69.2 us
    pallas_call x2, Pallas kernels, run_attention_backward(): pl.pallas_call(body, grid=(steps,), input_output_aliases={len(after) + n:...  34.1 us
    all_to_all x1, blocking collectives, trade(): lax.all_to_all(array.reshape(row_count, shard_len, dim), 'seq', 0, 0, axi...  33.1 us
    ppermute x29, starting transfers between devices, partner(): return lax.ppermute(array, ('seq', 'rows'), pairs)  32.1 us
    pallas_call x1, Pallas kernels, run_forward(): pl.pallas_call(functools.partial(forward_kernel, len(entry)), grid=(lengt...  26.4 us
    pallas_call x1, Pallas kernels, run_ffn_backward(): pl.pallas_call(functools.partial(ffn_backward_kernel, first, last), grid=...  23.3 us
    all_to_all x3, starting transfers between devices, trade(): lax.all_to_all(array.reshape(row_count, shard_len, dim), 'seq', 0, 0, axi...  14.1 us
    pallas_call x2, Pallas kernels, run_finish(): pl.pallas_call(functools.partial(finish_kernel, len(after), across), in_s...  9.73 us
  transfers between devices with their start and end apart: 32, of which 11 were waited for; matrix products, arithmetic and copies ran while one was open for 6% of the time, Pallas kernels for 22%

profile of v2, /device:TPU:0, one launch (start us, length us, event | category | flops | bytes accessed | tf_op | source)
XLA Modules:
  0.0 273.7 jit_solution(3268354732486652294)
XLA Ops:
  0.6 33.1 %all_to_all.20 = bf16[8,128,512]{2,1,0:T(8,128)(2,1)} all-to-all(bf16[8,128,512]{2,1,0:T(8,128)(2,1)} %param.11), channel_id=1, replica_groups={{0,4,8,12,16,20,24,28},{1,5,9,13,17,21,25,29},{2,6,10,14,18,22,26,30},{..., dimensions={0} | all-to-all | bytes 2097152 | tf_op jit(solution)/shard_map/all_to_all | solution.py:777
  33.8 3.6 %all-to-all-start.2 = ((bf16[8,128,512]{2,1,0:T(8,128)(2,1)}), bf16[8,128,512]{2,1,0:T(8,128)(2,1)S(1)}, u32[]{:S(2)}, u32[]{:S(2)}) async-start(bf16[8,128,512]{2,1,0:T(8,128)(2,1)} %param.21), calls=%async_computation.2 | async-start | bytes 2097152 | tf_op jit(solution)/shard_map/all_to_all | solution.py:777
  37.9 26.4 %layer_forward.1 = (bf16[1024,512]{1,0:T(8,128)(2,1)}, f32[1024,512]{1,0:T(8,128)}, bf16[1024,512]{1,0:T(8,128)(2,1)}, bf16[1024,512]{1,0:T(8,128)(2,1)}, bf16[1...) custom-call(bf16[1024,512]{1,0:T(8,128)(2,1)} %bitcast.65, ...), custom_call_target="tpu_custom_call" | custom-call | tf_op jit(solution)/shard_map/layer_forward/pallas_call | solution.py:482
  65.4 23.3 %ffn_backward.1 = (f32[1024,512]{1,0:T(8,128)}, bf16[1024,512]{1,0:T(8,128)(2,1)}, f32[8,512]{1,0:T(8,128)}, bf16[2304,512]{1,0:T(8,128)(2,1)}, bf16[2304,512]{1,0:T(8,128)(2,1)}) custom-call(bf16[1024,512]{1,0:T(8,128)(2,1)} %bitcast.67, f32[1024,512]{1,0:T(8,128)} %get-tuple-element.42.refs_1_, f32[1,512]{1,0:T(1,128)} %bitcast.82, ...), custom_call_target="tpu_custom_call" | custom-call | tf_op jit(solution)/shard_map/ffn_backward/pallas_call | solution.py:534
  88.8 6.0 %all-to-all-start.1 = ((bf16[8,128,512]{2,1,0:T(8,128)(2,1)}), bf16[8,128,512]{2,1,0:T(8,128)(2,1)S(1)}, u32[]{:S(2)}, u32[]{:S(2)}) async-start(bf16[8,128,512]{2,1,0:T(8,128)(2,1)} %bitcast.69), calls=%async_computation.1 | async-start | bytes 2097152 | tf_op jit(solution)/shard_map/all_to_all | solution.py:777
  94.8 2.3 add_convert_fusion
  101.8 20.6 %attention_backward.2 = (bf16[576,512]{1,0:T(8,128)(2,1)}, bf16[1024,384]{1,0:T(8,128)(2,1)}, bf16[384,1024]{1,0:T(8,128)(2,1)}, bf16[384,1024]{1,0:T(8,128)(2,1...) custom-call(bf16[576,512]{1,0:T(8,128)(2,1)} %copy-done.7, ...), custom_call_target="tpu_custom_call", output_to_operand_aliasing={{0}: (3, {})} | custom-call | tf_op jit(solution)/shard_map/attention_backward/pallas_call | solution.py:603
  122.6 12.7 %collective-permute-done.3 = bf16[576,512]{1,0:T(8,128)(2,1)} collective-permute-done((bf16[576,512]{1,0:T(8,128)(2,1)S(1)}, bf16[576,512]{1,0:T(8,128)(2,1)}, u32[]{:S(2)}, u32[]{:S(2)}) %collective-permute-start.3) | collective-permute-done | bytes 589856 | tf_op jit(solution)/shard_map/ppermute | solution.py:669
  139.5 2.7 collective-permute-start.20
  143.4 13.5 %attention_backward.3 = (bf16[144,512]{1,0:T(8,128)(2,1)}, bf16[1024,512]{1,0:T(8,128)(2,1)}, bf16[1024,128]{1,0:T(8,128)(2,1)}, bf16[128,1024]{1,0:T(8,128)(2,1...) custom-call(bf16[144,512]{1,0:T(8,128)(2,1)} %copy-done.11, ...), custom_call_target="tpu_custom_call", output_to_operand_aliasing={{0}: (4, {})} | custom-call | tf_op jit(solution)/shard_map/attention_backward/pallas_call | solution.py:603
  158.8 3.6 %collective-permute-start.23 = (bf16[144,512]{1,0:T(8,128)(2,1)S(1)}, bf16[144,512]{1,0:T(8,128)(2,1)S(1)}, u32[]{:S(2)}, u32[]{:S(2)}) collective-permute-start(bf16[144,512]{1,0:T(8,128)(2,1)S(1)} %add_convert_fusion.5), channel_id=1, source_target_pairs={{0,16},{1,17},{2,18},{3,19},{4,20},{5,21},{6,22},{7,23},{8,24},{9,... | collective-permute-start | bytes 442376 | tf_op jit(solution)/shard_map/ppermute | solution.py:669
  163.8 3.6 %collective-permute-done.22 = bf16[144,512]{1,0:T(8,128)(2,1)S(1)} collective-permute-done((bf16[144,512]{1,0:T(8,128)(2,1)S(1)}, bf16[144,512]{1,0:T(8,128)(2,1)S(1)}, u32[]{:S(2)}, u32[]{:S(2)}) %collective-permute-start.22) | collective-permute-done | bytes 147488 | tf_op jit(solution)/shard_map/ppermute | solution.py:669
  167.3 6.0 %collective-permute-done.23 = bf16[144,512]{1,0:T(8,128)(2,1)S(1)} collective-permute-done((bf16[144,512]{1,0:T(8,128)(2,1)S(1)}, bf16[144,512]{1,0:T(8,128)(2,1)S(1)}, u32[]{:S(2)}, u32[]{:S(2)}) %collective-permute-start.23) | collective-permute-done | bytes 147488 | tf_op jit(solution)/shard_map/ppermute | solution.py:669
  174.9 3.0 %collective-permute-start.27 = (bf16[576,512]{1,0:T(8,128)(2,1)}, bf16[576,512]{1,0:T(8,128)(2,1)S(1)}, u32[]{:S(2)}, u32[]{:S(2)}) collective-permute-start(bf16[576,512]{1,0:T(8,128)(2,1)} %get-tuple-element.88), channel_id=1, source_target_pairs={{0,6},{1,7},{2,4},{3,5},{4,2},{5,3},{6,0},{7,1},{8,14},{9,15},{10,... | collective-permute-start | bytes 1769480 | tf_op jit(solution)/shard_map/ppermute | solution.py:669
  180.1 30.9 %collective-permute-done.7 = bf16[208,512]{1,0:T(8,128)(2,1)} collective-permute-done((bf16[208,512]{1,0:T(8,128)(2,1)}, bf16[208,512]{1,0:T(8,128)(2,1)}, u32[]{:S(2)}, u32[]{:S(2)}) %collective-permute-start.7) | collective-permute-done | bytes 213024 | tf_op jit(solution)/shard_map/ppermute | solution.py:669
  212.3 4.8 %collective-permute-start.10 = (bf16[52,512]{1,0:T(8,128)(2,1)S(1)}, bf16[52,512]{1,0:T(8,128)(2,1)S(1)}, u32[]{:S(2)}, u32[]{:S(2)}) collective-permute-start(bf16[52,512]{1,0:T(8,128)(2,1)S(1)} %get-tuple-element.103), channel_id=1, source_target_pairs={{0,16},{1,17},{2,18},{3,19},{4,20},{5,21},{6,22},{7,23},{8,24},{9,... | collective-permute-start | bytes 159752 | tf_op jit(solution)/shard_map/ppermute | solution.py:669
  219.3 3.9 %collective-permute-done.11 = bf16[52,512]{1,0:T(8,128)(2,1)S(1)} collective-permute-done((bf16[52,512]{1,0:T(8,128)(2,1)S(1)}, bf16[52,512]{1,0:T(8,128)(2,1)S(1)}, u32[]{:S(2)}, u32[]{:S(2)}) %collective-permute-start.11) | collective-permute-done | bytes 53280 | tf_op jit(solution)/shard_map/ppermute | solution.py:669
  223.4 2.4 collective-permute-start.13
  228.8 3.0 %collective-permute-done.14 = bf16[52,512]{1,0:T(8,128)(2,1)S(1)} collective-permute-done((bf16[52,512]{1,0:T(8,128)(2,1)S(1)}, bf16[52,512]{1,0:T(8,128)(2,1)S(1)}, u32[]{:S(2)}, u32[]{:S(2)}) %collective-permute-start.14) | collective-permute-done | bytes 53280 | tf_op jit(solution)/shard_map/ppermute | solution.py:669
  236.1 4.5 %all-to-all-start.3 = ((bf16[8,128,512]{2,1,0:T(8,128)(2,1)}), bf16[8,128,512]{2,1,0:T(8,128)(2,1)S(1)}, u32[]{:S(2)}, u32[]{:S(2)}) async-start(bf16[8,128,512]{2,1,0:T(8,128)(2,1)} %bitcast.68), calls=%async_computation.3 | async-start | bytes 2097152 | tf_op jit(solution)/shard_map/all_to_all | solution.py:777
  241.5 5.9 %collective-permute-done.17 = bf16[208,512]{1,0:T(8,128)(2,1)} collective-permute-done((bf16[208,512]{1,0:T(8,128)(2,1)}, bf16[208,512]{1,0:T(8,128)(2,1)}, u32[]{:S(2)}, u32[]{:S(2)}) %collective-permute-start.17) | collective-permute-done | bytes 213024 | tf_op jit(solution)/shard_map/ppermute | solution.py:669
  254.5 7.5 %all-to-all-done.3 = bf16[8,128,512]{2,1,0:T(8,128)(2,1)S(1)} async-done(((bf16[8,128,512]{2,1,0:T(8,128)(2,1)}), bf16[8,128,512]{2,1,0:T(8,128)(2,1)S(1)}, u32[]{:S(2)}, u32[]{:S(2)}) %all-to-all-start.3) | async-done | bytes 1048608 | tf_op jit(solution)/shard_map/all_to_all | solution.py:777
  262.0 6.5 %finish.2 = (f32[2048,512]{1,0:T(8,128)}, f32[512,2048]{1,0:T(8,128)}, f32[512,512]{1,0:T(8,128)}) custom-call(s32[1]{0:T(128)} %bitcast.3.refs_5_.core_ref, bf16[2304,512]{1,0:T(8,128)(2,1)} %copy-done.2, bf16[2304,512]{1,0:T(8,128)(2,1)} %collective-permute-done.28.other_ref), custom_call_target="tpu_custom_call" | custom-call | tf_op jit(solution)/shard_map/finish/pallas_call | solution.py:652
  268.5 3.3 %finish.3 = (f32[512,512]{1,0:T(8,128)}, f32[512,512]{1,0:T(8,128)}, f32[512,512]{1,0:T(8,128)}) custom-call(s32[1]{0:T(128)} %bitcast.3.refs_5_.core_ref, bf16[832,512]{1,0:T(8,128)(2,1)} %pad_maximum_fusion.3.own_ref, bf16[832,512]{1,0:T(8,128)(2,1)} %collective-permute-done.18.other_ref, f32[2048,512]{1,0:T(8,128)} %get-tuple-element.125.refs_0_, ...), custom_call_target="tpu_custom_call" | custom-call | tf_op jit(solution)/shard_map/finish/pallas_call | solution.py:652
  (110 shorter events, 39.6 us)
Async XLA Ops:
  33.8 30.6 %all-to-all-start.2 = ((bf16[8,128,512]{2,1,0:T(8,128)(2,1)}), bf16[8,128,512]{2,1,0:T(8,128)(2,1)S(1)}, u32[]{:S(2)}, u32[]{:S(2)}) async-start(bf16[8,128,512]{2,1,0:T(8,128)(2,1)} %param.21), calls=%async_computation.2 | async-start | bytes 2097152 | tf_op jit(solution)/shard_map/all_to_all | solution.py:777
  88.8 53.6 %all-to-all-start.1 = ((bf16[8,128,512]{2,1,0:T(8,128)(2,1)}), bf16[8,128,512]{2,1,0:T(8,128)(2,1)S(1)}, u32[]{:S(2)}, u32[]{:S(2)}) async-start(bf16[8,128,512]{2,1,0:T(8,128)(2,1)} %bitcast.69), calls=%async_computation.1 | async-start | bytes 2097152 | tf_op jit(solution)/shard_map/all_to_all | solution.py:777
  98.3 24.3 %collective-permute-start.1 = (bf16[576,512]{1,0:T(8,128)(2,1)S(1)}, bf16[576,512]{1,0:T(8,128)(2,1)}, u32[]{:S(2)}, u32[]{:S(2)}) collective-permute-start(bf16[576,512]{1,0:T(8,128)(2,1)S(1)} %get-tuple-element.79.refs_0_), channel_id=1, source_target_pairs={{0,4},{1,5},{2,6},{3,7},{4,0},{5,1},{6,2},{7,3},{8,12},{9,13},{10,... | collective-permute-start | bytes 1769480 | tf_op jit(solution)/shard_map/ppermute | solution.py:669
  100.3 22.3 %collective-permute-start.2 = (bf16[576,512]{1,0:T(8,128)(2,1)S(1)}, bf16[576,512]{1,0:T(8,128)(2,1)}, u32[]{:S(2)}, u32[]{:S(2)}) collective-permute-start(bf16[576,512]{1,0:T(8,128)(2,1)S(1)} %get-tuple-element.78.refs_1_), channel_id=1, source_target_pairs={{0,2},{1,3},{2,0},{3,1},{4,6},{5,7},{6,4},{7,5},{8,10},{9,11},{10,... | collective-permute-start | bytes 1769480 | tf_op jit(solution)/shard_map/ppermute | solution.py:669
  101.8 33.6 %collective-permute-start.3 = (bf16[576,512]{1,0:T(8,128)(2,1)S(1)}, bf16[576,512]{1,0:T(8,128)(2,1)}, u32[]{:S(2)}, u32[]{:S(2)}) collective-permute-start(bf16[576,512]{1,0:T(8,128)(2,1)S(1)} %get-tuple-element.77.refs_2_), channel_id=1, source_target_pairs={{0,6},{1,7},{2,4},{3,5},{4,2},{5,3},{6,0},{7,1},{8,14},{9,15},{10,... | collective-permute-start | bytes 1769480 | tf_op jit(solution)/shard_map/ppermute | solution.py:669
  122.4 34.6 %collective-permute-start.4 = (bf16[832,384]{1,0:T(8,128)(2,1)}, bf16[832,384]{1,0:T(8,128)(2,1)S(1)}, u32[]{:S(2)}, u32[]{:S(2)}) collective-permute-start(bf16[832,384]{1,0:T(8,128)(2,1)} %get-tuple-element.62), channel_id=1, source_target_pairs={{0,1},{1,0},{2,3},{3,2},{4,5},{5,4},{6,7},{7,6},{8,9},{9,8},{10,11... | collective-permute-start | bytes 1916936 | tf_op jit(solution)/shard_map/ppermute | solution.py:669
  138.0 19.2 %collective-permute-start.19 = (bf16[144,512]{1,0:T(8,128)(2,1)S(1)}, bf16[144,512]{1,0:T(8,128)(2,1)S(1)}, u32[]{:S(2)}, u32[]{:S(2)}) collective-permute-start(bf16[144,512]{1,0:T(8,128)(2,1)S(1)} %get-tuple-element.96.refs_0_), channel_id=1, source_target_pairs={{0,8},{1,9},{2,10},{3,11},{4,12},{5,13},{6,14},{7,15},{8,0},{9,1},... | collective-permute-start | bytes 442376 | tf_op jit(solution)/shard_map/ppermute | solution.py:669
  139.5 17.8 %collective-permute-start.20 = (bf16[144,512]{1,0:T(8,128)(2,1)S(1)}, bf16[144,512]{1,0:T(8,128)(2,1)S(1)}, u32[]{:S(2)}, u32[]{:S(2)}) collective-permute-start(bf16[144,512]{1,0:T(8,128)(2,1)S(1)} %get-tuple-element.95.refs_1_), channel_id=1, source_target_pairs={{0,16},{1,17},{2,18},{3,19},{4,20},{5,21},{6,22},{7,23},{8,24},{9,... | collective-permute-start | bytes 442376 | tf_op jit(solution)/shard_map/ppermute | solution.py:669
  142.1 15.1 %collective-permute-start.21 = (bf16[144,512]{1,0:T(8,128)(2,1)S(1)}, bf16[144,512]{1,0:T(8,128)(2,1)S(1)}, u32[]{:S(2)}, u32[]{:S(2)}) collective-permute-start(bf16[144,512]{1,0:T(8,128)(2,1)S(1)} %get-tuple-element.94.refs_2_), channel_id=1, source_target_pairs={{0,24},{1,25},{2,26},{3,27},{4,28},{5,29},{6,30},{7,31},{8,16},{9,... | collective-permute-start | bytes 442376 | tf_op jit(solution)/shard_map/ppermute | solution.py:669
  158.2 9.1 %collective-permute-start.22 = (bf16[144,512]{1,0:T(8,128)(2,1)S(1)}, bf16[144,512]{1,0:T(8,128)(2,1)S(1)}, u32[]{:S(2)}, u32[]{:S(2)}) collective-permute-start(bf16[144,512]{1,0:T(8,128)(2,1)S(1)} %add_convert_fusion.5), channel_id=1, source_target_pairs={{0,8},{1,9},{2,10},{3,11},{4,12},{5,13},{6,14},{7,15},{8,0},{9,1},... | collective-permute-start | bytes 442376 | tf_op jit(solution)/shard_map/ppermute | solution.py:669
  158.8 14.5 %collective-permute-start.23 = (bf16[144,512]{1,0:T(8,128)(2,1)S(1)}, bf16[144,512]{1,0:T(8,128)(2,1)S(1)}, u32[]{:S(2)}, u32[]{:S(2)}) collective-permute-start(bf16[144,512]{1,0:T(8,128)(2,1)S(1)} %add_convert_fusion.5), channel_id=1, source_target_pairs={{0,16},{1,17},{2,18},{3,19},{4,20},{5,21},{6,22},{7,23},{8,24},{9,... | collective-permute-start | bytes 442376 | tf_op jit(solution)/shard_map/ppermute | solution.py:669
  162.4 11.0 %collective-permute-start.24 = (bf16[144,512]{1,0:T(8,128)(2,1)S(1)}, bf16[144,512]{1,0:T(8,128)(2,1)S(1)}, u32[]{:S(2)}, u32[]{:S(2)}) collective-permute-start(bf16[144,512]{1,0:T(8,128)(2,1)S(1)} %add_convert_fusion.5), channel_id=1, source_target_pairs={{0,24},{1,25},{2,26},{3,27},{4,28},{5,29},{6,30},{7,31},{8,16},{9,... | collective-permute-start | bytes 442376 | tf_op jit(solution)/shard_map/ppermute | solution.py:669
  163.5 14.9 %collective-permute-start.6 = (bf16[208,512]{1,0:T(8,128)(2,1)S(1)}, bf16[208,512]{1,0:T(8,128)(2,1)S(1)}, u32[]{:S(2)}, u32[]{:S(2)}) collective-permute-start(bf16[208,512]{1,0:T(8,128)(2,1)S(1)} %get-tuple-element.84), channel_id=1, source_target_pairs={{0,4},{1,5},{2,6},{3,7},{4,0},{5,1},{6,2},{7,3},{8,12},{9,13},{10,... | collective-permute-start | bytes 638984 | tf_op jit(solution)/shard_map/ppermute | solution.py:669
  174.4 44.1 %collective-permute-start.25 = (bf16[576,512]{1,0:T(8,128)(2,1)}, bf16[576,512]{1,0:T(8,128)(2,1)S(1)}, u32[]{:S(2)}, u32[]{:S(2)}) collective-permute-start(bf16[576,512]{1,0:T(8,128)(2,1)} %get-tuple-element.88), channel_id=1, source_target_pairs={{0,4},{1,5},{2,6},{3,7},{4,0},{5,1},{6,2},{7,3},{8,12},{9,13},{10,... | collective-permute-start | bytes 1769480 | tf_op jit(solution)/shard_map/ppermute | solution.py:669
  174.4 44.1 %collective-permute-start.26 = (bf16[576,512]{1,0:T(8,128)(2,1)}, bf16[576,512]{1,0:T(8,128)(2,1)S(1)}, u32[]{:S(2)}, u32[]{:S(2)}) collective-permute-start(bf16[576,512]{1,0:T(8,128)(2,1)} %get-tuple-element.88), channel_id=1, source_target_pairs={{0,2},{1,3},{2,0},{3,1},{4,6},{5,7},{6,4},{7,5},{8,10},{9,11},{10,... | collective-permute-start | bytes 1769480 | tf_op jit(solution)/shard_map/ppermute | solution.py:669
  174.9 43.6 %collective-permute-start.27 = (bf16[576,512]{1,0:T(8,128)(2,1)}, bf16[576,512]{1,0:T(8,128)(2,1)S(1)}, u32[]{:S(2)}, u32[]{:S(2)}) collective-permute-start(bf16[576,512]{1,0:T(8,128)(2,1)} %get-tuple-element.88), channel_id=1, source_target_pairs={{0,6},{1,7},{2,4},{3,5},{4,2},{5,3},{6,0},{7,1},{8,14},{9,15},{10,... | collective-permute-start | bytes 1769480 | tf_op jit(solution)/shard_map/ppermute | solution.py:669
  177.9 33.0 %collective-permute-start.7 = (bf16[208,512]{1,0:T(8,128)(2,1)}, bf16[208,512]{1,0:T(8,128)(2,1)}, u32[]{:S(2)}, u32[]{:S(2)}) collective-permute-start(bf16[208,512]{1,0:T(8,128)(2,1)} %get-tuple-element.85), channel_id=1, source_target_pairs={{0,2},{1,3},{2,0},{3,1},{4,6},{5,7},{6,4},{7,5},{8,10},{9,11},{10,... | collective-permute-start | bytes 638984 | tf_op jit(solution)/shard_map/ppermute | solution.py:669
  179.1 31.8 %collective-permute-start.8 = (bf16[208,512]{1,0:T(8,128)(2,1)S(1)}, bf16[208,512]{1,0:T(8,128)(2,1)}, u32[]{:S(2)}, u32[]{:S(2)}) collective-permute-start(bf16[208,512]{1,0:T(8,128)(2,1)S(1)} %get-tuple-element.86), channel_id=1, source_target_pairs={{0,6},{1,7},{2,4},{3,5},{4,2},{5,3},{6,0},{7,1},{8,14},{9,15},{10,... | collective-permute-start | bytes 638984 | tf_op jit(solution)/shard_map/ppermute | solution.py:669
  212.3 7.0 %collective-permute-start.10 = (bf16[52,512]{1,0:T(8,128)(2,1)S(1)}, bf16[52,512]{1,0:T(8,128)(2,1)S(1)}, u32[]{:S(2)}, u32[]{:S(2)}) collective-permute-start(bf16[52,512]{1,0:T(8,128)(2,1)S(1)} %get-tuple-element.103), channel_id=1, source_target_pairs={{0,16},{1,17},{2,18},{3,19},{4,20},{5,21},{6,22},{7,23},{8,24},{9,... | collective-permute-start | bytes 159752 | tf_op jit(solution)/shard_map/ppermute | solution.py:669
  219.2 42.8 %collective-permute-start.28 = (bf16[2304,512]{1,0:T(8,128)(2,1)S(1)}, bf16[2304,512]{1,0:T(8,128)(2,1)}, u32[]{:S(2)}, u32[]{:S(2)}) collective-permute-start(bf16[2304,512]{1,0:T(8,128)(2,1)S(1)} %pad_maximum_fusion.1.own_ref), channel_id=1, source_target_pairs={{0,1},{1,0},{2,3},{3,2},{4,5},{5,4},{6,7},{7,6},{8,9},{9,8},{10,11... | collective-permute-start | bytes 7077896 | tf_op jit(solution)/shard_map/ppermute | solution.py:669
  232.6 8.9 %collective-permute-start.15 = (bf16[208,512]{1,0:T(8,128)(2,1)}, bf16[208,512]{1,0:T(8,128)(2,1)}, u32[]{:S(2)}, u32[]{:S(2)}) collective-permute-start(bf16[208,512]{1,0:T(8,128)(2,1)} %pad_maximum_fusion.7), channel_id=1, source_target_pairs={{0,4},{1,5},{2,6},{3,7},{4,0},{5,1},{6,2},{7,3},{8,12},{9,13},{10,... | collective-permute-start | bytes 638984 | tf_op jit(solution)/shard_map/ppermute | solution.py:669
  234.3 7.1 %collective-permute-start.16 = (bf16[208,512]{1,0:T(8,128)(2,1)}, bf16[208,512]{1,0:T(8,128)(2,1)}, u32[]{:S(2)}, u32[]{:S(2)}) collective-permute-start(bf16[208,512]{1,0:T(8,128)(2,1)} %pad_maximum_fusion.7), channel_id=1, source_target_pairs={{0,2},{1,3},{2,0},{3,1},{4,6},{5,7},{6,4},{7,5},{8,10},{9,11},{10,... | collective-permute-start | bytes 638984 | tf_op jit(solution)/shard_map/ppermute | solution.py:669
  234.8 12.5 %collective-permute-start.17 = (bf16[208,512]{1,0:T(8,128)(2,1)}, bf16[208,512]{1,0:T(8,128)(2,1)}, u32[]{:S(2)}, u32[]{:S(2)}) collective-permute-start(bf16[208,512]{1,0:T(8,128)(2,1)} %pad_maximum_fusion.7), channel_id=1, source_target_pairs={{0,6},{1,7},{2,4},{3,5},{4,2},{5,3},{6,0},{7,1},{8,14},{9,15},{10,... | collective-permute-start | bytes 638984 | tf_op jit(solution)/shard_map/ppermute | solution.py:669
  236.1 25.9 %all-to-all-start.3 = ((bf16[8,128,512]{2,1,0:T(8,128)(2,1)}), bf16[8,128,512]{2,1,0:T(8,128)(2,1)S(1)}, u32[]{:S(2)}, u32[]{:S(2)}) async-start(bf16[8,128,512]{2,1,0:T(8,128)(2,1)} %bitcast.68), calls=%async_computation.3 | async-start | bytes 2097152 | tf_op jit(solution)/shard_map/all_to_all | solution.py:777
  (24 other events, 130.4 us)

commit v3 on v2

--- a/solution.py
+++ b/solution.py
@@ -18,8 +18,11 @@
 NEG = -1e30
 STEP_PAIRS = 2
 GAIN_ROWS = 64
-CALLS = ((0, 3), (3, 1))
-STEPS_BEFORE = (1, 2)
+TAIL = "faffafaafaafa"
+GATE_KIB = 512
+TRADED = 11
+FFN_ROWS = 2
+FORWARD_MIB, FFN_MIB, ATTENTION_MIB = 52, 50, 54
 GELU_A = 0.7978845608028654
 GELU_B = 0.044715
 F32 = jnp.float32
@@ -126,6 +129,7 @@
         wkt_ref[...] = wk_ref[...].T
         wvt_ref[...] = wv_ref[...].T
 
+    block = pl.ds(pl.multiple_of(step * BLOCK, BLOCK), BLOCK)
     x = x_ref[...].astype(F32)
     inv = lax.rsqrt(jnp.mean(x * x, -1, keepdims=True) + EPSILON)
     hidden = (x * inv * ga_ref[...]).astype(BF16)
@@ -135,8 +139,9 @@
     v_ref[...] = nt(wvt_ref[...], hidden).astype(BF16)
     same_head = head_mask(CHUNK)
     for sub in range(BLOCK // CHUNK):
+        chunk = step * (BLOCK // CHUNK) + sub
         rows = slice(sub * CHUNK, (sub + 1) * CHUNK)
-        chunk = step * (BLOCK // CHUNK) + sub
+        tokens = pl.ds(pl.multiple_of(chunk * CHUNK, CHUNK), CHUNK)
         band, far_mask, carry, tail, keep = chunk_masks(seg_ref, place_ref, chunk)
         tail_rows = jnp.broadcast_to(tail, (16, CHUNK))
 
@@ -186,7 +191,7 @@
             both = jnp.concatenate([prob_prev, weight.astype(BF16)], 1)
             yield
             attended = pick(nt(both, vt_ext)) + nn(jnp.concatenate(scaled, 1), state_low)
-            a_ref[rows, lanes] = attended.astype(BF16)
+            a_ref[tokens, lanes] = attended.astype(BF16)
             for n, column in enumerate(columns):
                 stats_ref[sub, p, n] = jnp.broadcast_to(column, (2 * CHUNK, CHUNK))
 
@@ -196,8 +201,8 @@
         vp_ref[...] = v_ref[:, rows]
     for end_ref, ref in zip(end_refs, (s_ref, z_ref)):
         end_ref[...] = ref[...]
-    x1 = x + nn(a_ref[...], wo_ref[...])
-    x1_ref[...] = x1
+    x1 = x + nn(a_ref[block], wo_ref[...])
+    x1_ref[block] = x1
     inv = lax.rsqrt(jnp.mean(x1 * x1, -1, keepdims=True) + EPSILON)
     hidden = (x1 * inv * gf_ref[...]).astype(BF16)
     total = x1
@@ -218,37 +223,28 @@
     return inv * (scaled - unit * jnp.mean(unit * scaled, -1, keepdims=True)), d_gain
 
 
-def ffn_backward_kernel(first, last, *refs):
-    dy_ref, x1_ref, gf_ref, wu_ref, wd_ref, core_ref, *refs = refs
-    if not first:
-        dh_in_ref, *refs = refs
-    if last:
-        a_ref, wo_ref, dx1_ref, da_ref, dg_ref, *refs = refs
-    else:
-        dh_out_ref, *refs = refs
-    keep_ref, send_ref, dwd_acc, dwu_acc, *refs = refs
-    if last:
-        dwo_acc, dg_acc = refs
+def ffn_backward_kernel(
+    dy_ref, x1_ref, a_ref, gf_ref, wo_ref, wu_ref, wd_ref, core_ref,
+    dx1_ref, da_ref, dg_ref, keep_ref, send_ref, keep_out_ref, send_out_ref,
+    hidden_ref, dh_ref, dwd_ref, dwu_ref,
+):
     step = pl.program_id(0)
+    core = core_ref[0]
+    gain = gf_ref[...]
 
     @pl.when(step == 0)
     def _():
-        dwd_acc[...] = jnp.zeros_like(dwd_acc)
-        dwu_acc[...] = jnp.zeros_like(dwu_acc)
-        if last:
-            dwo_acc[...] = jnp.zeros_like(dwo_acc)
-            dg_acc[...] = jnp.zeros_like(dg_acc)
-
-    dy = dy_ref[...]
-    x1 = x1_ref[...]
-    gain = gf_ref[...]
-    inv = lax.rsqrt(jnp.mean(x1 * x1, -1, keepdims=True) + EPSILON)
-    hidden = (x1 * inv * gain).astype(BF16)
-    d_hidden = jnp.zeros(x1.shape, F32) if first else dh_in_ref[...]
-    width = x1.shape[1]
-    for f in range(wu_ref.shape[1] // width):
-        cols = slice(f * width, (f + 1) * width)
-        up = nn(hidden, wu_ref[:, cols])
+        x1 = x1_ref[...]
+        inv = lax.rsqrt(jnp.mean(x1 * x1, -1, keepdims=True) + EPSILON)
+        hidden_ref[...] = (x1 * inv * gain).astype(BF16)
+        dh_ref[...] = jnp.zeros_like(dh_ref)
+
+    for part in range(FFN_ROWS):
+        size = dy_ref.shape[0] // FFN_ROWS
+        rows = slice(part * size, (part + 1) * size)
+        dy = dy_ref[rows]
+        hidden = hidden_ref[rows]
+        up = nn(hidden, wu_ref[...])
         square = up * up
         tanh = jnp.tanh(GELU_A * up * (1.0 + GELU_B * square))
         half = 0.5 * (1.0 + tanh)
@@ -256,27 +252,25 @@
         slope = half + 0.5 * up * (1.0 - tanh * tanh) * (
             GELU_A + (3.0 * GELU_A * GELU_B) * square
         )
-        d_up = (slope * nt(dy, wd_ref[cols])).astype(BF16)
-        dwd_acc[cols] += tn(act, dy)
-        dwu_acc[cols] += tn(hidden, d_up)
-        d_hidden = d_hidden + nt(d_up, wu_ref[:, cols])
-    if last:
-        d_norm, d_gain = norm_backward(x1, gain, d_hidden)
-        dx1 = dy.astype(F32) + d_norm
-        dg_acc[...] += jnp.broadcast_to(d_gain, dg_acc.shape)
+        d_up = (slope * nt(dy, wd_ref[...])).astype(BF16)
+        dh_ref[rows] += nt(d_up, wu_ref[...])
+        dwd, dwu = tn(act, dy), tn(hidden, d_up)
+        if part:
+            dwd, dwu = dwd + dwd_ref[...], dwu + dwu_ref[...]
+        dwd_ref[...], dwu_ref[...] = dwd, dwu
+    put_halves((dwd_ref, dwu_ref), core, keep_ref, send_ref)
+
+    @pl.when(step == pl.num_programs(0) - 1)
+    def _():
+        x1 = x1_ref[...]
+        d_norm, d_gain = norm_backward(x1, gain, dh_ref[...])
+        dx1 = dy_ref[...].astype(F32) + d_norm
+        dg_ref[...] = jnp.broadcast_to(d_gain, dg_ref.shape)
         dx1_ref[...] = dx1
         d_branch = dx1.astype(BF16)
-        dwo_acc[...] += tn(a_ref[...], d_branch)
         da_ref[...] = nt(d_branch, wo_ref[...]).astype(BF16)
-    else:
-        dh_out_ref[...] = d_hidden
-
-    @pl.when(step == pl.num_programs(0) - 1)
-    def _():
-        sums = (dwd_acc, dwu_acc) + ((dwo_acc,) if last else ())
-        put_halves(sums, core_ref[0], keep_ref, send_ref)
-        if last:
-            dg_ref[...] = dg_acc[...]
+        dwd_ref[...] = tn(a_ref[...], d_branch)
+        put_halves((dwd_ref,), core, keep_out_ref, send_out_ref)
 
 
 def put_halves(sums, core, keep_ref, send_ref):
@@ -290,19 +284,14 @@
     return at
 
 
-def attention_backward_kernel(last, earlier, entries, *refs):
-    (da_ref, q_ref, k_ref, v_ref, kprev_ref, vprev_ref, stats_ref, states_ref, sums_ref,
-     seg_ref, h_ref, place_ref, *refs) = refs
+def attention_backward_kernel(entries, *refs):
+    (x_ref, q_ref, h_ref, k_ref, v_ref, kprev_ref, vprev_ref, stats_ref, states_ref, sums_ref,
+     da_ref, seg_ref, dx1_ref, place_ref, ga_ref, dgf_ref, wq_ref, wk_ref, wv_ref, *refs) = refs
     entry_refs, refs = refs[:entries], refs[entries:]
-    if last:
-        x_ref, dx1_ref, ga_ref, dgf_ref, wq_ref, wk_ref, wv_ref, *refs = refs
-        earlier_refs, refs = refs[: 3 * earlier], refs[3 * earlier :]
-        dx_ref, *refs = refs
-    dq_ref, dk_ref, dv_ref, keep_ref, send_ref, *refs = refs
+    dx_ref, keep_ref, send_ref, *refs = refs
     end_refs, refs = refs[: min(entries, 3)], refs[min(entries, 3) :]
-    r_ref, dkc_ref, dvc_ref, dwq_acc, dwk_acc, dwv_acc, *refs = refs
-    if last:
-        dg_acc, wkt_ref, wvt_ref = refs
+    (r_ref, dkc_ref, dvc_ref, dq_ref, dk_ref, dv_ref, dwq_acc, dwk_acc, dwv_acc, dg_acc,
+     wkt_ref, wvt_ref) = refs
     step = pl.program_id(0)
     block = pl.num_programs(0) - 1 - step
 
@@ -312,23 +301,23 @@
         dwq_acc[...] = jnp.zeros_like(dwq_acc)
         dwk_acc[...] = jnp.zeros_like(dwk_acc)
         dwv_acc[...] = jnp.zeros_like(dwv_acc)
-        if last:
-            dg_acc[...] = jnp.zeros_like(dg_acc)
-            wkt_ref[...] = wk_ref[...].T
-            wvt_ref[...] = wv_ref[...].T
+        dg_acc[...] = jnp.zeros_like(dg_acc)
+        wkt_ref[...] = wk_ref[...].T
+        wvt_ref[...] = wv_ref[...].T
 
     lane = lax.broadcasted_iota(jnp.int32, (CHUNK, CHUNK), 1)
     same_head = head_mask(2 * CHUNK)
     for sub in reversed(range(BLOCK // CHUNK)):
+        chunk = block * (BLOCK // CHUNK) + sub
         rows = slice(sub * CHUNK, (sub + 1) * CHUNK)
-        chunk = block * (BLOCK // CHUNK) + sub
+        tokens = pl.ds(pl.multiple_of(chunk * CHUNK, CHUNK), CHUNK)
         band, far_mask, carry, tail, keep = chunk_masks(seg_ref, place_ref, chunk)
         tail_rows = jnp.broadcast_to(tail, (CHUNK, CHUNK))
 
         def body(p):
             lanes = slice(p * 128, (p + 1) * 128)
             qp = q_ref[rows, lanes]
-            da = da_ref[rows, lanes]
+            da = da_ref[tokens, lanes]
             kt = k_ref[lanes, rows]
             vt = v_ref[lanes, rows]
             if sub == 0:
@@ -414,24 +403,21 @@
             dq_ref[rows, lanes] = dq.astype(BF16)
             dk_ref[lanes, rows] = dk.astype(BF16)
 
-        in_step(body(p) for p in range(r_ref.shape[0]))
+        for first in range(0, PAIRS, STEP_PAIRS):
+            in_step(body(p) for p in range(first, first + STEP_PAIRS))
     for end_ref, ref in zip(end_refs, (r_ref, dkc_ref, dvc_ref)):
         end_ref[...] = ref[...]
-    dim = h_ref.shape[1]
+    dim = x_ref.shape[1]
+    tokens = pl.ds(pl.multiple_of(block * BLOCK, BLOCK), BLOCK)
     hidden_t = h_ref[...].T
-    dwq_acc[...] += nn(hidden_t, dq_ref[...])
-    dwk_acc[...] += nt(hidden_t, dk_ref[...])
-    dwv_acc[...] += nt(hidden_t, dv_ref[...])
-    if last:
-        mine = (dq_ref, dk_ref, dv_ref)
-        dq, dk, dv = (
-            jnp.concatenate([ref[...] for ref in earlier_refs[n::3] + [mine[n]]], min(n, 1) ^ 1)
-            for n in range(3)
-        )
-        d_hidden = nt(dq, wq_ref[...]) + tn(dk, wkt_ref[...]) + tn(dv, wvt_ref[...])
-        d_norm, d_gain = norm_backward(x_ref[...].astype(F32), ga_ref[...], d_hidden)
-        dg_acc[...] += jnp.broadcast_to(d_gain, dg_acc.shape)
-        dx_ref[...] = (dx1_ref[...] + d_norm).astype(BF16)
+    dq, dk, dv = dq_ref[...], dk_ref[...], dv_ref[...]
+    dwq_acc[...] += nn(hidden_t, dq)
+    dwk_acc[...] += nt(hidden_t, dk)
+    dwv_acc[...] += nt(hidden_t, dv)
+    d_hidden = nt(dq, wq_ref[...]) + tn(dk, wkt_ref[...]) + tn(dv, wvt_ref[...])
+    d_norm, d_gain = norm_backward(x_ref[...].astype(F32), ga_ref[...], d_hidden)
+    dg_acc[...] += jnp.broadcast_to(d_gain, dg_acc.shape)
+    dx_ref[...] = (dx1_ref[tokens] + d_norm).astype(BF16)
 
     @pl.when(step == pl.num_programs(0) - 1)
     def _():
@@ -439,28 +425,32 @@
         at = put_halves((dwq_acc, dwk_acc, dwv_acc), core, keep_ref, send_ref)
         keep_ref[at:] = jnp.zeros((GAIN_ROWS, keep_ref.shape[1]), BF16)
         send_ref[at:] = jnp.zeros((GAIN_ROWS, keep_ref.shape[1]), BF16)
-        if last:
-            width = keep_ref.shape[1]
-            gains = [
-                ref[:1, n : n + width] for ref in (dg_acc, dgf_ref) for n in range(0, dim, width)
-            ]
-            gains += [jnp.zeros((16 - len(gains), width), F32)]
-            gains = jnp.concatenate(gains, 0)
-            keep_ref[at : at + 16] = jnp.where(core == 0, gains, 0.0).astype(BF16)
-            send_ref[at : at + 16] = jnp.where(core == 0, 0.0, gains).astype(BF16)
+        gains = jnp.concatenate([dg_acc[:1], dgf_ref[:1], jnp.zeros((14, dim), F32)], 0)
+        keep_ref[at : at + 16] = jnp.where(core == 0, gains, 0.0).astype(BF16)
+        send_ref[at : at + 16] = jnp.where(core == 0, 0.0, gains).astype(BF16)
+
+
+HELD = pl.BlockSpec(memory_space=pltpu.VMEM)
 
 
 def whole(shape):
     return pl.BlockSpec(shape, lambda i: (0,) * len(shape))
 
 
+FFN_IN = HELD
+
+
 def tokens_of(width, index=lambda i: i):
     return pl.BlockSpec((BLOCK, width), lambda i: (index(i), 0))
 
 
-def params():
+def of_chunks(shape, index=lambda i: i):
+    return pl.BlockSpec((BLOCK // CHUNK,) + shape, lambda i: (index(i),) + (0,) * len(shape))
+
+
+def params(mib):
     return pltpu.CompilerParams(
-        vmem_limit_bytes=VMEM_LIMIT, dimension_semantics=("arbitrary",)
+        vmem_limit_bytes=mib * 1024 * 1024, dimension_semantics=("arbitrary",)
     )
 
 
@@ -472,7 +462,6 @@
     length, dim = x.shape
     ff = wu.shape[1]
     chunks = length // CHUNK
-    per = BLOCK // CHUNK
     row = tokens_of(dim)
     column = pl.BlockSpec((dim, BLOCK), lambda i: (0, i))
     state_shape = (PAIRS, 4 * HEAD, 2 * HEAD)
@@ -483,15 +472,11 @@
         functools.partial(forward_kernel, len(entry)),
         grid=(length // BLOCK,),
         in_specs=[
-            row, whole(segments.shape), SMEM, whole((1, dim)), whole((1, dim)),
-            whole((dim, dim)), whole((dim, dim)), whole((dim, dim)), whole((dim, dim)),
-            whole((dim, ff)), whole((ff, dim)),
+            row, HELD, SMEM, HELD, HELD, HELD, HELD, HELD, HELD, HELD, HELD,
         ] + [whole(array.shape) for array in entry],
         out_specs=[
-            row, row, row, row, row, column, column,
-            pl.BlockSpec((per,) + stat_shape, lambda i: (i, 0, 0, 0, 0)),
-            pl.BlockSpec((per,) + state_shape, lambda i: (i, 0, 0, 0)),
-            pl.BlockSpec((per,) + sum_shape, lambda i: (i, 0, 0, 0)),
+            row, HELD, HELD, row, row, column, column,
+            of_chunks(stat_shape), of_chunks(state_shape), of_chunks(sum_shape),
         ] + [whole(shape) for shape, _ in ends],
         out_shape=[
             sds((length, dim), BF16), sds((length, dim), F32), sds((length, dim), BF16),
@@ -505,7 +490,7 @@
             pltpu.VMEM((dim, CHUNK), BF16), pltpu.VMEM((dim, CHUNK), BF16),
             pltpu.VMEM((dim, dim), BF16), pltpu.VMEM((dim, dim), BF16),
         ],
-        compiler_params=params(),
+        compiler_params=params(FORWARD_MIB),
         name="layer_forward",
     )(x, segments, place, gain_attn, gain_ffn, wq, wk, wv, wo, wu, wd, *entry)
 
@@ -514,88 +499,53 @@
 ANY = pl.BlockSpec(memory_space=pl.ANY)
 
 
-def run_ffn_backward(part, part_count, dy, x1, gain_ffn, wu, wd, core, d_hidden, a, wo):
-    first, last = part == 0, part == part_count - 1
+def run_ffn_backward(dy, x1, a, gain_ffn, wo, wu, wd, core):
     length, dim = dy.shape
-    ff = wu.shape[1] // part_count
-    half = ff + (dim // 2 if last else 0)
-    row = tokens_of(dim)
-    more_in, more_args, outs, shapes, scratch = [], [], [], [], []
-    if not first:
-        more_in, more_args = [row], [d_hidden]
-    if last:
-        more_in += [row, whole((dim, dim))]
-        more_args += [a, wo]
-        outs = [row, row, whole((8, dim))]
-        shapes = [sds((length, dim), F32), sds((length, dim), BF16), sds((8, dim), F32)]
-        scratch = [pltpu.VMEM((dim, dim), F32), pltpu.VMEM((8, dim), F32)]
-    else:
-        outs, shapes = [row], [sds((length, dim), F32)]
+    ff = wu.shape[1]
+    step_half = pl.BlockSpec((dim, dim), lambda i: (i, 0))
     return pl.pallas_call(
-        functools.partial(ffn_backward_kernel, first, last),
-        grid=(length // BLOCK,),
+        ffn_backward_kernel,
+        grid=(ff // dim,),
         in_specs=[
-            row, row, whole((1, dim)),
-            pl.BlockSpec((dim, ff), lambda i: (0, part)),
-            pl.BlockSpec((ff, dim), lambda i: (part, 0)),
-            SMEM,
-        ] + more_in,
-        out_specs=outs + [whole((half, dim))] * 2,
-        out_shape=shapes + [sds((half, dim), BF16)] * 2,
-        scratch_shapes=[pltpu.VMEM((ff, dim), F32), pltpu.VMEM((ff, dim), F32)] + scratch,
-        compiler_params=params(),
+            FFN_IN, FFN_IN, FFN_IN, HELD, HELD,
+            pl.BlockSpec((dim, dim), lambda i: (0, i)), step_half, SMEM,
+        ],
+        out_specs=[FFN_IN, FFN_IN, HELD, step_half, step_half, HELD, HELD],
+        out_shape=[
+            sds((length, dim), F32), sds((length, dim), BF16), sds((8, dim), F32),
+            sds((ff, dim), BF16), sds((ff, dim), BF16),
+            sds((dim // 2, dim), BF16), sds((dim // 2, dim), BF16),
+        ],
+        scratch_shapes=[
+            pltpu.VMEM((length, dim), BF16), pltpu.VMEM((length, dim), F32),
+            pltpu.VMEM((dim, dim), F32), pltpu.VMEM((dim, dim), F32),
+        ],
+        compiler_params=params(FFN_MIB),
         name="ffn_backward",
-    )(dy, x1, gain_ffn, wu, wd, core, *more_args)
+    )(dy, x1, a, gain_ffn, wo, wu, wd, core)
 
 
 def run_attention_backward(
-    first, pairs, after, through, x, dx1, da, h, q, k, v, stats, states, sums, segments, place,
-    gain_attn, dgf, wq, wk, wv, earlier, entry,
+    after, through, x, dx1, da, h, q, k, v, stats, states, sums, segments, place,
+    gain_attn, dgf, wq, wk, wv, entry,
 ):
-    last = first + pairs == PAIRS
     length, dim = x.shape
-    width = 2 * HEAD * pairs
-    call = first // pairs
     half = 3 * dim // 2 + GAIN_ROWS
     steps = length // BLOCK
-    per = BLOCK // CHUNK
     back = lambda i: steps - 1 - i
     row = tokens_of(dim, back)
-    part_row = pl.BlockSpec((BLOCK, width), lambda i: (back(i), call))
-    part_column = pl.BlockSpec((width, BLOCK), lambda i: (call, back(i)))
-    prev = pl.BlockSpec((width, CHUNK), lambda i: (call, jnp.maximum(back(i) * per - 1, 0)))
-    rim_in = pl.BlockSpec((width, CHUNK), lambda i: (call, 0))
-    rim = whole((width, CHUNK))
-    r_shape = (pairs, 4 * HEAD, 4 * HEAD)
-    rim_shape = (width, CHUNK)
-
-    def of_pairs(array):
-        shape = array.shape[2:]
-        return pl.BlockSpec((per, pairs) + shape, lambda i: (back(i), call) + (0,) * len(shape))
-
-    entry_in = [whole(r_shape), rim, rim, rim_in, rim_in][: len(entry)]
+    column = pl.BlockSpec((dim, BLOCK), lambda i: (0, back(i)))
+    per = BLOCK // CHUNK
+    prev = pl.BlockSpec((dim, CHUNK), lambda i: (0, jnp.maximum(back(i) * per - 1, 0)))
+    streams = [of_chunks(array.shape[1:], back) for array in (stats, states, sums)]
+    r_shape = (PAIRS, 4 * HEAD, 4 * HEAD)
+    rim_shape = (dim, CHUNK)
     ends = [r_shape, rim_shape, rim_shape][: len(entry)]
-    more_in, more_args, outs, shapes, scratch = [], [], [], [], []
-    if last:
-        square = whole((dim, dim))
-        more_in = [row, row, whole((1, dim)), whole(dgf.shape), square, square, square]
-        more_args = [x, dx1, gain_attn, dgf, wq, wk, wv]
-        for group in earlier:
-            size = group[0].shape[1]
-            column = pl.BlockSpec((size, BLOCK), lambda i: (0, back(i)))
-            more_in += [tokens_of(size, back), column, column]
-            more_args += group
-        outs = [row]
-        shapes = [sds((length, dim), BF16)]
-        scratch = [
-            pltpu.VMEM((8, dim), F32), pltpu.VMEM((dim, dim), BF16), pltpu.VMEM((dim, dim), BF16),
-        ]
-    kernel = functools.partial(attention_backward_kernel, last, len(earlier), len(entry))
+    kernel = functools.partial(attention_backward_kernel, len(entry))
     skip = len(after) + len(through)
-    args = [
-        da, q, k, v, k, v, stats, states, sums, segments, h, place, *entry, *more_args,
-    ]
-    inputs = skip + len(args)
+    streamed = [x, q, h, k, v, k, v, stats, states, sums]
+    held = [da, segments, dx1, place, gain_attn, dgf, wq, wk, wv, *entry]
+    inputs = skip + len(streamed) + len(held)
 
     def body(*refs):
         kernel(*refs[skip:inputs], *refs[inputs + len(through) :])
@@ -604,59 +554,65 @@
         body,
         grid=(steps,),
         input_output_aliases={len(after) + n: n for n in range(len(through))},
-        in_specs=[ANY] * skip + [
-            part_row, part_row, part_column, part_column, prev, prev,
-            of_pairs(stats), of_pairs(states), of_pairs(sums), whole(segments.shape), row, SMEM,
-        ] + entry_in + more_in,
-        out_specs=[ANY] * len(through) + outs + [
-            tokens_of(width, back),
-            pl.BlockSpec((width, BLOCK), lambda i: (0, back(i))),
-            pl.BlockSpec((width, BLOCK), lambda i: (0, back(i))),
-            whole((half, width)), whole((half, width)),
-        ] + [whole(shape) for shape in ends],
-        out_shape=[sds(array.shape, array.dtype) for array in through] + shapes + [
-            sds((length, width), BF16), sds((width, length), BF16), sds((width, length), BF16),
-            sds((half, width), BF16), sds((half, width), BF16),
+        in_specs=[ANY] * skip + [row, row, row, column, column, prev, prev] + streams
+        + [SMEM if array is place else HELD for array in held],
+        out_specs=[ANY] * len(through) + [row, HELD, HELD] + [whole(shape) for shape in ends],
+        out_shape=[sds(array.shape, array.dtype) for array in through] + [
+            sds((length, dim), BF16), sds((half, dim), BF16), sds((half, dim), BF16),
         ] + [sds(shape, F32) for shape in ends],
         scratch_shapes=[
             pltpu.VMEM(r_shape, F32), pltpu.VMEM(rim_shape, F32), pltpu.VMEM(rim_shape, F32),
-            pltpu.VMEM((dim, width), F32), pltpu.VMEM((dim, width), F32),
-            pltpu.VMEM((dim, width), F32),
-        ] + scratch,
-        compiler_params=params(),
+            pltpu.VMEM((BLOCK, dim), BF16), pltpu.VMEM((dim, BLOCK), BF16),
+            pltpu.VMEM((dim, BLOCK), BF16),
+            pltpu.VMEM((dim, dim), F32), pltpu.VMEM((dim, dim), F32), pltpu.VMEM((dim, dim), F32),
+            pltpu.VMEM((8, dim), F32),
+            pltpu.VMEM((dim, dim), BF16), pltpu.VMEM((dim, dim), BF16),
+        ],
+        compiler_params=params(ATTENTION_MIB),
         name="attention_backward",
-    )(*after, *through, *args)
-
-
-def finish_kernel(skip, across, core_ref, own_ref, other_ref, *refs):
-    out_refs = refs[skip:]
-    at = 0
-    width = own_ref.shape[1]
-    for wide, out_ref in zip(across, out_refs):
-        half = out_ref.shape[0] * out_ref.shape[1] // width // 2
+    )(*after, *through, *streamed, *held)
+
+
+def finish_ffn_kernel(core_ref, own_ref, other_ref, down_ref, up_ref, done_ref):
+    half = down_ref.shape[0] // 2
+    for ref, which in ((own_ref, core_ref[0]), (other_ref, 1 - core_ref[0])):
+        rows = pl.ds(pl.multiple_of(which * half, half), half)
+        down_ref[rows] = ref[:half].astype(F32)
+        up_ref[rows] = ref[half:].astype(F32)
+    done_ref[...] = jnp.zeros_like(done_ref)
+
+
+def run_finish_ffn(core_ref, own, other, dim):
+    ff = own.shape[0]
+    block = pl.BlockSpec((dim, dim), lambda i: (i, 0))
+    return pl.pallas_call(
+        finish_ffn_kernel,
+        grid=(ff // dim,),
+        in_specs=[SMEM, block, block],
+        out_specs=[block, pl.BlockSpec((dim, dim), lambda i: (0, i)), whole((8, 128))],
+        out_shape=[sds((ff, dim), F32), sds((dim, ff), F32), sds((8, 128), F32)],
+        compiler_params=params(12),
+        name="finish_ffn",
+    )(core_ref, own, other)
+
+
+def finish_kernel(starts, core_ref, own_ref, other_ref, *out_refs):
+    for at, out_ref in zip(starts, out_refs):
+        half = out_ref.shape[0] // 2
         for ref, which in ((own_ref, core_ref[0]), (other_ref, 1 - core_ref[0])):
-            if wide:
-                rows = out_ref.shape[0]
-                for c in range(half // rows):
-                    start = pl.multiple_of((which * (half // rows) + c) * width, width)
-                    block = ref[at + c * rows : at + (c + 1) * rows]
-                    out_ref[:, pl.ds(start, width)] = block.astype(F32)
-            else:
-                rows = pl.ds(pl.multiple_of(which * half, half), half)
-                out_ref[rows] = ref[at : at + half].astype(F32)
-        at += half
-
-
-def run_finish(core_ref, own, other, across, shapes, after):
-    full = pl.BlockSpec(memory_space=pltpu.VMEM)
+            rows = pl.ds(pl.multiple_of(which * half, half), half)
+            out_ref[rows] = ref[at : at + half].astype(F32)
+
+
+def run_finish(core_ref, own, other, starts, shape):
     return pl.pallas_call(
-        functools.partial(finish_kernel, len(after), across),
-        in_specs=[SMEM, full, full] + [ANY] * len(after),
-        out_specs=[full] * len(shapes),
-        out_shape=[sds(shape, F32) for shape in shapes],
-        compiler_params=pltpu.CompilerParams(vmem_limit_bytes=VMEM_LIMIT),
+        functools.partial(finish_kernel, starts),
+        in_specs=[SMEM, HELD, HELD],
+        out_specs=[HELD] * len(starts),
+        out_shape=[sds(shape, F32)] * len(starts),
+        compiler_params=pltpu.CompilerParams(vmem_limit_bytes=12 * 1024 * 1024),
         name="finish",
-    )(core_ref, own, other, *after)
+    )(core_ref, own, other)
 
 
 def partner(array, seq_bits, row_bits):
@@ -681,7 +637,7 @@
 
 
 PLANE_BITS = ((1, 0), (0, 2), (1, 2))
-DEPTH_BITS = ((2, 0), (4, 0), (6, 0))
+DEPTH_BITS = (2, 4)
 
 
 def cut(total, place):
@@ -691,6 +647,15 @@
 
 def traded(parts, all_bits):
     return [parts[0]] + [partner(part, *bits) for part, bits in zip(parts[1:], all_bits)]
+
+
+def cut_half(total, bit):
+    size = total.shape[0] // 2
+    return [take(total, bit, size), take(total, 1 - bit, size)]
+
+
+def joined_half(own, other, bit):
+    return jnp.where(bit == 0, jnp.concatenate([own, other], 0), jnp.concatenate([other, own], 0))
 
 
 def joined(parts, place):
@@ -704,25 +669,41 @@
     others = [partner(send, 0, 1) for _, send in halves]
     keeps = yield [keep for keep, _ in halves]
     sums = [add(keep, other) for keep, other in zip(keeps, others)]
-    parts = yield cut(jnp.concatenate(sums, 1) if len(sums) > 1 else sums[0], plane)
+    parts = yield cut(jnp.concatenate(sums, 0) if len(sums) > 1 else sums[0], plane)
     parts = traded(parts, PLANE_BITS)
     parts = yield parts
-    parts = yield cut(add(*parts), depth)
-    parts = traded(parts, DEPTH_BITS)
-    parts = yield parts
     total = add(*parts)
+    for bits, bit in zip(DEPTH_BITS, depth):
+        keep, send = yield cut_half(total, bit)
+        other = partner(send, bits, 0)
+        keep, other = yield [keep, other]
+        total = add(keep, other)
     for bits in further_bits():
         total = add(total, partner(total, *bits))
-    (total,) = yield [total]
-    parts = traded([total] * 4, DEPTH_BITS)
-    parts = yield parts
-    (block,) = yield [joined(parts, depth)]
+    for bits, bit in reversed(list(zip(DEPTH_BITS, depth))):
+        (total,) = yield [total]
+        other = partner(total, bits, 0)
+        total, other = yield [total, other]
+        total = joined_half(total, other, bit)
+    (block,) = yield [total]
     parts = traded([block] * 4, PLANE_BITS)
     parts = yield parts
     (own,) = yield [joined(parts, plane)]
     yield [own, partner(own, 0, 1)]
 
 
+def gate(array, *others):
+    return pl.pallas_call(
+        lambda *refs: None,
+        in_specs=[ANY] * (1 + len(others)),
+        out_specs=ANY,
+        out_shape=sds(array.shape, array.dtype),
+        input_output_aliases={0: 0},
+        compiler_params=pltpu.CompilerParams(vmem_limit_bytes=GATE_KIB * 1024),
+        name="gate",
+    )(array, *others)
+
+
 class Reduction:
     def __init__(self, *args):
         self.steps = all_reduce(*args)
@@ -731,11 +712,12 @@
     def step(self):
         self.arrays = self.steps.send(self.arrays)
 
-    def finish(self):
-        for arrays in iter(lambda: self.steps.send(self.arrays), None):
-            self.arrays = arrays
-            if len(arrays) == 2:
-                return arrays
+    def run(self, count):
+        for _ in range(count):
+            self.step()
+
+    def hold(self, *others):
+        self.arrays[0] = gate(self.arrays[0], *others)
 
 
 def further_bits():
@@ -789,7 +771,7 @@
     ga, gf = gain_attn.reshape(1, dim), gain_ffn.reshape(1, dim)
     seq_index, row_index = lax.axis_index("seq"), lax.axis_index("rows")
     core, plane = row_index % 2, seq_index % 2 + 2 * (row_index // 2 % 2)
-    places = core, plane, seq_index // 2 % 4
+    places = core, plane, (seq_index // 2 % 2, seq_index // 4 % 2)
     place = jnp.stack([my_row, my_part * (length // CHUNK), core]).astype(jnp.int32)
 
     x = trade(tokens).reshape(length, dim)
@@ -809,59 +791,52 @@
             entry = shifted((*ends, k[:, length - CHUNK :], v[:, length - CHUNK :]), 1)
     output = trade(out)
     core_ref = place[2:]
-    dx1, da, dgf, keep, send = run_ffn_backward(
-        0, 1, dy, x1, gf, w_up, w_down, core_ref, None, a, w_out
+    dx1, da, dgf, keep, send, keep_out, send_out = run_ffn_backward(
+        dy, x1, a, gf, w_out, w_up, w_down, core_ref
     )
     ffn = Reduction(places, [(keep, send)])
-    backs = [()] * len(CALLS)
+    ffn.run(1)
+    back = ()
     if parts > 1:
-        backs = [
-            (
-                jnp.zeros((pairs, 4 * HEAD, 4 * HEAD), F32),
-                jnp.zeros((pairs * 2 * HEAD, CHUNK), F32),
-                jnp.zeros((pairs * 2 * HEAD, CHUNK), F32),
-            )
-            for _, pairs in CALLS
-        ]
+        rim = jnp.zeros((dim, CHUNK), F32)
+        back = (jnp.zeros((PAIRS, 4 * HEAD, 4 * HEAD), F32), rim, rim)
     for turn in range(parts):
-        earlier, halves = [], []
-        for n, (first, pairs) in enumerate(CALLS):
-            after, through = [], []
-            if turn == parts - 1:
-                for _ in range(STEPS_BEFORE[n]):
-                    ffn.step()
-                through, after = ffn.arrays[:1], ffn.arrays[1:]
-                if first + pairs == PAIRS:
-                    after.append(output)
-            outs = run_attention_backward(
-                first, pairs, after, through, x, dx1, da, h, q, k, v, stats, states, sums,
-                segments, place, ga, dgf, w_query, w_key, w_value, earlier,
-                backs[n] + entry[2:] if parts > 1 else (),
-            )
-            if through:
-                ffn.arrays[0], *outs = outs
-            if first + pairs == PAIRS:
-                dx, *outs = outs
-            dq, dk, dv, keep, send, *ends = outs
-            earlier.append((dq, dk, dv))
-            halves.append((keep, send))
-            if turn < parts - 1:
-                backs[n] = shifted(tuple(ends), -1)
+        through, after = [], []
+        if turn == parts - 1:
+            through, after = ffn.arrays[:1], ffn.arrays[1:]
+        outs = run_attention_backward(
+            after, through, x, dx1, da, h, q, k, v, stats, states, sums,
+            segments, place, ga, dgf, w_query, w_key, w_value,
+            back + entry[2:] if parts > 1 else (),
+        )
+        if turn < parts - 1:
+            back = shifted(tuple(outs[3:]), -1)
+    ffn.arrays[0], dx, keep, send = outs[:4]
     d_tokens = trade(dx)
-    attention = Reduction(places, halves)
-    ff = w_up.shape[1]
-    own, other = ffn.finish()
-    dwd, dwu, dwo = run_finish(
-        core_ref, own, other, (False, True, False), ((ff, dim), (dim, ff), (dim, dim)), []
-    )
-    own, other = attention.finish()
-    dwq, dwk, dwv = run_finish(
-        core_ref, own, other, (False,) * 3, ((dim, dim),) * 3, [dwd, dwu, dwo]
+    attention = Reduction(places, [(keep, send), (keep_out, send_out)])
+    before = [output[0, :16, :128]]
+    for n, name in enumerate(TAIL):
+        reduction = ffn if name == "f" else attention
+        if name == "f" or n != TAIL.index("a"):
+            reduction.run(1)
+        reduction.hold(*before)
+        reduction.run(1)
+        before = reduction.arrays[-3:] if len(reduction.arrays) < 4 else reduction.arrays[1:]
+        if n == TRADED:
+            before = before + [d_tokens[0, :16, :128]]
+        if n == len(TAIL) - 2:
+            ffn.run(1)
+            dwd, dwu, finished = run_finish_ffn(core_ref, *ffn.arrays, dim)
+            before = [finished]
+    attention.run(1)
+    own, other = attention.arrays
+    half = dim // 2
+    dwq, dwk, dwv, dwo = run_finish(
+        core_ref, own, other, (0, half, 2 * half, 3 * half + GAIN_ROWS), (dim, dim)
     )
     at = 3 * dim // 2
-    gains = jnp.where(core == 0, own[at : at + 16], other[at : at + 16])
-    gains = gains[:, dim - 2 * HEAD * CALLS[-1][1] :].astype(F32).reshape(-1)
-    return output, d_tokens, gains[:dim], gains[dim : 2 * dim], dwq, dwk, dwv, dwo, dwu, dwd
+    gains = jnp.where(core == 0, own[at : at + 2], other[at : at + 2]).astype(F32)
+    return output, d_tokens, gains[0], gains[1], dwq, dwk, dwv, dwo, dwu, dwd
 
 
 def solution(mesh):

time: 274 us -> 242 us (0.88)
  waiting for transfers between devices: 76.7 us -> 64.1 us
  Pallas kernels: 93.5 us -> 83.4 us
  starting transfers between devices: 46.1 us -> 40.1 us
  other arithmetic: 13.3 us -> 9.36 us
    ppermute x29 -> x25, waiting for transfers between devices: 69.2 us -> 53.6 us  [partner(): return lax.ppermute(array, ('seq', 'rows'), pairs)]
    ppermute x29 -> x25, starting transfers between devices: 32.1 us -> 25.2 us  [partner(): return lax.ppermute(array, ('seq', 'rows'), pairs)]
    pallas_call x3 -> x16, Pallas kernels: 33 us -> 28.2 us  [the longest x1 20.6 us: run_ffn_backward(): pl.pallas_call(ffn_backward_kernel, grid=(ff // dim,), in_specs=[FFN_IN,...]
    pallas_call x2 -> x1, Pallas kernels: 34.1 us -> 29.5 us  [run_attention_backward(): pl.pallas_call(body, grid=(steps,), input_output_aliases={len(after) + n:...]
    all_to_all x3, waiting for transfers between devices: 7.49 us -> 10.6 us  [trade(): lax.all_to_all(array.reshape(row_count, shard_len, dim), 'seq', 0, 0, axi...]
    unnamed x34 -> x45, local copies, waits for them, and re-layouts: 5.5 us -> 7.54 us
  transfers between devices with their start and end apart: 32 -> 28, of which waited for: 11 -> 12; matrix products, arithmetic and copies ran while one was open for 6% -> 4% of each run, Pallas kernels for 22% -> 25%
where the time goes in v3:
time: 242 us; the launch traced here: 241 us
  Pallas kernels  83.4 us (34%)
  waiting for transfers between devices  64.1 us (26%)
  starting transfers between devices  40.1 us (17%)
  blocking collectives  33.3 us (14%)
  local copies, waits for them, and re-layouts  9.78 us (4%)
  other arithmetic  9.36 us (4%)
    ppermute x25, waiting for transfers between devices, partner(): return lax.ppermute(array, ('seq', 'rows'), pairs)  53.6 us
    all_to_all x1, blocking collectives, trade(): lax.all_to_all(array.reshape(row_count, shard_len, dim), 'seq', 0, 0, axi...  33.3 us
    pallas_call x1, Pallas kernels, run_attention_backward(): pl.pallas_call(body, grid=(steps,), input_output_aliases={len(after) + n:...  29.5 us
    pallas_call x1, Pallas kernels, run_forward(): pl.pallas_call(functools.partial(forward_kernel, len(entry)), grid=(lengt...  25.7 us
    ppermute x25, starting transfers between devices, partner(): return lax.ppermute(array, ('seq', 'rows'), pairs)  25.2 us
    pallas_call x1, Pallas kernels, run_ffn_backward(): pl.pallas_call(ffn_backward_kernel, grid=(ff // dim,), in_specs=[FFN_IN,...  20.6 us
    all_to_all x3, starting transfers between devices, trade(): lax.all_to_all(array.reshape(row_count, shard_len, dim), 'seq', 0, 0, axi...  14.9 us
    all_to_all x3, waiting for transfers between devices, trade(): lax.all_to_all(array.reshape(row_count, shard_len, dim), 'seq', 0, 0, axi...  10.6 us
  transfers between devices with their start and end apart: 28, of which 12 were waited for; matrix products, arithmetic and copies ran while one was open for 4% of the time, Pallas kernels for 25%

profile of v3, /device:TPU:0, one launch (start us, length us, event | category | flops | bytes accessed | tf_op | source)
XLA Modules:
  0.0 241.2 jit_solution(3244890677093550120)
XLA Ops:
  0.7 33.3 %all_to_all.20 = bf16[8,128,512]{2,1,0:T(8,128)(2,1)} all-to-all(bf16[8,128,512]{2,1,0:T(8,128)(2,1)} %param.11), channel_id=1, replica_groups={{0,4,8,12,16,20,24,28},{1,5,9,13,17,21,25,29},{2,6,10,14,18,22,26,30},{..., dimensions={0} | all-to-all | bytes 2097152 | tf_op jit(solution)/shard_map/all_to_all | solution.py:759
  34.0 3.6 %all-to-all-start.2 = ((bf16[8,128,512]{2,1,0:T(8,128)(2,1)}), bf16[8,128,512]{2,1,0:T(8,128)(2,1)S(1)}, u32[]{:S(2)}, u32[]{:S(2)}) async-start(bf16[8,128,512]{2,1,0:T(8,128)(2,1)} %param.21), calls=%async_computation.2 | async-start | bytes 2097152 | tf_op jit(solution)/shard_map/all_to_all | solution.py:759
  37.7 25.7 %layer_forward.1 = (bf16[1024,512]{1,0:T(8,128)(2,1)}, f32[1024,512]{1,0:T(8,128)}, bf16[1024,512]{1,0:T(8,128)(2,1)}, bf16[1024,512]{1,0:T(8,128)(2,1)}, bf16[1...) custom-call(bf16[1024,512]{1,0:T(8,128)(2,1)} %bitcast.48, ...), custom_call_target="tpu_custom_call" | custom-call | tf_op jit(solution)/shard_map/layer_forward/pallas_call | solution.py:471
  64.2 20.6 %ffn_backward.1 = (f32[1024,512]{1,0:T(8,128)}, bf16[1024,512]{1,0:T(8,128)(2,1)S(1)}, f32[8,512]{1,0:T(8,128)S(1)}, bf16[2048,512]{1,0:T(8,128)(2,1)}, bf16[204...) custom-call(bf16[1024,512]{1,0:T(8,128)(2,1)S(1)} %bitcast.43, ...), custom_call_target="tpu_custom_call" | custom-call | tf_op jit(solution)/shard_map/ffn_backward/pallas_call | solution.py:506
  85.4 6.0 %all-to-all-start.1 = ((bf16[8,128,512]{2,1,0:T(8,128)(2,1)}), bf16[8,128,512]{2,1,0:T(8,128)(2,1)S(1)}, u32[]{:S(2)}, u32[]{:S(2)}) async-start(bf16[8,128,512]{2,1,0:T(8,128)(2,1)} %bitcast.50), calls=%async_computation.1 | async-start | bytes 2097152 | tf_op jit(solution)/shard_map/all_to_all | solution.py:759
  91.6 2.8 %add_convert_fusion = bf16[2048,512]{1,0:T(8,128)(2,1)S(1)} fusion(bf16[2048,512]{1,0:T(8,128)(2,1)} %collective-permute-done, bf16[2048,512]{1,0:T(8,128)(2,1)} %get-tuple-element.41), kind=kLoop, calls=%fused_computation | loop fusion | flops 4194304 | bytes 6291456 | tf_op jit(solution)/shard_map/convert_element_type | solution.py:632
  99.1 29.5 %attention_backward.1 = (bf16[512,512]{1,0:T(8,128)(2,1)}, bf16[1024,512]{1,0:T(8,128)(2,1)}, bf16[832,512]{1,0:T(8,128)(2,1)}, bf16[832,512]{1,0:T(8,128)(2,1)}) custom-call(bf16[512,512]{1,0:T(8,128)(2,1)} %get-tuple-element.73.refs_0_, bf16[512,512]{1,0:T(8,128)(2,1)} %get-tuple-element.72.refs_1_, ...), custom_call_target="tpu_custom_call", output_to_operand_aliasing={{0}: (3, {})} | custom-call | tf_op jit(solution)/shard_map/attention_backward/pallas_call | solution.py:553
  137.0 4.8 %collective-permute-done.6 = bf16[256,512]{1,0:T(8,128)(2,1)S(1)} collective-permute-done((bf16[256,512]{1,0:T(8,128)(2,1)S(1)}, bf16[256,512]{1,0:T(8,128)(2,1)S(1)}, u32[]{:S(2)}, u32[]{:S(2)}) %collective-permute-start.6) | collective-permute-done | bytes 262176 | tf_op jit(solution)/shard_map/ppermute | solution.py:625
  141.9 2.7 %collective-permute-start.7 = (bf16[128,512]{1,0:T(8,128)(2,1)S(1)}, bf16[128,512]{1,0:T(8,128)(2,1)S(1)}, u32[]{:S(2)}, u32[]{:S(2)}) collective-permute-start(bf16[128,512]{1,0:T(8,128)(2,1)S(1)} %get-tuple-element.87.refs_2_), channel_id=1, source_target_pairs={{0,16},{1,17},{2,18},{3,19},{4,20},{5,21},{6,22},{7,23},{8,24},{9,... | collective-permute-start | bytes 393224 | tf_op jit(solution)/shard_map/ppermute | solution.py:625
  144.6 2.4 %collective-permute-start.10 = (bf16[272,512]{1,0:T(8,128)(2,1)S(1)}, bf16[272,512]{1,0:T(8,128)(2,1)S(1)}, u32[]{:S(2)}, u32[]{:S(2)}) collective-permute-start(bf16[272,512]{1,0:T(8,128)(2,1)S(1)} %get-tuple-element.81.refs_3_), channel_id=1, source_target_pairs={{0,6},{1,7},{2,4},{3,5},{4,2},{5,3},{6,0},{7,1},{8,14},{9,15},{10,... | collective-permute-start | bytes 835592 | tf_op jit(solution)/shard_map/ppermute | solution.py:625
  148.1 2.7 %collective-permute-done.7 = bf16[128,512]{1,0:T(8,128)(2,1)S(1)} collective-permute-done((bf16[128,512]{1,0:T(8,128)(2,1)S(1)}, bf16[128,512]{1,0:T(8,128)(2,1)S(1)}, u32[]{:S(2)}, u32[]{:S(2)}) %collective-permute-start.7) | collective-permute-done | bytes 131104 | tf_op jit(solution)/shard_map/ppermute | solution.py:625
  151.0 4.2 %collective-permute-done.10 = bf16[272,512]{1,0:T(8,128)(2,1)S(1)} collective-permute-done((bf16[272,512]{1,0:T(8,128)(2,1)S(1)}, bf16[272,512]{1,0:T(8,128)(2,1)S(1)}, u32[]{:S(2)}, u32[]{:S(2)}) %collective-permute-start.10) | collective-permute-done | bytes 278560 | tf_op jit(solution)/shard_map/ppermute | solution.py:625
  155.2 4.4 %collective-permute-done.8 = bf16[272,512]{1,0:T(8,128)(2,1)S(1)} collective-permute-done((bf16[272,512]{1,0:T(8,128)(2,1)S(1)}, bf16[272,512]{1,0:T(8,128)(2,1)S(1)}, u32[]{:S(2)}, u32[]{:S(2)}) %collective-permute-start.8) | collective-permute-done | bytes 278560 | tf_op jit(solution)/shard_map/ppermute | solution.py:625
  161.4 4.0 %collective-permute-done.12 = bf16[136,512]{1,0:T(8,128)(2,1)S(1)} collective-permute-done((bf16[136,512]{1,0:T(8,128)(2,1)S(1)}, bf16[136,512]{1,0:T(8,128)(2,1)S(1)}, u32[]{:S(2)}, u32[]{:S(2)}) %collective-permute-start.12) | collective-permute-done | bytes 139296 | tf_op jit(solution)/shard_map/ppermute | solution.py:625
  167.5 3.3 %collective-permute-done.13 = bf16[68,512]{1,0:T(8,128)(2,1)S(1)} collective-permute-done((bf16[68,512]{1,0:T(8,128)(2,1)S(1)}, bf16[68,512]{1,0:T(8,128)(2,1)S(1)}, u32[]{:S(2)}, u32[]{:S(2)}) %collective-permute-start.13) | collective-permute-done | bytes 69664 | tf_op jit(solution)/shard_map/ppermute | solution.py:625
  170.9 3.5 %collective-permute-done.14 = bf16[256,512]{1,0:T(8,128)(2,1)S(1)} collective-permute-done((bf16[256,512]{1,0:T(8,128)(2,1)S(1)}, bf16[256,512]{1,0:T(8,128)(2,1)S(1)}, u32[]{:S(2)}, u32[]{:S(2)}) %collective-permute-start.14) | collective-permute-done | bytes 262176 | tf_op jit(solution)/shard_map/ppermute | solution.py:625
  178.2 2.3 collective-permute-start.15
  180.5 3.9 %collective-permute-done.15 = bf16[68,512]{1,0:T(8,128)(2,1)S(1)} collective-permute-done((bf16[68,512]{1,0:T(8,128)(2,1)S(1)}, bf16[68,512]{1,0:T(8,128)(2,1)S(1)}, u32[]{:S(2)}, u32[]{:S(2)}) %collective-permute-start.15) | collective-permute-done | bytes 69664 | tf_op jit(solution)/shard_map/ppermute | solution.py:625
  184.6 4.9 %collective-permute-done.16 = bf16[136,512]{1,0:T(8,128)(2,1)S(1)} collective-permute-done((bf16[136,512]{1,0:T(8,128)(2,1)S(1)}, bf16[136,512]{1,0:T(8,128)(2,1)S(1)}, u32[]{:S(2)}, u32[]{:S(2)}) %collective-permute-start.16) | collective-permute-done | bytes 139296 | tf_op jit(solution)/shard_map/ppermute | solution.py:625
  189.6 10.2 %collective-permute-done.18 = bf16[512,512]{1,0:T(8,128)(2,1)S(1)} collective-permute-done((bf16[512,512]{1,0:T(8,128)(2,1)S(1)}, bf16[512,512]{1,0:T(8,128)(2,1)S(1)}, u32[]{:S(2)}, u32[]{:S(2)}) %collective-permute-start.18) | collective-permute-done | bytes 524320 | tf_op jit(solution)/shard_map/ppermute | solution.py:625
  204.1 5.3 %all-to-all-start.3 = ((bf16[8,128,512]{2,1,0:T(8,128)(2,1)}), bf16[8,128,512]{2,1,0:T(8,128)(2,1)}, u32[]{:S(2)}, u32[]{:S(2)}) async-start(bf16[8,128,512]{2,1,0:T(8,128)(2,1)} %bitcast.8), calls=%async_computation.3 | async-start | bytes 2097152 | tf_op jit(solution)/shard_map/all_to_all | solution.py:759
  209.4 5.4 %finish_ffn.1 = (f32[2048,512]{1,0:T(8,128)}, f32[512,2048]{1,0:T(8,128)}, f32[8,128]{1,0:T(8,128)S(1)}) custom-call(s32[1]{0:T(128)} %bitcast.3.core_ref, bf16[2048,512]{1,0:T(8,128)(2,1)S(1)} %pad_maximum_fusion.1.own_ref, bf16[2048,512]{1,0:T(8,128)(2,1)} %collective-permute-done.20.other_ref), custom_call_target="tpu_custom_call" | custom-call | tf_op jit(solution)/shard_map/finish_ffn/pallas_call | solution.py:588
  214.8 7.6 %collective-permute-done.23 = bf16[272,512]{1,0:T(8,128)(2,1)S(1)} collective-permute-done((bf16[272,512]{1,0:T(8,128)(2,1)S(1)}, bf16[272,512]{1,0:T(8,128)(2,1)S(1)}, u32[]{:S(2)}, u32[]{:S(2)}) %collective-permute-start.23) | collective-permute-done | bytes 278560 | tf_op jit(solution)/shard_map/ppermute | solution.py:625
  224.6 10.6 %all-to-all-done.3 = bf16[8,128,512]{2,1,0:T(8,128)(2,1)} async-done(((bf16[8,128,512]{2,1,0:T(8,128)(2,1)}), bf16[8,128,512]{2,1,0:T(8,128)(2,1)}, u32[]{:S(2)}, u32[]{:S(2)}) %all-to-all-start.3) | async-done | bytes 1048608 | tf_op jit(solution)/shard_map/all_to_all | solution.py:759
  (125 shorter events, 36.4 us)
Async XLA Ops:
  34.0 30.2 %all-to-all-start.2 = ((bf16[8,128,512]{2,1,0:T(8,128)(2,1)}), bf16[8,128,512]{2,1,0:T(8,128)(2,1)S(1)}, u32[]{:S(2)}, u32[]{:S(2)}) async-start(bf16[8,128,512]{2,1,0:T(8,128)(2,1)} %param.21), calls=%async_computation.2 | async-start | bytes 2097152 | tf_op jit(solution)/shard_map/all_to_all | solution.py:759
  85.4 6.2 %collective-permute-start = (bf16[2048,512]{1,0:T(8,128)(2,1)}, bf16[2048,512]{1,0:T(8,128)(2,1)}, u32[]{:S(2)}, u32[]{:S(2)}) collective-permute-start(bf16[2048,512]{1,0:T(8,128)(2,1)} %get-tuple-element.42), channel_id=1, source_target_pairs={{0,1},{1,0},{2,3},{3,2},{4,5},{5,4},{6,7},{7,6},{8,9},{9,8},{10,11... | collective-permute-start | bytes 6291464 | tf_op jit(solution)/shard_map/ppermute | solution.py:625
  85.4 43.4 %all-to-all-start.1 = ((bf16[8,128,512]{2,1,0:T(8,128)(2,1)}), bf16[8,128,512]{2,1,0:T(8,128)(2,1)S(1)}, u32[]{:S(2)}, u32[]{:S(2)}) async-start(bf16[8,128,512]{2,1,0:T(8,128)(2,1)} %bitcast.50), calls=%async_computation.1 | async-start | bytes 2097152 | tf_op jit(solution)/shard_map/all_to_all | solution.py:759
  91.4 37.3 %collective-permute-start.5 = (bf16[256,512]{1,0:T(8,128)(2,1)S(1)}, bf16[256,512]{1,0:T(8,128)(2,1)S(1)}, u32[]{:S(2)}, u32[]{:S(2)}) collective-permute-start(bf16[256,512]{1,0:T(8,128)(2,1)S(1)} %get-tuple-element.58), channel_id=1, source_target_pairs={{0,1},{1,0},{2,3},{3,2},{4,5},{5,4},{6,7},{7,6},{8,9},{9,8},{10,11... | collective-permute-start | bytes 786440 | tf_op jit(solution)/shard_map/ppermute | solution.py:625
  95.6 35.4 %collective-permute-start.1 = (bf16[512,512]{1,0:T(8,128)(2,1)}, bf16[512,512]{1,0:T(8,128)(2,1)}, u32[]{:S(2)}, u32[]{:S(2)}) collective-permute-start(bf16[512,512]{1,0:T(8,128)(2,1)} %get-tuple-element.73.refs_0_), channel_id=1, source_target_pairs={{0,4},{1,5},{2,6},{3,7},{4,0},{5,1},{6,2},{7,3},{8,12},{9,13},{10,... | collective-permute-start | bytes 1572872 | tf_op jit(solution)/shard_map/ppermute | solution.py:625
  97.4 33.6 %collective-permute-start.2 = (bf16[512,512]{1,0:T(8,128)(2,1)}, bf16[512,512]{1,0:T(8,128)(2,1)}, u32[]{:S(2)}, u32[]{:S(2)}) collective-permute-start(bf16[512,512]{1,0:T(8,128)(2,1)} %get-tuple-element.72.refs_1_), channel_id=1, source_target_pairs={{0,2},{1,3},{2,0},{3,1},{4,6},{5,7},{6,4},{7,5},{8,10},{9,11},{10,... | collective-permute-start | bytes 1572872 | tf_op jit(solution)/shard_map/ppermute | solution.py:625
  99.0 32.1 %collective-permute-start.3 = (bf16[512,512]{1,0:T(8,128)(2,1)S(1)}, bf16[512,512]{1,0:T(8,128)(2,1)}, u32[]{:S(2)}, u32[]{:S(2)}) collective-permute-start(bf16[512,512]{1,0:T(8,128)(2,1)S(1)} %get-tuple-element.71.refs_2_), channel_id=1, source_target_pairs={{0,6},{1,7},{2,4},{3,5},{4,2},{5,3},{6,0},{7,1},{8,14},{9,15},{10,... | collective-permute-start | bytes 1572872 | tf_op jit(solution)/shard_map/ppermute | solution.py:625
  128.6 6.2 %collective-permute-start.4 = (bf16[832,512]{1,0:T(8,128)(2,1)}, bf16[832,512]{1,0:T(8,128)(2,1)S(1)}, u32[]{:S(2)}, u32[]{:S(2)}) collective-permute-start(bf16[832,512]{1,0:T(8,128)(2,1)} %get-tuple-element.56), channel_id=1, source_target_pairs={{0,1},{1,0},{2,3},{3,2},{4,5},{5,4},{6,7},{7,6},{8,9},{9,8},{10,11... | collective-permute-start | bytes 2555912 | tf_op jit(solution)/shard_map/ppermute | solution.py:625
  133.0 8.8 %collective-permute-start.6 = (bf16[256,512]{1,0:T(8,128)(2,1)S(1)}, bf16[256,512]{1,0:T(8,128)(2,1)S(1)}, u32[]{:S(2)}, u32[]{:S(2)}) collective-permute-start(bf16[256,512]{1,0:T(8,128)(2,1)S(1)} %get-tuple-element.82.refs_2_), channel_id=1, source_target_pairs={{0,8},{1,9},{2,10},{3,11},{4,12},{5,13},{6,14},{7,15},{8,0},{9,1},... | collective-permute-start | bytes 786440 | tf_op jit(solution)/shard_map/ppermute | solution.py:625
  141.9 8.9 %collective-permute-start.7 = (bf16[128,512]{1,0:T(8,128)(2,1)S(1)}, bf16[128,512]{1,0:T(8,128)(2,1)S(1)}, u32[]{:S(2)}, u32[]{:S(2)}) collective-permute-start(bf16[128,512]{1,0:T(8,128)(2,1)S(1)} %get-tuple-element.87.refs_2_), channel_id=1, source_target_pairs={{0,16},{1,17},{2,18},{3,19},{4,20},{5,21},{6,22},{7,23},{8,24},{9,... | collective-permute-start | bytes 393224 | tf_op jit(solution)/shard_map/ppermute | solution.py:625
  144.6 10.5 %collective-permute-start.10 = (bf16[272,512]{1,0:T(8,128)(2,1)S(1)}, bf16[272,512]{1,0:T(8,128)(2,1)S(1)}, u32[]{:S(2)}, u32[]{:S(2)}) collective-permute-start(bf16[272,512]{1,0:T(8,128)(2,1)S(1)} %get-tuple-element.81.refs_3_), channel_id=1, source_target_pairs={{0,6},{1,7},{2,4},{3,5},{4,2},{5,3},{6,0},{7,1},{8,14},{9,15},{10,... | collective-permute-start | bytes 835592 | tf_op jit(solution)/shard_map/ppermute | solution.py:625
  147.1 12.5 %collective-permute-start.8 = (bf16[272,512]{1,0:T(8,128)(2,1)S(1)}, bf16[272,512]{1,0:T(8,128)(2,1)S(1)}, u32[]{:S(2)}, u32[]{:S(2)}) collective-permute-start(bf16[272,512]{1,0:T(8,128)(2,1)S(1)} %get-tuple-element.79.refs_1_), channel_id=1, source_target_pairs={{0,4},{1,5},{2,6},{3,7},{4,0},{5,1},{6,2},{7,3},{8,12},{9,13},{10,... | collective-permute-start | bytes 835592 | tf_op jit(solution)/shard_map/ppermute | solution.py:625
  147.6 12.0 %collective-permute-start.9 = (bf16[272,512]{1,0:T(8,128)(2,1)S(1)}, bf16[272,512]{1,0:T(8,128)(2,1)S(1)}, u32[]{:S(2)}, u32[]{:S(2)}) collective-permute-start(bf16[272,512]{1,0:T(8,128)(2,1)S(1)} %get-tuple-element.80.refs_2_), channel_id=1, source_target_pairs={{0,2},{1,3},{2,0},{3,1},{4,6},{5,7},{6,4},{7,5},{8,10},{9,11},{10,... | collective-permute-start | bytes 835592 | tf_op jit(solution)/shard_map/ppermute | solution.py:625
  150.9 10.4 %collective-permute-start.11 = (bf16[128,512]{1,0:T(8,128)(2,1)S(1)}, bf16[128,512]{1,0:T(8,128)(2,1)S(1)}, u32[]{:S(2)}, u32[]{:S(2)}) collective-permute-start(bf16[128,512]{1,0:T(8,128)(2,1)S(1)} %add_convert_fusion.7.refs_1_.refs_0_), channel_id=1, source_target_pairs={{0,16},{1,17},{2,18},{3,19},{4,20},{5,21},{6,22},{7,23},{8,24},{9,... | collective-permute-start | bytes 393224 | tf_op jit(solution)/shard_map/ppermute | solution.py:625
  165.9 8.6 %collective-permute-start.14 = (bf16[256,512]{1,0:T(8,128)(2,1)S(1)}, bf16[256,512]{1,0:T(8,128)(2,1)S(1)}, u32[]{:S(2)}, u32[]{:S(2)}) collective-permute-start(bf16[256,512]{1,0:T(8,128)(2,1)S(1)} %maximum_select_fusion.2.refs_1_.refs_0_), channel_id=1, source_target_pairs={{0,8},{1,9},{2,10},{3,11},{4,12},{5,13},{6,14},{7,15},{8,0},{9,1},... | collective-permute-start | bytes 786440 | tf_op jit(solution)/shard_map/ppermute | solution.py:625
  174.6 15.0 %collective-permute-start.17 = (bf16[512,512]{1,0:T(8,128)(2,1)S(1)}, bf16[512,512]{1,0:T(8,128)(2,1)S(1)}, u32[]{:S(2)}, u32[]{:S(2)}) collective-permute-start(bf16[512,512]{1,0:T(8,128)(2,1)S(1)} %maximum_select_fusion.refs_1_.refs_0_), channel_id=1, source_target_pairs={{0,4},{1,5},{2,6},{3,7},{4,0},{5,1},{6,2},{7,3},{8,12},{9,13},{10,... | collective-permute-start | bytes 1572872 | tf_op jit(solution)/shard_map/ppermute | solution.py:625
  176.4 23.4 %collective-permute-start.18 = (bf16[512,512]{1,0:T(8,128)(2,1)S(1)}, bf16[512,512]{1,0:T(8,128)(2,1)S(1)}, u32[]{:S(2)}, u32[]{:S(2)}) collective-permute-start(bf16[512,512]{1,0:T(8,128)(2,1)S(1)} %maximum_select_fusion.refs_1_.refs_0_), channel_id=1, source_target_pairs={{0,2},{1,3},{2,0},{3,1},{4,6},{5,7},{6,4},{7,5},{8,10},{9,11},{10,... | collective-permute-start | bytes 1572872 | tf_op jit(solution)/shard_map/ppermute | solution.py:625
  178.0 21.8 %collective-permute-start.19 = (bf16[512,512]{1,0:T(8,128)(2,1)S(1)}, bf16[512,512]{1,0:T(8,128)(2,1)S(1)}, u32[]{:S(2)}, u32[]{:S(2)}) collective-permute-start(bf16[512,512]{1,0:T(8,128)(2,1)S(1)} %maximum_select_fusion.refs_1_.refs_0_), channel_id=1, source_target_pairs={{0,6},{1,7},{2,4},{3,5},{4,2},{5,3},{6,0},{7,1},{8,14},{9,15},{10,... | collective-permute-start | bytes 1572872 | tf_op jit(solution)/shard_map/ppermute | solution.py:625
  200.4 9.0 %collective-permute-start.20 = (bf16[2048,512]{1,0:T(8,128)(2,1)S(1)}, bf16[2048,512]{1,0:T(8,128)(2,1)}, u32[]{:S(2)}, u32[]{:S(2)}) collective-permute-start(bf16[2048,512]{1,0:T(8,128)(2,1)S(1)} %pad_maximum_fusion.1.own_ref), channel_id=1, source_target_pairs={{0,1},{1,0},{2,3},{3,2},{4,5},{5,4},{6,7},{7,6},{8,9},{9,8},{10,11... | collective-permute-start | bytes 6291464 | tf_op jit(solution)/shard_map/ppermute | solution.py:625
  200.5 14.3 %collective-permute-start.21 = (bf16[272,512]{1,0:T(8,128)(2,1)S(1)}, bf16[272,512]{1,0:T(8,128)(2,1)S(1)}, u32[]{:S(2)}, u32[]{:S(2)}) collective-permute-start(bf16[272,512]{1,0:T(8,128)(2,1)S(1)} %maximum_select_fusion.1.refs_1_.refs_0_), channel_id=1, source_target_pairs={{0,4},{1,5},{2,6},{3,7},{4,0},{5,1},{6,2},{7,3},{8,12},{9,13},{10,... | collective-permute-start | bytes 835592 | tf_op jit(solution)/shard_map/ppermute | solution.py:625
  202.0 12.7 %collective-permute-start.22 = (bf16[272,512]{1,0:T(8,128)(2,1)S(1)}, bf16[272,512]{1,0:T(8,128)(2,1)S(1)}, u32[]{:S(2)}, u32[]{:S(2)}) collective-permute-start(bf16[272,512]{1,0:T(8,128)(2,1)S(1)} %maximum_select_fusion.1.refs_1_.refs_0_), channel_id=1, source_target_pairs={{0,2},{1,3},{2,0},{3,1},{4,6},{5,7},{6,4},{7,5},{8,10},{9,11},{10,... | collective-permute-start | bytes 835592 | tf_op jit(solution)/shard_map/ppermute | solution.py:625
  202.7 19.7 %collective-permute-start.23 = (bf16[272,512]{1,0:T(8,128)(2,1)S(1)}, bf16[272,512]{1,0:T(8,128)(2,1)S(1)}, u32[]{:S(2)}, u32[]{:S(2)}) collective-permute-start(bf16[272,512]{1,0:T(8,128)(2,1)S(1)} %maximum_select_fusion.1.refs_1_.refs_0_), channel_id=1, source_target_pairs={{0,6},{1,7},{2,4},{3,5},{4,2},{5,3},{6,0},{7,1},{8,14},{9,15},{10,... | collective-permute-start | bytes 835592 | tf_op jit(solution)/shard_map/ppermute | solution.py:625
  204.1 31.1 %all-to-all-start.3 = ((bf16[8,128,512]{2,1,0:T(8,128)(2,1)}), bf16[8,128,512]{2,1,0:T(8,128)(2,1)}, u32[]{:S(2)}, u32[]{:S(2)}) async-start(bf16[8,128,512]{2,1,0:T(8,128)(2,1)} %bitcast.8), calls=%async_computation.3 | async-start | bytes 2097152 | tf_op jit(solution)/shard_map/all_to_all | solution.py:759
  224.5 10.7 %collective-permute-start.24 = (bf16[1088,512]{1,0:T(8,128)(2,1)S(1)}, bf16[1088,512]{1,0:T(8,128)(2,1)S(1)}, u32[]{:S(2)}, u32[]{:S(2)}) collective-permute-start(bf16[1088,512]{1,0:T(8,128)(2,1)S(1)} %pad_maximum_fusion.3.own_ref), channel_id=1, source_target_pairs={{0,1},{1,0},{2,3},{3,2},{4,5},{5,4},{6,7},{7,6},{8,9},{9,8},{10,11... | collective-permute-start | bytes 3342344 | tf_op jit(solution)/shard_map/ppermute | solution.py:625
  (24 other events, 339.2 us)

commit v4 on v3

--- a/solution.py
+++ b/solution.py
@@ -18,9 +18,10 @@
 NEG = -1e30
 STEP_PAIRS = 2
 GAIN_ROWS = 64
-TAIL = "faffafaafaafa"
+TAIL = "duadudAuaduaaduaduDUa"
 GATE_KIB = 512
-TRADED = 11
+TRADE_AFTER = 13
+TRADED = 18
 FFN_ROWS = 2
 FORWARD_MIB, FFN_MIB, ATTENTION_MIB = 52, 50, 54
 GELU_A = 0.7978845608028654
@@ -573,24 +574,27 @@
     )(*after, *through, *streamed, *held)
 
 
-def finish_ffn_kernel(core_ref, own_ref, other_ref, down_ref, up_ref, done_ref):
-    half = down_ref.shape[0] // 2
+def finish_ffn_kernel(core_ref, own_ref, other_ref, out_ref, done_ref):
+    half = out_ref.shape[0] // 2
     for ref, which in ((own_ref, core_ref[0]), (other_ref, 1 - core_ref[0])):
         rows = pl.ds(pl.multiple_of(which * half, half), half)
-        down_ref[rows] = ref[:half].astype(F32)
-        up_ref[rows] = ref[half:].astype(F32)
+        out_ref[rows] = ref[...].astype(F32)
     done_ref[...] = jnp.zeros_like(done_ref)
 
 
-def run_finish_ffn(core_ref, own, other, dim):
-    ff = own.shape[0]
-    block = pl.BlockSpec((dim, dim), lambda i: (i, 0))
+def run_finish_ffn(core_ref, own, other, across):
+    dim = own.shape[1]
+    ff = own.shape[0] * 2
+    block = pl.BlockSpec((dim // 2, dim), lambda i: (i, 0))
     return pl.pallas_call(
         finish_ffn_kernel,
         grid=(ff // dim,),
         in_specs=[SMEM, block, block],
-        out_specs=[block, pl.BlockSpec((dim, dim), lambda i: (0, i)), whole((8, 128))],
-        out_shape=[sds((ff, dim), F32), sds((dim, ff), F32), sds((8, 128), F32)],
+        out_specs=[
+            pl.BlockSpec((dim, dim), (lambda i: (0, i)) if across else (lambda i: (i, 0))),
+            whole((8, 128)),
+        ],
+        out_shape=[sds((dim, ff) if across else (ff, dim), F32), sds((8, 128), F32)],
         compiler_params=params(12),
         name="finish_ffn",
     )(core_ref, own, other)
@@ -664,7 +668,7 @@
     return jnp.concatenate(blocks, 0)
 
 
-def all_reduce(places, halves):
+def sum_planes(places, halves):
     core, plane, depth = places
     others = [partner(send, 0, 1) for _, send in halves]
     keeps = yield [keep for keep, _ in halves]
@@ -672,8 +676,13 @@
     parts = yield cut(jnp.concatenate(sums, 0) if len(sums) > 1 else sums[0], plane)
     parts = traded(parts, PLANE_BITS)
     parts = yield parts
-    total = add(*parts)
-    for bits, bit in zip(DEPTH_BITS, depth):
+    yield [add(*parts)]
+
+
+def sum_depth_and_gather(places, total):
+    core, plane, depth = places
+    (total,) = yield [total]
+    for n, (bits, bit) in enumerate(zip(DEPTH_BITS, depth)):
         keep, send = yield cut_half(total, bit)
         other = partner(send, bits, 0)
         keep, other = yield [keep, other]
@@ -704,20 +713,40 @@
     )(array, *others)
 
 
+def settled(array):
+    def kernel(in_ref, out_ref, done_ref):
+        out_ref[...] = in_ref[...]
+        done_ref[...] = jnp.zeros_like(done_ref)
+
+    block = pl.BlockSpec((1,) + array.shape[1:], lambda i: (i, 0, 0))
+    return pl.pallas_call(
+        kernel,
+        grid=(array.shape[0],),
+        in_specs=[block],
+        out_specs=[block, whole((8, 128))],
+        out_shape=[sds(array.shape, array.dtype), sds((8, 128), F32)],
+        compiler_params=params(2),
+        name="settled",
+    )(array)
+
+
 class Reduction:
-    def __init__(self, *args):
-        self.steps = all_reduce(*args)
-        self.arrays = next(self.steps)
+    def __init__(self, steps):
+        self.steps = steps
+        self.arrays = next(steps)
+        self.waits = False
 
     def step(self):
         self.arrays = self.steps.send(self.arrays)
 
-    def run(self, count):
-        for _ in range(count):
+    def turn(self, before):
+        if self.waits:
             self.step()
-
-    def hold(self, *others):
-        self.arrays[0] = gate(self.arrays[0], *others)
+        if before:
+            self.arrays[0] = gate(self.arrays[0], *before)
+        self.step()
+        self.waits = True
+        return self.arrays[1:] or self.arrays
 
 
 def further_bits():
@@ -794,8 +823,8 @@
     dx1, da, dgf, keep, send, keep_out, send_out = run_ffn_backward(
         dy, x1, a, gf, w_out, w_up, w_down, core_ref
     )
-    ffn = Reduction(places, [(keep, send)])
-    ffn.run(1)
+    ffn = Reduction(sum_planes(places, [(keep, send)]))
+    ffn.step()
     back = ()
     if parts > 1:
         rim = jnp.zeros((dim, CHUNK), F32)
@@ -812,23 +841,41 @@
         if turn < parts - 1:
             back = shifted(tuple(outs[3:]), -1)
     ffn.arrays[0], dx, keep, send = outs[:4]
-    d_tokens = trade(dx)
-    attention = Reduction(places, [(keep, send), (keep_out, send_out)])
-    before = [output[0, :16, :128]]
+    attention = Reduction(sum_planes(places, [(keep, send), (keep_out, send_out)]))
+    output, arrived = settled(output)
+    ffn.step()
+    ffn.arrays[0] = gate(ffn.arrays[0], arrived)
+    ffn.step()
+    (total,) = ffn.arrays
+    middle = total.shape[0] // 2
+    sums = {
+        "d": Reduction(sum_depth_and_gather(places, total[:middle])),
+        "u": Reduction(sum_depth_and_gather(places, total[middle:])),
+    }
+    done = {}
+    before = []
     for n, name in enumerate(TAIL):
-        reduction = ffn if name == "f" else attention
-        if name == "f" or n != TAIL.index("a"):
-            reduction.run(1)
-        reduction.hold(*before)
-        reduction.run(1)
-        before = reduction.arrays[-3:] if len(reduction.arrays) < 4 else reduction.arrays[1:]
+        if name == "a" and "a" not in sums:
+            sums["a"] = attention
+            before = attention.turn(before)
+        elif name == "A":
+            attention.turn(before)
+            sums["a"] = attention = Reduction(sum_depth_and_gather(places, attention.arrays[0]))
+            before = attention.turn([])
+        elif name in "DU":
+            reduction = sums[name.lower()]
+            reduction.step()
+            done[name], finished = run_finish_ffn(core_ref, *reduction.arrays, name == "U")
+            before = before + [finished]
+        else:
+            before = sums[name].turn(before)
+        if n == TRADE_AFTER:
+            d_tokens = trade(gate(dx, *before))
         if n == TRADED:
-            before = before + [d_tokens[0, :16, :128]]
-        if n == len(TAIL) - 2:
-            ffn.run(1)
-            dwd, dwu, finished = run_finish_ffn(core_ref, *ffn.arrays, dim)
-            before = [finished]
-    attention.run(1)
+            d_tokens, arrived = settled(d_tokens)
+            before = before + [arrived]
+    attention.step()
+    dwd, dwu = done["D"], done["U"]
     own, other = attention.arrays
     half = dim // 2
     dwq, dwk, dwv, dwo = run_finish(

time: 242 us -> 233 us (0.963)
  waiting for transfers between devices: 64.1 us -> 37.6 us
  starting transfers between devices: 40.1 us -> 56.8 us
  Pallas kernels: 83.4 us -> 88.3 us
  local copies, waits for them, and re-layouts: 9.78 us -> 5.3 us
    ppermute x25 -> x33, starting transfers between devices: 25.2 us -> 43.6 us  [partner(): return lax.ppermute(array, ('seq', 'rows'), pairs)]
    ppermute x25 -> x33, waiting for transfers between devices: 53.6 us -> 37.5 us  [partner(): return lax.ppermute(array, ('seq', 'rows'), pairs)]
    all_to_all x3, waiting for transfers between devices: 10.6 us -> 0.01 us  [trade(): lax.all_to_all(array.reshape(row_count, shard_len, dim), 'seq', 0, 0, axi...]
    pallas_call x0 -> x2, Pallas kernels: none -> 5.43 us  [settled(): pl.pallas_call(kernel, grid=(array.shape[0],), in_specs=[block], out_spec...]
    unnamed x45 -> x37, local copies, waits for them, and re-layouts: 7.54 us -> 3.11 us
    pallas_call x1 -> x2, Pallas kernels: 5.35 us -> 4.85 us  [run_finish_ffn(): pl.pallas_call(finish_ffn_kernel, grid=(ff // dim,), in_specs=[SMEM, bloc...]
  transfers between devices with their start and end apart: 28 -> 36, of which waited for: 12 -> 12; matrix products, arithmetic and copies ran while one was open for 4% -> 4% of each run, Pallas kernels for 25% -> 28%
where the time goes in v4:
time: 233 us
  Pallas kernels  88.3 us (38%)
  starting transfers between devices  56.8 us (24%)
  waiting for transfers between devices  37.6 us (16%)
  blocking collectives  33.3 us (14%)
  other arithmetic  10.3 us (4%)
  local copies, waits for them, and re-layouts  5.3 us (2%)
    ppermute x33, starting transfers between devices, partner(): return lax.ppermute(array, ('seq', 'rows'), pairs)  43.6 us
    ppermute x33, waiting for transfers between devices, partner(): return lax.ppermute(array, ('seq', 'rows'), pairs)  37.5 us
    all_to_all x1, blocking collectives, trade(): lax.all_to_all(array.reshape(row_count, shard_len, dim), 'seq', 0, 0, axi...  33.3 us
    pallas_call x1, Pallas kernels, run_attention_backward(): pl.pallas_call(body, grid=(steps,), input_output_aliases={len(after) + n:...  29.5 us
    pallas_call x1, Pallas kernels, run_forward(): pl.pallas_call(functools.partial(forward_kernel, len(entry)), grid=(lengt...  25.7 us
    pallas_call x1, Pallas kernels, run_ffn_backward(): pl.pallas_call(ffn_backward_kernel, grid=(ff // dim,), in_specs=[FFN_IN,...  20.6 us
    all_to_all x3, starting transfers between devices, trade(): lax.all_to_all(array.reshape(row_count, shard_len, dim), 'seq', 0, 0, axi...  13.1 us
    pallas_call x2, Pallas kernels, settled(): pl.pallas_call(kernel, grid=(array.shape[0],), in_specs=[block], out_spec...  5.43 us
  transfers between devices with their start and end apart: 36, of which 12 were waited for; matrix products, arithmetic and copies ran while one was open for 4% of the time, Pallas kernels for 28%

profile of v4, /device:TPU:0, one launch (start us, length us, event | category | flops | bytes accessed | tf_op | source)
XLA Modules:
  0.0 232.6 jit_solution(10096297406644560279)
XLA Ops:
  0.7 33.3 %all_to_all.20 = bf16[8,128,512]{2,1,0:T(8,128)(2,1)} all-to-all(bf16[8,128,512]{2,1,0:T(8,128)(2,1)} %param.11), channel_id=1, replica_groups={{0,4,8,12,16,20,24,28},{1,5,9,13,17,21,25,29},{2,6,10,14,18,22,26,30},{..., dimensions={0} | all-to-all | bytes 2097152 | tf_op jit(solution)/shard_map/all_to_all | solution.py:788
  34.0 3.6 %all-to-all-start.2 = ((bf16[8,128,512]{2,1,0:T(8,128)(2,1)}), bf16[8,128,512]{2,1,0:T(8,128)(2,1)S(1)}, u32[]{:S(2)}, u32[]{:S(2)}) async-start(bf16[8,128,512]{2,1,0:T(8,128)(2,1)} %param.21), calls=%async_computation.2 | async-start | bytes 2097152 | tf_op jit(solution)/shard_map/all_to_all | solution.py:788
  37.7 25.7 %layer_forward.1 = (bf16[1024,512]{1,0:T(8,128)(2,1)}, f32[1024,512]{1,0:T(8,128)}, bf16[1024,512]{1,0:T(8,128)(2,1)}, bf16[1024,512]{1,0:T(8,128)(2,1)}, bf16[1...) custom-call(bf16[1024,512]{1,0:T(8,128)(2,1)} %bitcast.59, ...), custom_call_target="tpu_custom_call" | custom-call | tf_op jit(solution)/shard_map/layer_forward/pallas_call | solution.py:472
  64.1 20.6 %ffn_backward.1 = (f32[1024,512]{1,0:T(8,128)}, bf16[1024,512]{1,0:T(8,128)(2,1)S(1)}, f32[8,512]{1,0:T(8,128)S(1)}, bf16[2048,512]{1,0:T(8,128)(2,1)}, bf16[204...) custom-call(bf16[1024,512]{1,0:T(8,128)(2,1)S(1)} %bitcast.53, ...), custom_call_target="tpu_custom_call" | custom-call | tf_op jit(solution)/shard_map/ffn_backward/pallas_call | solution.py:507
  86.3 6.0 %all-to-all-start.1 = ((bf16[8,128,512]{2,1,0:T(8,128)(2,1)}), bf16[8,128,512]{2,1,0:T(8,128)(2,1)S(1)}, u32[]{:S(2)}, u32[]{:S(2)}) async-start(bf16[8,128,512]{2,1,0:T(8,128)(2,1)} %bitcast.6), calls=%async_computation.1 | async-start | bytes 2097152 | tf_op jit(solution)/shard_map/all_to_all | solution.py:788
  92.3 2.8 %add_convert_fusion = bf16[2048,512]{1,0:T(8,128)(2,1)S(1)} fusion(bf16[2048,512]{1,0:T(8,128)(2,1)} %collective-permute-done, bf16[2048,512]{1,0:T(8,128)(2,1)} %get-tuple-element.47), kind=kLoop, calls=%fused_computation | loop fusion | flops 4194304 | bytes 6291456 | tf_op jit(solution)/shard_map/convert_element_type | solution.py:636
  99.8 29.5 %attention_backward.1 = (bf16[512,512]{1,0:T(8,128)(2,1)}, bf16[1024,512]{1,0:T(8,128)(2,1)}, bf16[832,512]{1,0:T(8,128)(2,1)}, bf16[832,512]{1,0:T(8,128)(2,1)}) custom-call(bf16[512,512]{1,0:T(8,128)(2,1)} %get-tuple-element.79.refs_0_, bf16[512,512]{1,0:T(8,128)(2,1)} %copy-done.14, bf16[512,512]{1,0:T(8,128)(2,1)} %copy-done.13, ...), custom_call_target="tpu_custom_call", output_to_operand_aliasing={{0}: (3, {})} | custom-call | tf_op jit(solution)/shard_map/attention_backward/pallas_call | solution.py:554
  130.0 2.7 %settled.2 = (bf16[8,128,512]{2,1,0:T(8,128)(2,1)}, f32[8,128]{1,0:T(8,128)S(1)}) custom-call(bf16[8,128,512]{2,1,0:T(8,128)(2,1)S(1)} %all-to-all-done.1.in_ref), custom_call_target="tpu_custom_call" | custom-call | tf_op jit(solution)/shard_map/settled/pallas_call | solution.py:722
  143.6 2.9 %collective-permute-start.8 = (bf16[64,512]{1,0:T(8,128)(2,1)S(1)}, bf16[64,512]{1,0:T(8,128)(2,1)S(1)}, u32[]{:S(2)}, u32[]{:S(2)}) collective-permute-start(bf16[64,512]{1,0:T(8,128)(2,1)S(1)} %get-tuple-element.109.refs_1_), channel_id=1, source_target_pairs={{0,16},{1,17},{2,18},{3,19},{4,20},{5,21},{6,22},{7,23},{8,24},{9,... | collective-permute-start | bytes 196616 | tf_op jit(solution)/shard_map/ppermute | solution.py:629
  146.8 2.5 %collective-permute-done.8 = bf16[64,512]{1,0:T(8,128)(2,1)S(1)} collective-permute-done((bf16[64,512]{1,0:T(8,128)(2,1)S(1)}, bf16[64,512]{1,0:T(8,128)(2,1)S(1)}, u32[]{:S(2)}, u32[]{:S(2)}) %collective-permute-start.8) | collective-permute-done | bytes 65568 | tf_op jit(solution)/shard_map/ppermute | solution.py:629
  149.3 2.6 %collective-permute-start.14 = (bf16[64,512]{1,0:T(8,128)(2,1)S(1)}, bf16[64,512]{1,0:T(8,128)(2,1)S(1)}, u32[]{:S(2)}, u32[]{:S(2)}) collective-permute-start(bf16[64,512]{1,0:T(8,128)(2,1)S(1)} %add_convert_fusion.10.refs_1_.refs_0_), channel_id=1, source_target_pairs={{0,16},{1,17},{2,18},{3,19},{4,20},{5,21},{6,22},{7,23},{8,24},{9,... | collective-permute-start | bytes 196616 | tf_op jit(solution)/shard_map/ppermute | solution.py:629
  157.6 2.4 %collective-permute-start.15 = (bf16[64,512]{1,0:T(8,128)(2,1)S(1)}, bf16[64,512]{1,0:T(8,128)(2,1)S(1)}, u32[]{:S(2)}, u32[]{:S(2)}) collective-permute-start(bf16[64,512]{1,0:T(8,128)(2,1)S(1)} %add_convert_fusion.9.refs_1_.refs_0_), channel_id=1, source_target_pairs={{0,16},{1,17},{2,18},{3,19},{4,20},{5,21},{6,22},{7,23},{8,24},{9,... | collective-permute-start | bytes 196616 | tf_op jit(solution)/shard_map/ppermute | solution.py:629
  169.1 3.0 %collective-permute-start.18 = (bf16[128,512]{1,0:T(8,128)(2,1)S(1)}, bf16[128,512]{1,0:T(8,128)(2,1)S(1)}, u32[]{:S(2)}, u32[]{:S(2)}) collective-permute-start(bf16[128,512]{1,0:T(8,128)(2,1)S(1)} %maximum_select_fusion.4.refs_1_.refs_0_), channel_id=1, source_target_pairs={{0,8},{1,9},{2,10},{3,11},{4,12},{5,13},{6,14},{7,15},{8,0},{9,1},... | collective-permute-start | bytes 393224 | tf_op jit(solution)/shard_map/ppermute | solution.py:629
  172.3 2.8 %collective-permute-done.18 = bf16[128,512]{1,0:T(8,128)(2,1)S(1)} collective-permute-done((bf16[128,512]{1,0:T(8,128)(2,1)S(1)}, bf16[128,512]{1,0:T(8,128)(2,1)S(1)}, u32[]{:S(2)}, u32[]{:S(2)}) %collective-permute-start.18) | collective-permute-done | bytes 131104 | tf_op jit(solution)/shard_map/ppermute | solution.py:629
  182.4 3.6 %all-to-all-start.3 = ((bf16[8,128,512]{2,1,0:T(8,128)(2,1)}), bf16[8,128,512]{2,1,0:T(8,128)(2,1)S(1)}, u32[]{:S(2)}, u32[]{:S(2)}) async-start(bf16[8,128,512]{2,1,0:T(8,128)(2,1)} %bitcast.8), calls=%async_computation.3 | async-start | bytes 2097152 | tf_op jit(solution)/shard_map/all_to_all | solution.py:788
  187.7 3.4 %collective-permute-start.26 = (bf16[256,512]{1,0:T(8,128)(2,1)S(1)}, bf16[256,512]{1,0:T(8,128)(2,1)S(1)}, u32[]{:S(2)}, u32[]{:S(2)}) collective-permute-start(bf16[256,512]{1,0:T(8,128)(2,1)S(1)} %maximum_select_fusion.2.refs_1_.refs_0_), channel_id=1, source_target_pairs={{0,6},{1,7},{2,4},{3,5},{4,2},{5,3},{6,0},{7,1},{8,14},{9,15},{10,... | collective-permute-start | bytes 786440 | tf_op jit(solution)/shard_map/ppermute | solution.py:629
  191.1 6.1 %collective-permute-done.23 = bf16[256,512]{1,0:T(8,128)(2,1)S(1)} collective-permute-done((bf16[256,512]{1,0:T(8,128)(2,1)S(1)}, bf16[256,512]{1,0:T(8,128)(2,1)S(1)}, u32[]{:S(2)}, u32[]{:S(2)}) %collective-permute-start.23) | collective-permute-done | bytes 262176 | tf_op jit(solution)/shard_map/ppermute | solution.py:629
  197.5 5.5 %collective-permute-done.24 = bf16[256,512]{1,0:T(8,128)(2,1)S(1)} collective-permute-done((bf16[256,512]{1,0:T(8,128)(2,1)S(1)}, bf16[256,512]{1,0:T(8,128)(2,1)S(1)}, u32[]{:S(2)}, u32[]{:S(2)}) %collective-permute-start.24) | collective-permute-done | bytes 262176 | tf_op jit(solution)/shard_map/ppermute | solution.py:629
  203.0 5.2 %collective-permute-done.26 = bf16[256,512]{1,0:T(8,128)(2,1)S(1)} collective-permute-done((bf16[256,512]{1,0:T(8,128)(2,1)S(1)}, bf16[256,512]{1,0:T(8,128)(2,1)S(1)}, u32[]{:S(2)}, u32[]{:S(2)}) %collective-permute-start.26) | collective-permute-done | bytes 262176 | tf_op jit(solution)/shard_map/ppermute | solution.py:629
  212.5 2.4 %finish_ffn.3 = (f32[512,2048]{1,0:T(8,128)}, f32[8,128]{1,0:T(8,128)S(1)}) custom-call(s32[1]{0:T(128)} %bitcast.3.core_ref, bf16[1024,512]{1,0:T(8,128)(2,1)S(1)} %pad_maximum_fusion.5.own_ref.refs_1_, bf16[1024,512]{1,0:T(8,128)(2,1)S(1)} %collective-permute-done.28.other_ref), custom_call_target="tpu_custom_call" | custom-call | tf_op jit(solution)/shard_map/finish_ffn/pallas_call | solution.py:589
  215.0 2.4 %finish_ffn.2 = (f32[2048,512]{1,0:T(8,128)}, f32[8,128]{1,0:T(8,128)S(1)}) custom-call(s32[1]{0:T(128)} %bitcast.3.core_ref, bf16[1024,512]{1,0:T(8,128)(2,1)S(1)} %pad_maximum_fusion.3.refs_1_.own_ref, bf16[1024,512]{1,0:T(8,128)(2,1)S(1)} %collective-permute-done.27.other_ref), custom_call_target="tpu_custom_call" | custom-call | tf_op jit(solution)/shard_map/finish_ffn/pallas_call | solution.py:589
  217.4 2.7 %settled.3 = (bf16[8,128,512]{2,1,0:T(8,128)(2,1)}, f32[8,128]{1,0:T(8,128)S(1)}) custom-call(bf16[8,128,512]{2,1,0:T(8,128)(2,1)S(1)} %all-to-all-done.3.in_ref), custom_call_target="tpu_custom_call" | custom-call | tf_op jit(solution)/shard_map/settled/pallas_call | solution.py:722
  220.1 4.7 %collective-permute-done.30 = bf16[272,512]{1,0:T(8,128)(2,1)S(1)} collective-permute-done((bf16[272,512]{1,0:T(8,128)(2,1)S(1)}, bf16[272,512]{1,0:T(8,128)(2,1)S(1)}, u32[]{:S(2)}, u32[]{:S(2)}) %collective-permute-start.30) | collective-permute-done | bytes 278560 | tf_op jit(solution)/shard_map/ppermute | solution.py:629
  227.1 2.7 %collective-permute-done.32.other_ref = bf16[1088,512]{1,0:T(8,128)(2,1)S(1)} collective-permute-done((bf16[1088,512]{1,0:T(8,128)(2,1)S(1)}, bf16[1088,512]{1,0:T(8,128)(2,1)S(1)}, u32[]{:S(2)}, u32[]{:S(2)}) %collective-permute-start.32) | collective-permute-done | bytes 1114144 | tf_op jit(solution)/shard_map/ppermute | solution.py:629
  (152 shorter events, 52.2 us)
Async XLA Ops:
  34.0 30.1 %all-to-all-start.2 = ((bf16[8,128,512]{2,1,0:T(8,128)(2,1)}), bf16[8,128,512]{2,1,0:T(8,128)(2,1)S(1)}, u32[]{:S(2)}, u32[]{:S(2)}) async-start(bf16[8,128,512]{2,1,0:T(8,128)(2,1)} %param.21), calls=%async_computation.2 | async-start | bytes 2097152 | tf_op jit(solution)/shard_map/all_to_all | solution.py:788
  86.3 43.7 %all-to-all-start.1 = ((bf16[8,128,512]{2,1,0:T(8,128)(2,1)}), bf16[8,128,512]{2,1,0:T(8,128)(2,1)S(1)}, u32[]{:S(2)}, u32[]{:S(2)}) async-start(bf16[8,128,512]{2,1,0:T(8,128)(2,1)} %bitcast.6), calls=%async_computation.1 | async-start | bytes 2097152 | tf_op jit(solution)/shard_map/all_to_all | solution.py:788
  96.3 36.5 %collective-permute-start.1 = (bf16[512,512]{1,0:T(8,128)(2,1)}, bf16[512,512]{1,0:T(8,128)(2,1)}, u32[]{:S(2)}, u32[]{:S(2)}) collective-permute-start(bf16[512,512]{1,0:T(8,128)(2,1)} %get-tuple-element.79.refs_0_), channel_id=1, source_target_pairs={{0,4},{1,5},{2,6},{3,7},{4,0},{5,1},{6,2},{7,3},{8,12},{9,13},{10,... | collective-permute-start | bytes 1572872 | tf_op jit(solution)/shard_map/ppermute | solution.py:629
  98.3 34.5 %collective-permute-start.2 = (bf16[512,512]{1,0:T(8,128)(2,1)S(1)}, bf16[512,512]{1,0:T(8,128)(2,1)}, u32[]{:S(2)}, u32[]{:S(2)}) collective-permute-start(bf16[512,512]{1,0:T(8,128)(2,1)S(1)} %get-tuple-element.78.refs_1_), channel_id=1, source_target_pairs={{0,2},{1,3},{2,0},{3,1},{4,6},{5,7},{6,4},{7,5},{8,10},{9,11},{10,... | collective-permute-start | bytes 1572872 | tf_op jit(solution)/shard_map/ppermute | solution.py:629
  99.8 32.9 %collective-permute-start.3 = (bf16[512,512]{1,0:T(8,128)(2,1)S(1)}, bf16[512,512]{1,0:T(8,128)(2,1)}, u32[]{:S(2)}, u32[]{:S(2)}) collective-permute-start(bf16[512,512]{1,0:T(8,128)(2,1)S(1)} %get-tuple-element.77.refs_2_), channel_id=1, source_target_pairs={{0,6},{1,7},{2,4},{3,5},{4,2},{5,3},{6,0},{7,1},{8,14},{9,15},{10,... | collective-permute-start | bytes 1572872 | tf_op jit(solution)/shard_map/ppermute | solution.py:629
  99.8 30.1 %collective-permute-start.5 = (bf16[256,512]{1,0:T(8,128)(2,1)S(1)}, bf16[256,512]{1,0:T(8,128)(2,1)S(1)}, u32[]{:S(2)}, u32[]{:S(2)}) collective-permute-start(bf16[256,512]{1,0:T(8,128)(2,1)S(1)} %get-tuple-element.65), channel_id=1, source_target_pairs={{0,1},{1,0},{2,3},{3,2},{4,5},{5,4},{6,7},{7,6},{8,9},{9,8},{10,11... | collective-permute-start | bytes 786440 | tf_op jit(solution)/shard_map/ppermute | solution.py:629
  134.6 9.0 %collective-permute-start.6 = (bf16[128,512]{1,0:T(8,128)(2,1)S(1)}, bf16[128,512]{1,0:T(8,128)(2,1)S(1)}, u32[]{:S(2)}, u32[]{:S(2)}) collective-permute-start(bf16[128,512]{1,0:T(8,128)(2,1)S(1)} %get-tuple-element.103.refs_1_), channel_id=1, source_target_pairs={{0,8},{1,9},{2,10},{3,11},{4,12},{5,13},{6,14},{7,15},{8,0},{9,1},... | collective-permute-start | bytes 393224 | tf_op jit(solution)/shard_map/ppermute | solution.py:629
  136.6 10.0 %collective-permute-start.7 = (bf16[128,512]{1,0:T(8,128)(2,1)S(1)}, bf16[128,512]{1,0:T(8,128)(2,1)S(1)}, u32[]{:S(2)}, u32[]{:S(2)}) collective-permute-start(bf16[128,512]{1,0:T(8,128)(2,1)S(1)} %get-tuple-element.101.refs_1_), channel_id=1, source_target_pairs={{0,8},{1,9},{2,10},{3,11},{4,12},{5,13},{6,14},{7,15},{8,0},{9,1},... | collective-permute-start | bytes 393224 | tf_op jit(solution)/shard_map/ppermute | solution.py:629
  140.0 14.3 %collective-permute-start.10 = (bf16[272,512]{1,0:T(8,128)(2,1)S(1)}, bf16[272,512]{1,0:T(8,128)(2,1)S(1)}, u32[]{:S(2)}, u32[]{:S(2)}) collective-permute-start(bf16[272,512]{1,0:T(8,128)(2,1)S(1)} %get-tuple-element.86.refs_2_), channel_id=1, source_target_pairs={{0,2},{1,3},{2,0},{3,1},{4,6},{5,7},{6,4},{7,5},{8,10},{9,11},{10,... | collective-permute-start | bytes 835592 | tf_op jit(solution)/shard_map/ppermute | solution.py:629
  141.6 12.7 %collective-permute-start.11 = (bf16[272,512]{1,0:T(8,128)(2,1)S(1)}, bf16[272,512]{1,0:T(8,128)(2,1)S(1)}, u32[]{:S(2)}, u32[]{:S(2)}) collective-permute-start(bf16[272,512]{1,0:T(8,128)(2,1)S(1)} %get-tuple-element.87.refs_3_), channel_id=1, source_target_pairs={{0,6},{1,7},{2,4},{3,5},{4,2},{5,3},{6,0},{7,1},{8,14},{9,15},{10,... | collective-permute-start | bytes 835592 | tf_op jit(solution)/shard_map/ppermute | solution.py:629
  143.5 12.1 %collective-permute-start.9 = (bf16[272,512]{1,0:T(8,128)(2,1)S(1)}, bf16[272,512]{1,0:T(8,128)(2,1)S(1)}, u32[]{:S(2)}, u32[]{:S(2)}) collective-permute-start(bf16[272,512]{1,0:T(8,128)(2,1)S(1)} %get-tuple-element.85.refs_1_), channel_id=1, source_target_pairs={{0,4},{1,5},{2,6},{3,7},{4,0},{5,1},{6,2},{7,3},{8,12},{9,13},{10,... | collective-permute-start | bytes 835592 | tf_op jit(solution)/shard_map/ppermute | solution.py:629
  146.6 10.9 %collective-permute-start.12 = (bf16[64,512]{1,0:T(8,128)(2,1)S(1)}, bf16[64,512]{1,0:T(8,128)(2,1)S(1)}, u32[]{:S(2)}, u32[]{:S(2)}) collective-permute-start(bf16[64,512]{1,0:T(8,128)(2,1)S(1)} %get-tuple-element.107.refs_1_), channel_id=1, source_target_pairs={{0,16},{1,17},{2,18},{3,19},{4,20},{5,21},{6,22},{7,23},{8,24},{9,... | collective-permute-start | bytes 196616 | tf_op jit(solution)/shard_map/ppermute | solution.py:629
  149.3 14.4 %collective-permute-start.14 = (bf16[64,512]{1,0:T(8,128)(2,1)S(1)}, bf16[64,512]{1,0:T(8,128)(2,1)S(1)}, u32[]{:S(2)}, u32[]{:S(2)}) collective-permute-start(bf16[64,512]{1,0:T(8,128)(2,1)S(1)} %add_convert_fusion.10.refs_1_.refs_0_), channel_id=1, source_target_pairs={{0,16},{1,17},{2,18},{3,19},{4,20},{5,21},{6,22},{7,23},{8,24},{9,... | collective-permute-start | bytes 196616 | tf_op jit(solution)/shard_map/ppermute | solution.py:629
  172.2 8.7 %collective-permute-start.19 = (bf16[128,512]{1,0:T(8,128)(2,1)S(1)}, bf16[128,512]{1,0:T(8,128)(2,1)S(1)}, u32[]{:S(2)}, u32[]{:S(2)}) collective-permute-start(bf16[128,512]{1,0:T(8,128)(2,1)S(1)} %maximum_select_fusion.5.refs_1_.refs_0_), channel_id=1, source_target_pairs={{0,8},{1,9},{2,10},{3,11},{4,12},{5,13},{6,14},{7,15},{8,0},{9,1},... | collective-permute-start | bytes 393224 | tf_op jit(solution)/shard_map/ppermute | solution.py:629
  175.2 12.5 %collective-permute-start.21 = (bf16[256,512]{1,0:T(8,128)(2,1)S(1)}, bf16[256,512]{1,0:T(8,128)(2,1)S(1)}, u32[]{:S(2)}, u32[]{:S(2)}) collective-permute-start(bf16[256,512]{1,0:T(8,128)(2,1)S(1)} %maximum_select_fusion.1.refs_1_.refs_0_), channel_id=1, source_target_pairs={{0,4},{1,5},{2,6},{3,7},{4,0},{5,1},{6,2},{7,3},{8,12},{9,13},{10,... | collective-permute-start | bytes 786440 | tf_op jit(solution)/shard_map/ppermute | solution.py:629
  176.7 14.4 %collective-permute-start.22 = (bf16[256,512]{1,0:T(8,128)(2,1)S(1)}, bf16[256,512]{1,0:T(8,128)(2,1)S(1)}, u32[]{:S(2)}, u32[]{:S(2)}) collective-permute-start(bf16[256,512]{1,0:T(8,128)(2,1)S(1)} %maximum_select_fusion.1.refs_1_.refs_0_), channel_id=1, source_target_pairs={{0,2},{1,3},{2,0},{3,1},{4,6},{5,7},{6,4},{7,5},{8,10},{9,11},{10,... | collective-permute-start | bytes 786440 | tf_op jit(solution)/shard_map/ppermute | solution.py:629
  178.2 19.0 %collective-permute-start.23 = (bf16[256,512]{1,0:T(8,128)(2,1)S(1)}, bf16[256,512]{1,0:T(8,128)(2,1)S(1)}, u32[]{:S(2)}, u32[]{:S(2)}) collective-permute-start(bf16[256,512]{1,0:T(8,128)(2,1)S(1)} %maximum_select_fusion.1.refs_1_.refs_0_), channel_id=1, source_target_pairs={{0,6},{1,7},{2,4},{3,5},{4,2},{5,3},{6,0},{7,1},{8,14},{9,15},{10,... | collective-permute-start | bytes 786440 | tf_op jit(solution)/shard_map/ppermute | solution.py:629
  180.9 22.1 %collective-permute-start.24 = (bf16[256,512]{1,0:T(8,128)(2,1)S(1)}, bf16[256,512]{1,0:T(8,128)(2,1)S(1)}, u32[]{:S(2)}, u32[]{:S(2)}) collective-permute-start(bf16[256,512]{1,0:T(8,128)(2,1)S(1)} %maximum_select_fusion.2.refs_1_.refs_0_), channel_id=1, source_target_pairs={{0,4},{1,5},{2,6},{3,7},{4,0},{5,1},{6,2},{7,3},{8,12},{9,13},{10,... | collective-permute-start | bytes 786440 | tf_op jit(solution)/shard_map/ppermute | solution.py:629
  182.4 35.0 %all-to-all-start.3 = ((bf16[8,128,512]{2,1,0:T(8,128)(2,1)}), bf16[8,128,512]{2,1,0:T(8,128)(2,1)S(1)}, u32[]{:S(2)}, u32[]{:S(2)}) async-start(bf16[8,128,512]{2,1,0:T(8,128)(2,1)} %bitcast.8), calls=%async_computation.3 | async-start | bytes 2097152 | tf_op jit(solution)/shard_map/all_to_all | solution.py:788
  186.0 17.0 %collective-permute-start.25 = (bf16[256,512]{1,0:T(8,128)(2,1)S(1)}, bf16[256,512]{1,0:T(8,128)(2,1)S(1)}, u32[]{:S(2)}, u32[]{:S(2)}) collective-permute-start(bf16[256,512]{1,0:T(8,128)(2,1)S(1)} %maximum_select_fusion.2.refs_1_.refs_0_), channel_id=1, source_target_pairs={{0,2},{1,3},{2,0},{3,1},{4,6},{5,7},{6,4},{7,5},{8,10},{9,11},{10,... | collective-permute-start | bytes 786440 | tf_op jit(solution)/shard_map/ppermute | solution.py:629
  187.7 20.5 %collective-permute-start.26 = (bf16[256,512]{1,0:T(8,128)(2,1)S(1)}, bf16[256,512]{1,0:T(8,128)(2,1)S(1)}, u32[]{:S(2)}, u32[]{:S(2)}) collective-permute-start(bf16[256,512]{1,0:T(8,128)(2,1)S(1)} %maximum_select_fusion.2.refs_1_.refs_0_), channel_id=1, source_target_pairs={{0,6},{1,7},{2,4},{3,5},{4,2},{5,3},{6,0},{7,1},{8,14},{9,15},{10,... | collective-permute-start | bytes 786440 | tf_op jit(solution)/shard_map/ppermute | solution.py:629
  209.0 11.1 %collective-permute-start.29 = (bf16[272,512]{1,0:T(8,128)(2,1)S(1)}, bf16[272,512]{1,0:T(8,128)(2,1)S(1)}, u32[]{:S(2)}, u32[]{:S(2)}) collective-permute-start(bf16[272,512]{1,0:T(8,128)(2,1)S(1)} %maximum_select_fusion.refs_1_.refs_0_), channel_id=1, source_target_pairs={{0,4},{1,5},{2,6},{3,7},{4,0},{5,1},{6,2},{7,3},{8,12},{9,13},{10,... | collective-permute-start | bytes 835592 | tf_op jit(solution)/shard_map/ppermute | solution.py:629
  210.4 14.3 %collective-permute-start.30 = (bf16[272,512]{1,0:T(8,128)(2,1)S(1)}, bf16[272,512]{1,0:T(8,128)(2,1)S(1)}, u32[]{:S(2)}, u32[]{:S(2)}) collective-permute-start(bf16[272,512]{1,0:T(8,128)(2,1)S(1)} %maximum_select_fusion.refs_1_.refs_0_), channel_id=1, source_target_pairs={{0,2},{1,3},{2,0},{3,1},{4,6},{5,7},{6,4},{7,5},{8,10},{9,11},{10,... | collective-permute-start | bytes 835592 | tf_op jit(solution)/shard_map/ppermute | solution.py:629
  211.0 13.8 %collective-permute-start.31 = (bf16[272,512]{1,0:T(8,128)(2,1)S(1)}, bf16[272,512]{1,0:T(8,128)(2,1)S(1)}, u32[]{:S(2)}, u32[]{:S(2)}) collective-permute-start(bf16[272,512]{1,0:T(8,128)(2,1)S(1)} %maximum_select_fusion.refs_1_.refs_0_), channel_id=1, source_target_pairs={{0,6},{1,7},{2,4},{3,5},{4,2},{5,3},{6,0},{7,1},{8,14},{9,15},{10,... | collective-permute-start | bytes 835592 | tf_op jit(solution)/shard_map/ppermute | solution.py:629
  (30 other events, 366.4 us)

commit v5 on v4

--- a/solution.py
+++ b/solution.py
@@ -20,10 +20,13 @@
 GAIN_ROWS = 64
 TAIL = "duadudAuaduaaduaduDUa"
 GATE_KIB = 512
-TRADE_AFTER = 13
+SETTLE = 12
+TRADE_AFTER = 12
 TRADED = 18
 FFN_ROWS = 2
-FORWARD_MIB, FFN_MIB, ATTENTION_MIB = 52, 50, 54
+FORWARD_MIB = 52
+FFN_MIB = 50
+ATTENTION_MIB = 54
 GELU_A = 0.7978845608028654
 GELU_B = 0.044715
 F32 = jnp.float32
@@ -701,14 +704,14 @@
     yield [own, partner(own, 0, 1)]
 
 
-def gate(array, *others):
+def gate(array, *others, mib=None):
     return pl.pallas_call(
         lambda *refs: None,
         in_specs=[ANY] * (1 + len(others)),
         out_specs=ANY,
         out_shape=sds(array.shape, array.dtype),
         input_output_aliases={0: 0},
-        compiler_params=pltpu.CompilerParams(vmem_limit_bytes=GATE_KIB * 1024),
+        compiler_params=pltpu.CompilerParams(vmem_limit_bytes=mib * 2**20 if mib else GATE_KIB * 1024),
         name="gate",
     )(array, *others)
 
@@ -842,9 +845,8 @@
             back = shifted(tuple(outs[3:]), -1)
     ffn.arrays[0], dx, keep, send = outs[:4]
     attention = Reduction(sum_planes(places, [(keep, send), (keep_out, send_out)]))
-    output, arrived = settled(output)
     ffn.step()
-    ffn.arrays[0] = gate(ffn.arrays[0], arrived)
+    ffn.arrays[0] = gate(ffn.arrays[0], output, mib=FFN_MIB)
     ffn.step()
     (total,) = ffn.arrays
     middle = total.shape[0] // 2
@@ -869,6 +871,9 @@
             before = before + [finished]
         else:
             before = sums[name].turn(before)
+        if n == SETTLE:
+            output, arrived = settled(output)
+            before = before + [arrived]
         if n == TRADE_AFTER:
             d_tokens = trade(gate(dx, *before))
         if n == TRADED:

time: 233 us -> 231 us (level)
  no operation moved by 1% of the time
where the time goes in v5:
time: 231 us
  Pallas kernels  88.3 us (38%)
  starting transfers between devices  55.4 us (24%)
  waiting for transfers between devices  36.3 us (16%)
  blocking collectives  33.3 us (14%)
  other arithmetic  10.2 us (4%)
  local copies, waits for them, and re-layouts  6.14 us (3%)
    ppermute x33, starting transfers between devices, partner(): return lax.ppermute(array, ('seq', 'rows'), pairs)  42.2 us
    ppermute x33, waiting for transfers between devices, partner(): return lax.ppermute(array, ('seq', 'rows'), pairs)  36.3 us
    all_to_all x1, blocking collectives, trade(): lax.all_to_all(array.reshape(row_count, shard_len, dim), 'seq', 0, 0, axi...  33.3 us
    pallas_call x1, Pallas kernels, run_attention_backward(): pl.pallas_call(body, grid=(steps,), input_output_aliases={len(after) + n:...  29.5 us
    pallas_call x1, Pallas kernels, run_forward(): pl.pallas_call(functools.partial(forward_kernel, len(entry)), grid=(lengt...  25.7 us
    pallas_call x1, Pallas kernels, run_ffn_backward(): pl.pallas_call(ffn_backward_kernel, grid=(ff // dim,), in_specs=[FFN_IN,...  20.6 us
    all_to_all x3, starting transfers between devices, trade(): lax.all_to_all(array.reshape(row_count, shard_len, dim), 'seq', 0, 0, axi...  13.1 us
    pallas_call x2, Pallas kernels, settled(): pl.pallas_call(kernel, grid=(array.shape[0],), in_specs=[block], out_spec...  5.4 us
  transfers between devices with their start and end apart: 36, of which 12 were waited for; matrix products, arithmetic and copies ran while one was open for 4% of the time, Pallas kernels for 28%

profile of v5, /device:TPU:0, one launch (start us, length us, event | category | flops | bytes accessed | tf_op | source)
XLA Modules:
  0.0 230.7 jit_solution(10230512297349255789)
XLA Ops:
  0.7 33.3 %all_to_all.20 = bf16[8,128,512]{2,1,0:T(8,128)(2,1)} all-to-all(bf16[8,128,512]{2,1,0:T(8,128)(2,1)} %param.11), channel_id=1, replica_groups={{0,4,8,12,16,20,24,28},{1,5,9,13,17,21,25,29},{2,6,10,14,18,22,26,30},{..., dimensions={0} | all-to-all | bytes 2097152 | tf_op jit(solution)/shard_map/all_to_all | solution.py:791
  34.0 3.6 %all-to-all-start.2 = ((bf16[8,128,512]{2,1,0:T(8,128)(2,1)}), bf16[8,128,512]{2,1,0:T(8,128)(2,1)S(1)}, u32[]{:S(2)}, u32[]{:S(2)}) async-start(bf16[8,128,512]{2,1,0:T(8,128)(2,1)} %param.21), calls=%async_computation.2 | async-start | bytes 2097152 | tf_op jit(solution)/shard_map/all_to_all | solution.py:791
  37.7 25.7 %layer_forward.1 = (bf16[1024,512]{1,0:T(8,128)(2,1)}, f32[1024,512]{1,0:T(8,128)}, bf16[1024,512]{1,0:T(8,128)(2,1)}, bf16[1024,512]{1,0:T(8,128)(2,1)}, bf16[1...) custom-call(bf16[1024,512]{1,0:T(8,128)(2,1)} %bitcast.59, ...), custom_call_target="tpu_custom_call" | custom-call | tf_op jit(solution)/shard_map/layer_forward/pallas_call | solution.py:475
  64.1 20.6 %ffn_backward.1 = (f32[1024,512]{1,0:T(8,128)}, bf16[1024,512]{1,0:T(8,128)(2,1)S(1)}, f32[8,512]{1,0:T(8,128)S(1)}, bf16[2048,512]{1,0:T(8,128)(2,1)}, bf16[204...) custom-call(bf16[1024,512]{1,0:T(8,128)(2,1)S(1)} %bitcast.52, ...), custom_call_target="tpu_custom_call" | custom-call | tf_op jit(solution)/shard_map/ffn_backward/pallas_call | solution.py:510
  86.3 6.0 %all-to-all-start.1 = ((bf16[8,128,512]{2,1,0:T(8,128)(2,1)}), bf16[8,128,512]{2,1,0:T(8,128)(2,1)S(1)}, u32[]{:S(2)}, u32[]{:S(2)}) async-start(bf16[8,128,512]{2,1,0:T(8,128)(2,1)} %bitcast.6), calls=%async_computation.1 | async-start | bytes 2097152 | tf_op jit(solution)/shard_map/all_to_all | solution.py:791
  92.3 2.8 %add_convert_fusion = bf16[2048,512]{1,0:T(8,128)(2,1)S(1)} fusion(bf16[2048,512]{1,0:T(8,128)(2,1)} %collective-permute-done, bf16[2048,512]{1,0:T(8,128)(2,1)} %get-tuple-element.47), kind=kLoop, calls=%fused_computation | loop fusion | flops 4194304 | bytes 6291456 | tf_op jit(solution)/shard_map/convert_element_type | solution.py:639
  99.7 29.5 %attention_backward.1 = (bf16[512,512]{1,0:T(8,128)(2,1)}, bf16[1024,512]{1,0:T(8,128)(2,1)}, bf16[832,512]{1,0:T(8,128)(2,1)}, bf16[832,512]{1,0:T(8,128)(2,1)}) custom-call(bf16[512,512]{1,0:T(8,128)(2,1)} %copy-done.15, bf16[512,512]{1,0:T(8,128)(2,1)} %copy-done.14, bf16[512,512]{1,0:T(8,128)(2,1)} %copy-done.13, ...), custom_call_target="tpu_custom_call", output_to_operand_aliasing={{0}: (3, {})} | custom-call | tf_op jit(solution)/shard_map/attention_backward/pallas_call | solution.py:557
  141.7 2.9 %collective-permute-start.8 = (bf16[64,512]{1,0:T(8,128)(2,1)S(1)}, bf16[64,512]{1,0:T(8,128)(2,1)S(1)}, u32[]{:S(2)}, u32[]{:S(2)}) collective-permute-start(bf16[64,512]{1,0:T(8,128)(2,1)S(1)} %get-tuple-element.109.refs_1_), channel_id=1, source_target_pairs={{0,16},{1,17},{2,18},{3,19},{4,20},{5,21},{6,22},{7,23},{8,24},{9,... | collective-permute-start | bytes 196616 | tf_op jit(solution)/shard_map/ppermute | solution.py:632
  144.9 2.5 %collective-permute-done.8 = bf16[64,512]{1,0:T(8,128)(2,1)S(1)} collective-permute-done((bf16[64,512]{1,0:T(8,128)(2,1)S(1)}, bf16[64,512]{1,0:T(8,128)(2,1)S(1)}, u32[]{:S(2)}, u32[]{:S(2)}) %collective-permute-start.8) | collective-permute-done | bytes 65568 | tf_op jit(solution)/shard_map/ppermute | solution.py:632
  147.4 2.6 %collective-permute-start.14 = (bf16[64,512]{1,0:T(8,128)(2,1)S(1)}, bf16[64,512]{1,0:T(8,128)(2,1)S(1)}, u32[]{:S(2)}, u32[]{:S(2)}) collective-permute-start(bf16[64,512]{1,0:T(8,128)(2,1)S(1)} %add_convert_fusion.10.refs_1_.refs_0_), channel_id=1, source_target_pairs={{0,16},{1,17},{2,18},{3,19},{4,20},{5,21},{6,22},{7,23},{8,24},{9,... | collective-permute-start | bytes 196616 | tf_op jit(solution)/shard_map/ppermute | solution.py:632
  150.0 2.4 %collective-permute-done.10 = bf16[272,512]{1,0:T(8,128)(2,1)S(1)} collective-permute-done((bf16[272,512]{1,0:T(8,128)(2,1)S(1)}, bf16[272,512]{1,0:T(8,128)(2,1)S(1)}, u32[]{:S(2)}, u32[]{:S(2)}) %collective-permute-start.10) | collective-permute-done | bytes 278560 | tf_op jit(solution)/shard_map/ppermute | solution.py:632
  155.6 2.4 %collective-permute-start.15 = (bf16[64,512]{1,0:T(8,128)(2,1)S(1)}, bf16[64,512]{1,0:T(8,128)(2,1)S(1)}, u32[]{:S(2)}, u32[]{:S(2)}) collective-permute-start(bf16[64,512]{1,0:T(8,128)(2,1)S(1)} %add_convert_fusion.9.refs_1_.refs_0_), channel_id=1, source_target_pairs={{0,16},{1,17},{2,18},{3,19},{4,20},{5,21},{6,22},{7,23},{8,24},{9,... | collective-permute-start | bytes 196616 | tf_op jit(solution)/shard_map/ppermute | solution.py:632
  167.1 3.1 %collective-permute-start.18 = (bf16[128,512]{1,0:T(8,128)(2,1)S(1)}, bf16[128,512]{1,0:T(8,128)(2,1)S(1)}, u32[]{:S(2)}, u32[]{:S(2)}) collective-permute-start(bf16[128,512]{1,0:T(8,128)(2,1)S(1)} %maximum_select_fusion.4.refs_1_.refs_0_), channel_id=1, source_target_pairs={{0,8},{1,9},{2,10},{3,11},{4,12},{5,13},{6,14},{7,15},{8,0},{9,1},... | collective-permute-start | bytes 393224 | tf_op jit(solution)/shard_map/ppermute | solution.py:632
  170.2 2.7 %settled.2 = (bf16[8,128,512]{2,1,0:T(8,128)(2,1)}, f32[8,128]{1,0:T(8,128)S(1)}) custom-call(bf16[8,128,512]{2,1,0:T(8,128)(2,1)S(1)} %all-to-all-done.1.in_ref.refs_1_), custom_call_target="tpu_custom_call" | custom-call | tf_op jit(solution)/shard_map/settled/pallas_call | solution.py:725
  180.4 3.6 %all-to-all-start.3 = ((bf16[8,128,512]{2,1,0:T(8,128)(2,1)}), bf16[8,128,512]{2,1,0:T(8,128)(2,1)S(1)}, u32[]{:S(2)}, u32[]{:S(2)}) async-start(bf16[8,128,512]{2,1,0:T(8,128)(2,1)} %bitcast.8), calls=%async_computation.3 | async-start | bytes 2097152 | tf_op jit(solution)/shard_map/all_to_all | solution.py:791
  185.7 2.7 %collective-permute-start.26 = (bf16[256,512]{1,0:T(8,128)(2,1)S(1)}, bf16[256,512]{1,0:T(8,128)(2,1)S(1)}, u32[]{:S(2)}, u32[]{:S(2)}) collective-permute-start(bf16[256,512]{1,0:T(8,128)(2,1)S(1)} %maximum_select_fusion.2.refs_1_.refs_0_), channel_id=1, source_target_pairs={{0,6},{1,7},{2,4},{3,5},{4,2},{5,3},{6,0},{7,1},{8,14},{9,15},{10,... | collective-permute-start | bytes 786440 | tf_op jit(solution)/shard_map/ppermute | solution.py:632
  188.4 7.4 %collective-permute-done.23 = bf16[256,512]{1,0:T(8,128)(2,1)S(1)} collective-permute-done((bf16[256,512]{1,0:T(8,128)(2,1)S(1)}, bf16[256,512]{1,0:T(8,128)(2,1)S(1)}, u32[]{:S(2)}, u32[]{:S(2)}) %collective-permute-start.23) | collective-permute-done | bytes 262176 | tf_op jit(solution)/shard_map/ppermute | solution.py:632
  196.1 4.9 %collective-permute-done.24 = bf16[256,512]{1,0:T(8,128)(2,1)S(1)} collective-permute-done((bf16[256,512]{1,0:T(8,128)(2,1)S(1)}, bf16[256,512]{1,0:T(8,128)(2,1)S(1)}, u32[]{:S(2)}, u32[]{:S(2)}) %collective-permute-start.24) | collective-permute-done | bytes 262176 | tf_op jit(solution)/shard_map/ppermute | solution.py:632
  201.0 5.2 %collective-permute-done.26 = bf16[256,512]{1,0:T(8,128)(2,1)S(1)} collective-permute-done((bf16[256,512]{1,0:T(8,128)(2,1)S(1)}, bf16[256,512]{1,0:T(8,128)(2,1)S(1)}, u32[]{:S(2)}, u32[]{:S(2)}) %collective-permute-start.26) | collective-permute-done | bytes 262176 | tf_op jit(solution)/shard_map/ppermute | solution.py:632
  210.5 2.4 %finish_ffn.3 = (f32[512,2048]{1,0:T(8,128)}, f32[8,128]{1,0:T(8,128)S(1)}) custom-call(s32[1]{0:T(128)} %bitcast.3.core_ref, bf16[1024,512]{1,0:T(8,128)(2,1)S(1)} %pad_maximum_fusion.5.own_ref.refs_1_, bf16[1024,512]{1,0:T(8,128)(2,1)S(1)} %collective-permute-done.28.other_ref), custom_call_target="tpu_custom_call" | custom-call | tf_op jit(solution)/shard_map/finish_ffn/pallas_call | solution.py:592
  213.0 2.4 %finish_ffn.2 = (f32[2048,512]{1,0:T(8,128)}, f32[8,128]{1,0:T(8,128)S(1)}) custom-call(s32[1]{0:T(128)} %bitcast.3.core_ref, bf16[1024,512]{1,0:T(8,128)(2,1)S(1)} %pad_maximum_fusion.3.refs_1_.own_ref, bf16[1024,512]{1,0:T(8,128)(2,1)S(1)} %collective-permute-done.27.other_ref), custom_call_target="tpu_custom_call" | custom-call | tf_op jit(solution)/shard_map/finish_ffn/pallas_call | solution.py:592
  215.4 2.7 %settled.3 = (bf16[8,128,512]{2,1,0:T(8,128)(2,1)}, f32[8,128]{1,0:T(8,128)S(1)}) custom-call(bf16[8,128,512]{2,1,0:T(8,128)(2,1)S(1)} %all-to-all-done.3.in_ref), custom_call_target="tpu_custom_call" | custom-call | tf_op jit(solution)/shard_map/settled/pallas_call | solution.py:725
  218.1 4.7 %collective-permute-done.30 = bf16[272,512]{1,0:T(8,128)(2,1)S(1)} collective-permute-done((bf16[272,512]{1,0:T(8,128)(2,1)S(1)}, bf16[272,512]{1,0:T(8,128)(2,1)S(1)}, u32[]{:S(2)}, u32[]{:S(2)}) %collective-permute-start.30) | collective-permute-done | bytes 278560 | tf_op jit(solution)/shard_map/ppermute | solution.py:632
  225.2 2.7 %collective-permute-done.32.other_ref = bf16[1088,512]{1,0:T(8,128)(2,1)S(1)} collective-permute-done((bf16[1088,512]{1,0:T(8,128)(2,1)S(1)}, bf16[1088,512]{1,0:T(8,128)(2,1)S(1)}, u32[]{:S(2)}, u32[]{:S(2)}) %collective-permute-start.32) | collective-permute-done | bytes 1114144 | tf_op jit(solution)/shard_map/ppermute | solution.py:632
  (154 shorter events, 50.6 us)
Async XLA Ops:
  34.0 30.2 %all-to-all-start.2 = ((bf16[8,128,512]{2,1,0:T(8,128)(2,1)}), bf16[8,128,512]{2,1,0:T(8,128)(2,1)S(1)}, u32[]{:S(2)}, u32[]{:S(2)}) async-start(bf16[8,128,512]{2,1,0:T(8,128)(2,1)} %param.21), calls=%async_computation.2 | async-start | bytes 2097152 | tf_op jit(solution)/shard_map/all_to_all | solution.py:791
  86.3 43.5 %all-to-all-start.1 = ((bf16[8,128,512]{2,1,0:T(8,128)(2,1)}), bf16[8,128,512]{2,1,0:T(8,128)(2,1)S(1)}, u32[]{:S(2)}, u32[]{:S(2)}) async-start(bf16[8,128,512]{2,1,0:T(8,128)(2,1)} %bitcast.6), calls=%async_computation.1 | async-start | bytes 2097152 | tf_op jit(solution)/shard_map/all_to_all | solution.py:791
  96.1 34.8 %collective-permute-start.1 = (bf16[512,512]{1,0:T(8,128)(2,1)S(1)}, bf16[512,512]{1,0:T(8,128)(2,1)}, u32[]{:S(2)}, u32[]{:S(2)}) collective-permute-start(bf16[512,512]{1,0:T(8,128)(2,1)S(1)} %get-tuple-element.79.refs_0_), channel_id=1, source_target_pairs={{0,4},{1,5},{2,6},{3,7},{4,0},{5,1},{6,2},{7,3},{8,12},{9,13},{10,... | collective-permute-start | bytes 1572872 | tf_op jit(solution)/shard_map/ppermute | solution.py:632
  98.1 32.8 %collective-permute-start.2 = (bf16[512,512]{1,0:T(8,128)(2,1)S(1)}, bf16[512,512]{1,0:T(8,128)(2,1)}, u32[]{:S(2)}, u32[]{:S(2)}) collective-permute-start(bf16[512,512]{1,0:T(8,128)(2,1)S(1)} %get-tuple-element.78.refs_1_), channel_id=1, source_target_pairs={{0,2},{1,3},{2,0},{3,1},{4,6},{5,7},{6,4},{7,5},{8,10},{9,11},{10,... | collective-permute-start | bytes 1572872 | tf_op jit(solution)/shard_map/ppermute | solution.py:632
  99.6 31.3 %collective-permute-start.3 = (bf16[512,512]{1,0:T(8,128)(2,1)S(1)}, bf16[512,512]{1,0:T(8,128)(2,1)}, u32[]{:S(2)}, u32[]{:S(2)}) collective-permute-start(bf16[512,512]{1,0:T(8,128)(2,1)S(1)} %get-tuple-element.77.refs_2_), channel_id=1, source_target_pairs={{0,6},{1,7},{2,4},{3,5},{4,2},{5,3},{6,0},{7,1},{8,14},{9,15},{10,... | collective-permute-start | bytes 1572872 | tf_op jit(solution)/shard_map/ppermute | solution.py:632
  99.6 30.1 %collective-permute-start.5 = (bf16[256,512]{1,0:T(8,128)(2,1)S(1)}, bf16[256,512]{1,0:T(8,128)(2,1)S(1)}, u32[]{:S(2)}, u32[]{:S(2)}) collective-permute-start(bf16[256,512]{1,0:T(8,128)(2,1)S(1)} %get-tuple-element.64), channel_id=1, source_target_pairs={{0,1},{1,0},{2,3},{3,2},{4,5},{5,4},{6,7},{7,6},{8,9},{9,8},{10,11... | collective-permute-start | bytes 786440 | tf_op jit(solution)/shard_map/ppermute | solution.py:632
  132.7 9.0 %collective-permute-start.6 = (bf16[128,512]{1,0:T(8,128)(2,1)S(1)}, bf16[128,512]{1,0:T(8,128)(2,1)S(1)}, u32[]{:S(2)}, u32[]{:S(2)}) collective-permute-start(bf16[128,512]{1,0:T(8,128)(2,1)S(1)} %get-tuple-element.103.refs_1_), channel_id=1, source_target_pairs={{0,8},{1,9},{2,10},{3,11},{4,12},{5,13},{6,14},{7,15},{8,0},{9,1},... | collective-permute-start | bytes 393224 | tf_op jit(solution)/shard_map/ppermute | solution.py:632
  134.7 9.9 %collective-permute-start.7 = (bf16[128,512]{1,0:T(8,128)(2,1)S(1)}, bf16[128,512]{1,0:T(8,128)(2,1)S(1)}, u32[]{:S(2)}, u32[]{:S(2)}) collective-permute-start(bf16[128,512]{1,0:T(8,128)(2,1)S(1)} %get-tuple-element.101.refs_1_), channel_id=1, source_target_pairs={{0,8},{1,9},{2,10},{3,11},{4,12},{5,13},{6,14},{7,15},{8,0},{9,1},... | collective-permute-start | bytes 393224 | tf_op jit(solution)/shard_map/ppermute | solution.py:632
  138.1 14.3 %collective-permute-start.10 = (bf16[272,512]{1,0:T(8,128)(2,1)S(1)}, bf16[272,512]{1,0:T(8,128)(2,1)S(1)}, u32[]{:S(2)}, u32[]{:S(2)}) collective-permute-start(bf16[272,512]{1,0:T(8,128)(2,1)S(1)} %get-tuple-element.86.refs_2_), channel_id=1, source_target_pairs={{0,2},{1,3},{2,0},{3,1},{4,6},{5,7},{6,4},{7,5},{8,10},{9,11},{10,... | collective-permute-start | bytes 835592 | tf_op jit(solution)/shard_map/ppermute | solution.py:632
  139.7 12.7 %collective-permute-start.11 = (bf16[272,512]{1,0:T(8,128)(2,1)S(1)}, bf16[272,512]{1,0:T(8,128)(2,1)S(1)}, u32[]{:S(2)}, u32[]{:S(2)}) collective-permute-start(bf16[272,512]{1,0:T(8,128)(2,1)S(1)} %get-tuple-element.87.refs_3_), channel_id=1, source_target_pairs={{0,6},{1,7},{2,4},{3,5},{4,2},{5,3},{6,0},{7,1},{8,14},{9,15},{10,... | collective-permute-start | bytes 835592 | tf_op jit(solution)/shard_map/ppermute | solution.py:632
  141.6 12.1 %collective-permute-start.9 = (bf16[272,512]{1,0:T(8,128)(2,1)S(1)}, bf16[272,512]{1,0:T(8,128)(2,1)S(1)}, u32[]{:S(2)}, u32[]{:S(2)}) collective-permute-start(bf16[272,512]{1,0:T(8,128)(2,1)S(1)} %get-tuple-element.85.refs_1_), channel_id=1, source_target_pairs={{0,4},{1,5},{2,6},{3,7},{4,0},{5,1},{6,2},{7,3},{8,12},{9,13},{10,... | collective-permute-start | bytes 835592 | tf_op jit(solution)/shard_map/ppermute | solution.py:632
  144.7 10.9 %collective-permute-start.12 = (bf16[64,512]{1,0:T(8,128)(2,1)S(1)}, bf16[64,512]{1,0:T(8,128)(2,1)S(1)}, u32[]{:S(2)}, u32[]{:S(2)}) collective-permute-start(bf16[64,512]{1,0:T(8,128)(2,1)S(1)} %get-tuple-element.107.refs_1_), channel_id=1, source_target_pairs={{0,16},{1,17},{2,18},{3,19},{4,20},{5,21},{6,22},{7,23},{8,24},{9,... | collective-permute-start | bytes 196616 | tf_op jit(solution)/shard_map/ppermute | solution.py:632
  147.4 14.3 %collective-permute-start.14 = (bf16[64,512]{1,0:T(8,128)(2,1)S(1)}, bf16[64,512]{1,0:T(8,128)(2,1)S(1)}, u32[]{:S(2)}, u32[]{:S(2)}) collective-permute-start(bf16[64,512]{1,0:T(8,128)(2,1)S(1)} %add_convert_fusion.10.refs_1_.refs_0_), channel_id=1, source_target_pairs={{0,16},{1,17},{2,18},{3,19},{4,20},{5,21},{6,22},{7,23},{8,24},{9,... | collective-permute-start | bytes 196616 | tf_op jit(solution)/shard_map/ppermute | solution.py:632
  164.8 8.1 %collective-permute-start.17 = (bf16[68,512]{1,0:T(8,128)(2,1)S(1)}, bf16[68,512]{1,0:T(8,128)(2,1)S(1)}, u32[]{:S(2)}, u32[]{:S(2)}) collective-permute-start(bf16[68,512]{1,0:T(8,128)(2,1)S(1)} %add_convert_fusion.8.refs_1_), channel_id=1, source_target_pairs={{0,16},{1,17},{2,18},{3,19},{4,20},{5,21},{6,22},{7,23},{8,24},{9,... | collective-permute-start | bytes 208904 | tf_op jit(solution)/shard_map/ppermute | solution.py:632
  173.8 11.9 %collective-permute-start.21 = (bf16[256,512]{1,0:T(8,128)(2,1)S(1)}, bf16[256,512]{1,0:T(8,128)(2,1)S(1)}, u32[]{:S(2)}, u32[]{:S(2)}) collective-permute-start(bf16[256,512]{1,0:T(8,128)(2,1)S(1)} %maximum_select_fusion.1.refs_1_.refs_0_), channel_id=1, source_target_pairs={{0,4},{1,5},{2,6},{3,7},{4,0},{5,1},{6,2},{7,3},{8,12},{9,13},{10,... | collective-permute-start | bytes 786440 | tf_op jit(solution)/shard_map/ppermute | solution.py:632
  175.3 13.1 %collective-permute-start.22 = (bf16[256,512]{1,0:T(8,128)(2,1)S(1)}, bf16[256,512]{1,0:T(8,128)(2,1)S(1)}, u32[]{:S(2)}, u32[]{:S(2)}) collective-permute-start(bf16[256,512]{1,0:T(8,128)(2,1)S(1)} %maximum_select_fusion.1.refs_1_.refs_0_), channel_id=1, source_target_pairs={{0,2},{1,3},{2,0},{3,1},{4,6},{5,7},{6,4},{7,5},{8,10},{9,11},{10,... | collective-permute-start | bytes 786440 | tf_op jit(solution)/shard_map/ppermute | solution.py:632
  176.8 19.0 %collective-permute-start.23 = (bf16[256,512]{1,0:T(8,128)(2,1)S(1)}, bf16[256,512]{1,0:T(8,128)(2,1)S(1)}, u32[]{:S(2)}, u32[]{:S(2)}) collective-permute-start(bf16[256,512]{1,0:T(8,128)(2,1)S(1)} %maximum_select_fusion.1.refs_1_.refs_0_), channel_id=1, source_target_pairs={{0,6},{1,7},{2,4},{3,5},{4,2},{5,3},{6,0},{7,1},{8,14},{9,15},{10,... | collective-permute-start | bytes 786440 | tf_op jit(solution)/shard_map/ppermute | solution.py:632
  178.9 22.1 %collective-permute-start.24 = (bf16[256,512]{1,0:T(8,128)(2,1)S(1)}, bf16[256,512]{1,0:T(8,128)(2,1)S(1)}, u32[]{:S(2)}, u32[]{:S(2)}) collective-permute-start(bf16[256,512]{1,0:T(8,128)(2,1)S(1)} %maximum_select_fusion.2.refs_1_.refs_0_), channel_id=1, source_target_pairs={{0,4},{1,5},{2,6},{3,7},{4,0},{5,1},{6,2},{7,3},{8,12},{9,13},{10,... | collective-permute-start | bytes 786440 | tf_op jit(solution)/shard_map/ppermute | solution.py:632
  180.4 35.0 %all-to-all-start.3 = ((bf16[8,128,512]{2,1,0:T(8,128)(2,1)}), bf16[8,128,512]{2,1,0:T(8,128)(2,1)S(1)}, u32[]{:S(2)}, u32[]{:S(2)}) async-start(bf16[8,128,512]{2,1,0:T(8,128)(2,1)} %bitcast.8), calls=%async_computation.3 | async-start | bytes 2097152 | tf_op jit(solution)/shard_map/all_to_all | solution.py:791
  184.0 17.0 %collective-permute-start.25 = (bf16[256,512]{1,0:T(8,128)(2,1)S(1)}, bf16[256,512]{1,0:T(8,128)(2,1)S(1)}, u32[]{:S(2)}, u32[]{:S(2)}) collective-permute-start(bf16[256,512]{1,0:T(8,128)(2,1)S(1)} %maximum_select_fusion.2.refs_1_.refs_0_), channel_id=1, source_target_pairs={{0,2},{1,3},{2,0},{3,1},{4,6},{5,7},{6,4},{7,5},{8,10},{9,11},{10,... | collective-permute-start | bytes 786440 | tf_op jit(solution)/shard_map/ppermute | solution.py:632
  185.7 20.5 %collective-permute-start.26 = (bf16[256,512]{1,0:T(8,128)(2,1)S(1)}, bf16[256,512]{1,0:T(8,128)(2,1)S(1)}, u32[]{:S(2)}, u32[]{:S(2)}) collective-permute-start(bf16[256,512]{1,0:T(8,128)(2,1)S(1)} %maximum_select_fusion.2.refs_1_.refs_0_), channel_id=1, source_target_pairs={{0,6},{1,7},{2,4},{3,5},{4,2},{5,3},{6,0},{7,1},{8,14},{9,15},{10,... | collective-permute-start | bytes 786440 | tf_op jit(solution)/shard_map/ppermute | solution.py:632
  207.1 11.1 %collective-permute-start.29 = (bf16[272,512]{1,0:T(8,128)(2,1)S(1)}, bf16[272,512]{1,0:T(8,128)(2,1)S(1)}, u32[]{:S(2)}, u32[]{:S(2)}) collective-permute-start(bf16[272,512]{1,0:T(8,128)(2,1)S(1)} %maximum_select_fusion.refs_1_.refs_0_), channel_id=1, source_target_pairs={{0,4},{1,5},{2,6},{3,7},{4,0},{5,1},{6,2},{7,3},{8,12},{9,13},{10,... | collective-permute-start | bytes 835592 | tf_op jit(solution)/shard_map/ppermute | solution.py:632
  208.5 14.3 %collective-permute-start.30 = (bf16[272,512]{1,0:T(8,128)(2,1)S(1)}, bf16[272,512]{1,0:T(8,128)(2,1)S(1)}, u32[]{:S(2)}, u32[]{:S(2)}) collective-permute-start(bf16[272,512]{1,0:T(8,128)(2,1)S(1)} %maximum_select_fusion.refs_1_.refs_0_), channel_id=1, source_target_pairs={{0,2},{1,3},{2,0},{3,1},{4,6},{5,7},{6,4},{7,5},{8,10},{9,11},{10,... | collective-permute-start | bytes 835592 | tf_op jit(solution)/shard_map/ppermute | solution.py:632
  209.1 13.8 %collective-permute-start.31 = (bf16[272,512]{1,0:T(8,128)(2,1)S(1)}, bf16[272,512]{1,0:T(8,128)(2,1)S(1)}, u32[]{:S(2)}, u32[]{:S(2)}) collective-permute-start(bf16[272,512]{1,0:T(8,128)(2,1)S(1)} %maximum_select_fusion.refs_1_.refs_0_), channel_id=1, source_target_pairs={{0,6},{1,7},{2,4},{3,5},{4,2},{5,3},{6,0},{7,1},{8,14},{9,15},{10,... | collective-permute-start | bytes 835592 | tf_op jit(solution)/shard_map/ppermute | solution.py:632
  (31 other events, 366.5 us)

commit v6 on v5

--- a/solution.py
+++ b/solution.py
@@ -18,12 +18,13 @@
 NEG = -1e30
 STEP_PAIRS = 2
 GAIN_ROWS = 64
+FLOPS_PER_US = 1000000000
 TAIL = "duadudAuaduaaduaduDUa"
 GATE_KIB = 512
 SETTLE = 12
 TRADE_AFTER = 12
 TRADED = 18
-FFN_ROWS = 2
+FFN_ROWS = 1
 FORWARD_MIB = 52
 FFN_MIB = 50
 ATTENTION_MIB = 54
@@ -452,6 +453,11 @@
     return pl.BlockSpec((BLOCK // CHUNK,) + shape, lambda i: (index(i),) + (0,) * len(shape))
 
 
+def work(micros):
+    flops = int(micros * FLOPS_PER_US)
+    return pl.CostEstimate(flops=flops, bytes_accessed=0, transcendentals=0)
+
+
 def params(mib):
     return pltpu.CompilerParams(
         vmem_limit_bytes=mib * 1024 * 1024, dimension_semantics=("arbitrary",)
@@ -495,6 +501,7 @@
             pltpu.VMEM((dim, dim), BF16), pltpu.VMEM((dim, dim), BF16),
         ],
         compiler_params=params(FORWARD_MIB),
+        cost_estimate=work(25),
         name="layer_forward",
     )(x, segments, place, gain_attn, gain_ffn, wq, wk, wv, wo, wu, wd, *entry)
 
@@ -525,6 +532,7 @@
             pltpu.VMEM((dim, dim), F32), pltpu.VMEM((dim, dim), F32),
         ],
         compiler_params=params(FFN_MIB),
+        cost_estimate=work(20),
         name="ffn_backward",
     )(dy, x1, a, gain_ffn, wo, wu, wd, core)
 
@@ -573,6 +581,7 @@
             pltpu.VMEM((dim, dim), BF16), pltpu.VMEM((dim, dim), BF16),
         ],
         compiler_params=params(ATTENTION_MIB),
+        cost_estimate=work(29),
         name="attention_backward",
     )(*after, *through, *streamed, *held)
 

time: 231 us -> 231 us (level)
  blocking collectives: 33.3 us -> 0 us
  waiting for transfers between devices: 36.3 us -> 60.2 us
  starting transfers between devices: 55.4 us -> 65.1 us
    all_to_all x1 -> x0, blocking collectives: 33.3 us -> none  [trade(): lax.all_to_all(array.reshape(row_count, shard_len, dim), 'seq', 0, 0, axi...]
    all_to_all x3 -> x4, waiting for transfers between devices: 0.01 us -> 25.7 us  [trade(): lax.all_to_all(array.reshape(row_count, shard_len, dim), 'seq', 0, 0, axi...]
    all_to_all x3 -> x4, starting transfers between devices: 13.1 us -> 20.5 us  [trade(): lax.all_to_all(array.reshape(row_count, shard_len, dim), 'seq', 0, 0, axi...]
  transfers between devices with their start and end apart: 36 -> 37, of which waited for: 12 -> 13; matrix products, arithmetic and copies ran while one was open for 4% -> 4% of each run, Pallas kernels for 28% -> 28%
where the time goes in v6:
time: 231 us
  Pallas kernels  88.3 us (38%)
  starting transfers between devices  65.1 us (28%)
  waiting for transfers between devices  60.2 us (26%)
  other arithmetic  8.91 us (4%)
  local copies, waits for them, and re-layouts  6.94 us (3%)
    ppermute x33, starting transfers between devices, partner(): return lax.ppermute(array, ('seq', 'rows'), pairs)  44.5 us
    ppermute x33, waiting for transfers between devices, partner(): return lax.ppermute(array, ('seq', 'rows'), pairs)  34.5 us
    pallas_call x1, Pallas kernels, run_attention_backward(): pl.pallas_call(body, grid=(steps,), input_output_aliases={len(after) + n:...  29.5 us
    pallas_call x1, Pallas kernels, run_forward(): pl.pallas_call(functools.partial(forward_kernel, len(entry)), grid=(lengt...  25.7 us
    all_to_all x4, waiting for transfers between devices, trade(): lax.all_to_all(array.reshape(row_count, shard_len, dim), 'seq', 0, 0, axi...  25.7 us
    pallas_call x1, Pallas kernels, run_ffn_backward(): pl.pallas_call(ffn_backward_kernel, grid=(ff // dim,), in_specs=[FFN_IN,...  20.6 us
    all_to_all x4, starting transfers between devices, trade(): lax.all_to_all(array.reshape(row_count, shard_len, dim), 'seq', 0, 0, axi...  20.5 us
    pallas_call x2, Pallas kernels, settled(): pl.pallas_call(kernel, grid=(array.shape[0],), in_specs=[block], out_spec...  5.4 us
  transfers between devices with their start and end apart: 37, of which 13 were waited for; matrix products, arithmetic and copies ran while one was open for 4% of the time, Pallas kernels for 28%

profile of v6, /device:TPU:0, one launch (start us, length us, event | category | flops | bytes accessed | tf_op | source)
XLA Modules:
  0.0 230.6 jit_solution(5582706300498509547)
XLA Ops:
  0.7 7.4 %all-to-all-start = ((bf16[8,128,512]{2,1,0:T(8,128)(2,1)}), bf16[8,128,512]{2,1,0:T(8,128)(2,1)S(1)}, u32[]{:S(2)}, u32[]{:S(2)}) async-start(bf16[8,128,512]{2,1,0:T(8,128)(2,1)} %param.11), calls=%async_computation | async-start | bytes 2097152 | tf_op jit(solution)/shard_map/all_to_all | solution.py:800
  8.2 25.7 %all-to-all-done = bf16[8,128,512]{2,1,0:T(8,128)(2,1)S(1)} async-done(((bf16[8,128,512]{2,1,0:T(8,128)(2,1)}), bf16[8,128,512]{2,1,0:T(8,128)(2,1)S(1)}, u32[]{:S(2)}, u32[]{:S(2)}) %all-to-all-start) | async-done | bytes 1048608 | tf_op jit(solution)/shard_map/all_to_all | solution.py:800
  34.8 3.6 %all-to-all-start.2 = ((bf16[8,128,512]{2,1,0:T(8,128)(2,1)}), bf16[8,128,512]{2,1,0:T(8,128)(2,1)S(1)}, u32[]{:S(2)}, u32[]{:S(2)}) async-start(bf16[8,128,512]{2,1,0:T(8,128)(2,1)} %param.21), calls=%async_computation.2 | async-start | bytes 2097152 | tf_op jit(solution)/shard_map/all_to_all | solution.py:800
  38.5 25.7 %layer_forward.1 = (bf16[1024,512]{1,0:T(8,128)(2,1)}, f32[1024,512]{1,0:T(8,128)}, bf16[1024,512]{1,0:T(8,128)(2,1)}, bf16[1024,512]{1,0:T(8,128)(2,1)}, bf16[1...) custom-call(bf16[1024,512]{1,0:T(8,128)(2,1)} %bitcast.59, ...), custom_call_target="tpu_custom_call" | custom-call | flops 24999999488 | tf_op jit(solution)/shard_map/layer_forward/pallas_call | solution.py:481
  65.0 20.6 %ffn_backward.1 = (f32[1024,512]{1,0:T(8,128)}, bf16[1024,512]{1,0:T(8,128)(2,1)S(1)}, f32[8,512]{1,0:T(8,128)S(1)}, bf16[2048,512]{1,0:T(8,128)(2,1)}, bf16[204...) custom-call(bf16[1024,512]{1,0:T(8,128)(2,1)S(1)} %bitcast.54, ...), custom_call_target="tpu_custom_call" | custom-call | flops 20000000000 | tf_op jit(solution)/shard_map/ffn_backward/pallas_call | solution.py:517
  87.1 6.0 %all-to-all-start.1 = ((bf16[8,128,512]{2,1,0:T(8,128)(2,1)}), bf16[8,128,512]{2,1,0:T(8,128)(2,1)S(1)}, u32[]{:S(2)}, u32[]{:S(2)}) async-start(bf16[8,128,512]{2,1,0:T(8,128)(2,1)} %bitcast.6), calls=%async_computation.1 | async-start | bytes 2097152 | tf_op jit(solution)/shard_map/all_to_all | solution.py:800
  93.1 2.8 %add_convert_fusion = bf16[2048,512]{1,0:T(8,128)(2,1)S(1)} fusion(bf16[2048,512]{1,0:T(8,128)(2,1)} %collective-permute-done, bf16[2048,512]{1,0:T(8,128)(2,1)} %get-tuple-element.47), kind=kLoop, calls=%fused_computation | loop fusion | flops 4194304 | bytes 6291456 | tf_op jit(solution)/shard_map/convert_element_type | solution.py:648
  100.9 29.5 %attention_backward.1 = (bf16[512,512]{1,0:T(8,128)(2,1)}, bf16[1024,512]{1,0:T(8,128)(2,1)}, bf16[832,512]{1,0:T(8,128)(2,1)}, bf16[832,512]{1,0:T(8,128)(2,1)}) custom-call(bf16[512,512]{1,0:T(8,128)(2,1)} %get-tuple-element.79.refs_0_, bf16[512,512]{1,0:T(8,128)(2,1)} %get-tuple-element.78.refs_1_, ...), custom_call_target="tpu_custom_call", output_to_operand_aliasing={{0}: (3, {})} | custom-call | flops 28999999488 | tf_op jit(solution)/shard_map/attention_backward/pallas_call | solution.py:565
  141.1 2.9 %collective-permute-start.8 = (bf16[64,512]{1,0:T(8,128)(2,1)S(1)}, bf16[64,512]{1,0:T(8,128)(2,1)S(1)}, u32[]{:S(2)}, u32[]{:S(2)}) collective-permute-start(bf16[64,512]{1,0:T(8,128)(2,1)S(1)} %get-tuple-element.109.refs_1_), channel_id=1, source_target_pairs={{0,16},{1,17},{2,18},{3,19},{4,20},{5,21},{6,22},{7,23},{8,24},{9,... | collective-permute-start | bytes 196616 | tf_op jit(solution)/shard_map/ppermute | solution.py:641
  146.7 3.1 %collective-permute-start.14 = (bf16[64,512]{1,0:T(8,128)(2,1)S(1)}, bf16[64,512]{1,0:T(8,128)(2,1)S(1)}, u32[]{:S(2)}, u32[]{:S(2)}) collective-permute-start(bf16[64,512]{1,0:T(8,128)(2,1)S(1)} %add_convert_fusion.10.refs_1_.refs_0_), channel_id=1, source_target_pairs={{0,16},{1,17},{2,18},{3,19},{4,20},{5,21},{6,22},{7,23},{8,24},{9,... | collective-permute-start | bytes 196616 | tf_op jit(solution)/shard_map/ppermute | solution.py:641
  149.8 2.5 %collective-permute-done.10 = bf16[272,512]{1,0:T(8,128)(2,1)S(1)} collective-permute-done((bf16[272,512]{1,0:T(8,128)(2,1)S(1)}, bf16[272,512]{1,0:T(8,128)(2,1)S(1)}, u32[]{:S(2)}, u32[]{:S(2)}) %collective-permute-start.10) | collective-permute-done | bytes 278560 | tf_op jit(solution)/shard_map/ppermute | solution.py:641
  155.5 2.4 %collective-permute-start.15 = (bf16[64,512]{1,0:T(8,128)(2,1)S(1)}, bf16[64,512]{1,0:T(8,128)(2,1)S(1)}, u32[]{:S(2)}, u32[]{:S(2)}) collective-permute-start(bf16[64,512]{1,0:T(8,128)(2,1)S(1)} %add_convert_fusion.9.refs_1_.refs_0_), channel_id=1, source_target_pairs={{0,16},{1,17},{2,18},{3,19},{4,20},{5,21},{6,22},{7,23},{8,24},{9,... | collective-permute-start | bytes 196616 | tf_op jit(solution)/shard_map/ppermute | solution.py:641
  167.0 3.3 %collective-permute-start.18 = (bf16[128,512]{1,0:T(8,128)(2,1)S(1)}, bf16[128,512]{1,0:T(8,128)(2,1)S(1)}, u32[]{:S(2)}, u32[]{:S(2)}) collective-permute-start(bf16[128,512]{1,0:T(8,128)(2,1)S(1)} %maximum_select_fusion.4.refs_1_.refs_0_), channel_id=1, source_target_pairs={{0,8},{1,9},{2,10},{3,11},{4,12},{5,13},{6,14},{7,15},{8,0},{9,1},... | collective-permute-start | bytes 393224 | tf_op jit(solution)/shard_map/ppermute | solution.py:641
  170.3 2.7 %settled.2 = (bf16[8,128,512]{2,1,0:T(8,128)(2,1)}, f32[8,128]{1,0:T(8,128)S(1)}) custom-call(bf16[8,128,512]{2,1,0:T(8,128)(2,1)S(1)} %all-to-all-done.1.in_ref.refs_1_), custom_call_target="tpu_custom_call" | custom-call | tf_op jit(solution)/shard_map/settled/pallas_call | solution.py:734
  180.5 3.6 %all-to-all-start.3 = ((bf16[8,128,512]{2,1,0:T(8,128)(2,1)}), bf16[8,128,512]{2,1,0:T(8,128)(2,1)S(1)}, u32[]{:S(2)}, u32[]{:S(2)}) async-start(bf16[8,128,512]{2,1,0:T(8,128)(2,1)} %bitcast.8), calls=%async_computation.3 | async-start | bytes 2097152 | tf_op jit(solution)/shard_map/all_to_all | solution.py:800
  185.8 3.8 %collective-permute-start.26 = (bf16[256,512]{1,0:T(8,128)(2,1)S(1)}, bf16[256,512]{1,0:T(8,128)(2,1)S(1)}, u32[]{:S(2)}, u32[]{:S(2)}) collective-permute-start(bf16[256,512]{1,0:T(8,128)(2,1)S(1)} %maximum_select_fusion.2.refs_1_.refs_0_), channel_id=1, source_target_pairs={{0,6},{1,7},{2,4},{3,5},{4,2},{5,3},{6,0},{7,1},{8,14},{9,15},{10,... | collective-permute-start | bytes 786440 | tf_op jit(solution)/shard_map/ppermute | solution.py:641
  189.6 5.9 %collective-permute-done.23 = bf16[256,512]{1,0:T(8,128)(2,1)S(1)} collective-permute-done((bf16[256,512]{1,0:T(8,128)(2,1)S(1)}, bf16[256,512]{1,0:T(8,128)(2,1)S(1)}, u32[]{:S(2)}, u32[]{:S(2)}) %collective-permute-start.23) | collective-permute-done | bytes 262176 | tf_op jit(solution)/shard_map/ppermute | solution.py:641
  195.8 5.1 %collective-permute-done.24 = bf16[256,512]{1,0:T(8,128)(2,1)S(1)} collective-permute-done((bf16[256,512]{1,0:T(8,128)(2,1)S(1)}, bf16[256,512]{1,0:T(8,128)(2,1)S(1)}, u32[]{:S(2)}, u32[]{:S(2)}) %collective-permute-start.24) | collective-permute-done | bytes 262176 | tf_op jit(solution)/shard_map/ppermute | solution.py:641
  200.9 5.2 %collective-permute-done.26 = bf16[256,512]{1,0:T(8,128)(2,1)S(1)} collective-permute-done((bf16[256,512]{1,0:T(8,128)(2,1)S(1)}, bf16[256,512]{1,0:T(8,128)(2,1)S(1)}, u32[]{:S(2)}, u32[]{:S(2)}) %collective-permute-start.26) | collective-permute-done | bytes 262176 | tf_op jit(solution)/shard_map/ppermute | solution.py:641
  210.4 2.4 %finish_ffn.3 = (f32[512,2048]{1,0:T(8,128)}, f32[8,128]{1,0:T(8,128)S(1)}) custom-call(s32[1]{0:T(128)} %bitcast.3.core_ref, bf16[1024,512]{1,0:T(8,128)(2,1)S(1)} %pad_maximum_fusion.5.own_ref.refs_1_, bf16[1024,512]{1,0:T(8,128)(2,1)S(1)} %collective-permute-done.28.other_ref), custom_call_target="tpu_custom_call" | custom-call | tf_op jit(solution)/shard_map/finish_ffn/pallas_call | solution.py:601
  212.8 2.4 %finish_ffn.2 = (f32[2048,512]{1,0:T(8,128)}, f32[8,128]{1,0:T(8,128)S(1)}) custom-call(s32[1]{0:T(128)} %bitcast.3.core_ref, bf16[1024,512]{1,0:T(8,128)(2,1)S(1)} %pad_maximum_fusion.3.refs_1_.own_ref, bf16[1024,512]{1,0:T(8,128)(2,1)S(1)} %collective-permute-done.27.other_ref), custom_call_target="tpu_custom_call" | custom-call | tf_op jit(solution)/shard_map/finish_ffn/pallas_call | solution.py:601
  215.3 2.7 %settled.3 = (bf16[8,128,512]{2,1,0:T(8,128)(2,1)}, f32[8,128]{1,0:T(8,128)S(1)}) custom-call(bf16[8,128,512]{2,1,0:T(8,128)(2,1)S(1)} %all-to-all-done.3.in_ref), custom_call_target="tpu_custom_call" | custom-call | tf_op jit(solution)/shard_map/settled/pallas_call | solution.py:734
  218.0 4.7 %collective-permute-done.30 = bf16[272,512]{1,0:T(8,128)(2,1)S(1)} collective-permute-done((bf16[272,512]{1,0:T(8,128)(2,1)S(1)}, bf16[272,512]{1,0:T(8,128)(2,1)S(1)}, u32[]{:S(2)}, u32[]{:S(2)}) %collective-permute-start.30) | collective-permute-done | bytes 278560 | tf_op jit(solution)/shard_map/ppermute | solution.py:641
  225.0 2.7 %collective-permute-done.32.other_ref = bf16[1088,512]{1,0:T(8,128)(2,1)S(1)} collective-permute-done((bf16[1088,512]{1,0:T(8,128)(2,1)S(1)}, bf16[1088,512]{1,0:T(8,128)(2,1)S(1)}, u32[]{:S(2)}, u32[]{:S(2)}) %collective-permute-start.32) | collective-permute-done | bytes 1114144 | tf_op jit(solution)/shard_map/ppermute | solution.py:641
  (151 shorter events, 52.6 us)
Async XLA Ops:
  0.7 33.2 %all-to-all-start = ((bf16[8,128,512]{2,1,0:T(8,128)(2,1)}), bf16[8,128,512]{2,1,0:T(8,128)(2,1)S(1)}, u32[]{:S(2)}, u32[]{:S(2)}) async-start(bf16[8,128,512]{2,1,0:T(8,128)(2,1)} %param.11), calls=%async_computation | async-start | bytes 2097152 | tf_op jit(solution)/shard_map/all_to_all | solution.py:800
  34.8 30.1 %all-to-all-start.2 = ((bf16[8,128,512]{2,1,0:T(8,128)(2,1)}), bf16[8,128,512]{2,1,0:T(8,128)(2,1)S(1)}, u32[]{:S(2)}, u32[]{:S(2)}) async-start(bf16[8,128,512]{2,1,0:T(8,128)(2,1)} %param.21), calls=%async_computation.2 | async-start | bytes 2097152 | tf_op jit(solution)/shard_map/all_to_all | solution.py:800
  86.6 43.8 %collective-permute-start.5 = (bf16[256,512]{1,0:T(8,128)(2,1)S(1)}, bf16[256,512]{1,0:T(8,128)(2,1)S(1)}, u32[]{:S(2)}, u32[]{:S(2)}) collective-permute-start(bf16[256,512]{1,0:T(8,128)(2,1)S(1)} %get-tuple-element.64), channel_id=1, source_target_pairs={{0,1},{1,0},{2,3},{3,2},{4,5},{5,4},{6,7},{7,6},{8,9},{9,8},{10,11... | collective-permute-start | bytes 786440 | tf_op jit(solution)/shard_map/ppermute | solution.py:641
  87.1 43.4 %all-to-all-start.1 = ((bf16[8,128,512]{2,1,0:T(8,128)(2,1)}), bf16[8,128,512]{2,1,0:T(8,128)(2,1)S(1)}, u32[]{:S(2)}, u32[]{:S(2)}) async-start(bf16[8,128,512]{2,1,0:T(8,128)(2,1)} %bitcast.6), calls=%async_computation.1 | async-start | bytes 2097152 | tf_op jit(solution)/shard_map/all_to_all | solution.py:800
  97.3 34.3 %collective-permute-start.1 = (bf16[512,512]{1,0:T(8,128)(2,1)}, bf16[512,512]{1,0:T(8,128)(2,1)S(1)}, u32[]{:S(2)}, u32[]{:S(2)}) collective-permute-start(bf16[512,512]{1,0:T(8,128)(2,1)} %get-tuple-element.79.refs_0_), channel_id=1, source_target_pairs={{0,4},{1,5},{2,6},{3,7},{4,0},{5,1},{6,2},{7,3},{8,12},{9,13},{10,... | collective-permute-start | bytes 1572872 | tf_op jit(solution)/shard_map/ppermute | solution.py:641
  99.3 32.2 %collective-permute-start.2 = (bf16[512,512]{1,0:T(8,128)(2,1)}, bf16[512,512]{1,0:T(8,128)(2,1)}, u32[]{:S(2)}, u32[]{:S(2)}) collective-permute-start(bf16[512,512]{1,0:T(8,128)(2,1)} %get-tuple-element.78.refs_1_), channel_id=1, source_target_pairs={{0,2},{1,3},{2,0},{3,1},{4,6},{5,7},{6,4},{7,5},{8,10},{9,11},{10,... | collective-permute-start | bytes 1572872 | tf_op jit(solution)/shard_map/ppermute | solution.py:641
  100.9 30.7 %collective-permute-start.3 = (bf16[512,512]{1,0:T(8,128)(2,1)}, bf16[512,512]{1,0:T(8,128)(2,1)}, u32[]{:S(2)}, u32[]{:S(2)}) collective-permute-start(bf16[512,512]{1,0:T(8,128)(2,1)} %get-tuple-element.77.refs_2_), channel_id=1, source_target_pairs={{0,6},{1,7},{2,4},{3,5},{4,2},{5,3},{6,0},{7,1},{8,14},{9,15},{10,... | collective-permute-start | bytes 1572872 | tf_op jit(solution)/shard_map/ppermute | solution.py:641
  135.3 8.8 %collective-permute-start.7 = (bf16[128,512]{1,0:T(8,128)(2,1)S(1)}, bf16[128,512]{1,0:T(8,128)(2,1)S(1)}, u32[]{:S(2)}, u32[]{:S(2)}) collective-permute-start(bf16[128,512]{1,0:T(8,128)(2,1)S(1)} %get-tuple-element.101.refs_1_), channel_id=1, source_target_pairs={{0,8},{1,9},{2,10},{3,11},{4,12},{5,13},{6,14},{7,15},{8,0},{9,1},... | collective-permute-start | bytes 393224 | tf_op jit(solution)/shard_map/ppermute | solution.py:641
  137.5 14.8 %collective-permute-start.10 = (bf16[272,512]{1,0:T(8,128)(2,1)S(1)}, bf16[272,512]{1,0:T(8,128)(2,1)S(1)}, u32[]{:S(2)}, u32[]{:S(2)}) collective-permute-start(bf16[272,512]{1,0:T(8,128)(2,1)S(1)} %get-tuple-element.86.refs_2_), channel_id=1, source_target_pairs={{0,2},{1,3},{2,0},{3,1},{4,6},{5,7},{6,4},{7,5},{8,10},{9,11},{10,... | collective-permute-start | bytes 835592 | tf_op jit(solution)/shard_map/ppermute | solution.py:641
  139.1 13.2 %collective-permute-start.11 = (bf16[272,512]{1,0:T(8,128)(2,1)S(1)}, bf16[272,512]{1,0:T(8,128)(2,1)S(1)}, u32[]{:S(2)}, u32[]{:S(2)}) collective-permute-start(bf16[272,512]{1,0:T(8,128)(2,1)S(1)} %get-tuple-element.87.refs_3_), channel_id=1, source_target_pairs={{0,6},{1,7},{2,4},{3,5},{4,2},{5,3},{6,0},{7,1},{8,14},{9,15},{10,... | collective-permute-start | bytes 835592 | tf_op jit(solution)/shard_map/ppermute | solution.py:641
  141.0 12.5 %collective-permute-start.9 = (bf16[272,512]{1,0:T(8,128)(2,1)S(1)}, bf16[272,512]{1,0:T(8,128)(2,1)S(1)}, u32[]{:S(2)}, u32[]{:S(2)}) collective-permute-start(bf16[272,512]{1,0:T(8,128)(2,1)S(1)} %get-tuple-element.85.refs_1_), channel_id=1, source_target_pairs={{0,4},{1,5},{2,6},{3,7},{4,0},{5,1},{6,2},{7,3},{8,12},{9,13},{10,... | collective-permute-start | bytes 835592 | tf_op jit(solution)/shard_map/ppermute | solution.py:641
  144.1 11.4 %collective-permute-start.12 = (bf16[64,512]{1,0:T(8,128)(2,1)S(1)}, bf16[64,512]{1,0:T(8,128)(2,1)S(1)}, u32[]{:S(2)}, u32[]{:S(2)}) collective-permute-start(bf16[64,512]{1,0:T(8,128)(2,1)S(1)} %get-tuple-element.107.refs_1_), channel_id=1, source_target_pairs={{0,16},{1,17},{2,18},{3,19},{4,20},{5,21},{6,22},{7,23},{8,24},{9,... | collective-permute-start | bytes 196616 | tf_op jit(solution)/shard_map/ppermute | solution.py:641
  146.7 14.9 %collective-permute-start.14 = (bf16[64,512]{1,0:T(8,128)(2,1)S(1)}, bf16[64,512]{1,0:T(8,128)(2,1)S(1)}, u32[]{:S(2)}, u32[]{:S(2)}) collective-permute-start(bf16[64,512]{1,0:T(8,128)(2,1)S(1)} %add_convert_fusion.10.refs_1_.refs_0_), channel_id=1, source_target_pairs={{0,16},{1,17},{2,18},{3,19},{4,20},{5,21},{6,22},{7,23},{8,24},{9,... | collective-permute-start | bytes 196616 | tf_op jit(solution)/shard_map/ppermute | solution.py:641
  165.0 8.1 %collective-permute-start.17 = (bf16[68,512]{1,0:T(8,128)(2,1)S(1)}, bf16[68,512]{1,0:T(8,128)(2,1)S(1)}, u32[]{:S(2)}, u32[]{:S(2)}) collective-permute-start(bf16[68,512]{1,0:T(8,128)(2,1)S(1)} %add_convert_fusion.8.refs_1_), channel_id=1, source_target_pairs={{0,16},{1,17},{2,18},{3,19},{4,20},{5,21},{6,22},{7,23},{8,24},{9,... | collective-permute-start | bytes 208904 | tf_op jit(solution)/shard_map/ppermute | solution.py:641
  173.7 12.1 %collective-permute-start.21 = (bf16[256,512]{1,0:T(8,128)(2,1)S(1)}, bf16[256,512]{1,0:T(8,128)(2,1)S(1)}, u32[]{:S(2)}, u32[]{:S(2)}) collective-permute-start(bf16[256,512]{1,0:T(8,128)(2,1)S(1)} %maximum_select_fusion.1.refs_1_.refs_0_), channel_id=1, source_target_pairs={{0,4},{1,5},{2,6},{3,7},{4,0},{5,1},{6,2},{7,3},{8,12},{9,13},{10,... | collective-permute-start | bytes 786440 | tf_op jit(solution)/shard_map/ppermute | solution.py:641
  175.2 14.4 %collective-permute-start.22 = (bf16[256,512]{1,0:T(8,128)(2,1)S(1)}, bf16[256,512]{1,0:T(8,128)(2,1)S(1)}, u32[]{:S(2)}, u32[]{:S(2)}) collective-permute-start(bf16[256,512]{1,0:T(8,128)(2,1)S(1)} %maximum_select_fusion.1.refs_1_.refs_0_), channel_id=1, source_target_pairs={{0,2},{1,3},{2,0},{3,1},{4,6},{5,7},{6,4},{7,5},{8,10},{9,11},{10,... | collective-permute-start | bytes 786440 | tf_op jit(solution)/shard_map/ppermute | solution.py:641
  176.7 18.8 %collective-permute-start.23 = (bf16[256,512]{1,0:T(8,128)(2,1)S(1)}, bf16[256,512]{1,0:T(8,128)(2,1)S(1)}, u32[]{:S(2)}, u32[]{:S(2)}) collective-permute-start(bf16[256,512]{1,0:T(8,128)(2,1)S(1)} %maximum_select_fusion.1.refs_1_.refs_0_), channel_id=1, source_target_pairs={{0,6},{1,7},{2,4},{3,5},{4,2},{5,3},{6,0},{7,1},{8,14},{9,15},{10,... | collective-permute-start | bytes 786440 | tf_op jit(solution)/shard_map/ppermute | solution.py:641
  179.0 21.9 %collective-permute-start.24 = (bf16[256,512]{1,0:T(8,128)(2,1)S(1)}, bf16[256,512]{1,0:T(8,128)(2,1)S(1)}, u32[]{:S(2)}, u32[]{:S(2)}) collective-permute-start(bf16[256,512]{1,0:T(8,128)(2,1)S(1)} %maximum_select_fusion.2.refs_1_.refs_0_), channel_id=1, source_target_pairs={{0,4},{1,5},{2,6},{3,7},{4,0},{5,1},{6,2},{7,3},{8,12},{9,13},{10,... | collective-permute-start | bytes 786440 | tf_op jit(solution)/shard_map/ppermute | solution.py:641
  180.5 34.7 %all-to-all-start.3 = ((bf16[8,128,512]{2,1,0:T(8,128)(2,1)}), bf16[8,128,512]{2,1,0:T(8,128)(2,1)S(1)}, u32[]{:S(2)}, u32[]{:S(2)}) async-start(bf16[8,128,512]{2,1,0:T(8,128)(2,1)} %bitcast.8), calls=%async_computation.3 | async-start | bytes 2097152 | tf_op jit(solution)/shard_map/all_to_all | solution.py:800
  184.1 16.8 %collective-permute-start.25 = (bf16[256,512]{1,0:T(8,128)(2,1)S(1)}, bf16[256,512]{1,0:T(8,128)(2,1)S(1)}, u32[]{:S(2)}, u32[]{:S(2)}) collective-permute-start(bf16[256,512]{1,0:T(8,128)(2,1)S(1)} %maximum_select_fusion.2.refs_1_.refs_0_), channel_id=1, source_target_pairs={{0,2},{1,3},{2,0},{3,1},{4,6},{5,7},{6,4},{7,5},{8,10},{9,11},{10,... | collective-permute-start | bytes 786440 | tf_op jit(solution)/shard_map/ppermute | solution.py:641
  185.8 20.3 %collective-permute-start.26 = (bf16[256,512]{1,0:T(8,128)(2,1)S(1)}, bf16[256,512]{1,0:T(8,128)(2,1)S(1)}, u32[]{:S(2)}, u32[]{:S(2)}) collective-permute-start(bf16[256,512]{1,0:T(8,128)(2,1)S(1)} %maximum_select_fusion.2.refs_1_.refs_0_), channel_id=1, source_target_pairs={{0,6},{1,7},{2,4},{3,5},{4,2},{5,3},{6,0},{7,1},{8,14},{9,15},{10,... | collective-permute-start | bytes 786440 | tf_op jit(solution)/shard_map/ppermute | solution.py:641
  206.9 11.1 %collective-permute-start.29 = (bf16[272,512]{1,0:T(8,128)(2,1)S(1)}, bf16[272,512]{1,0:T(8,128)(2,1)S(1)}, u32[]{:S(2)}, u32[]{:S(2)}) collective-permute-start(bf16[272,512]{1,0:T(8,128)(2,1)S(1)} %maximum_select_fusion.refs_1_.refs_0_), channel_id=1, source_target_pairs={{0,4},{1,5},{2,6},{3,7},{4,0},{5,1},{6,2},{7,3},{8,12},{9,13},{10,... | collective-permute-start | bytes 835592 | tf_op jit(solution)/shard_map/ppermute | solution.py:641
  208.4 14.3 %collective-permute-start.30 = (bf16[272,512]{1,0:T(8,128)(2,1)S(1)}, bf16[272,512]{1,0:T(8,128)(2,1)S(1)}, u32[]{:S(2)}, u32[]{:S(2)}) collective-permute-start(bf16[272,512]{1,0:T(8,128)(2,1)S(1)} %maximum_select_fusion.refs_1_.refs_0_), channel_id=1, source_target_pairs={{0,2},{1,3},{2,0},{3,1},{4,6},{5,7},{6,4},{7,5},{8,10},{9,11},{10,... | collective-permute-start | bytes 835592 | tf_op jit(solution)/shard_map/ppermute | solution.py:641
  208.9 13.8 %collective-permute-start.31 = (bf16[272,512]{1,0:T(8,128)(2,1)S(1)}, bf16[272,512]{1,0:T(8,128)(2,1)S(1)}, u32[]{:S(2)}, u32[]{:S(2)}) collective-permute-start(bf16[272,512]{1,0:T(8,128)(2,1)S(1)} %maximum_select_fusion.refs_1_.refs_0_), channel_id=1, source_target_pairs={{0,6},{1,7},{2,4},{3,5},{4,2},{5,3},{6,0},{7,1},{8,14},{9,15},{10,... | collective-permute-start | bytes 835592 | tf_op jit(solution)/shard_map/ppermute | solution.py:641
  (30 other events, 408.2 us)
